TPU v7x, 512 devices: a whole 4x4x16 slice. The times are simulated.
512 devices in a mesh: fsdp: 32 (over z, core), tp: 16 (over y, x).
Axes of the slice: x: 4, y: 4, z: 16, core: 2. Of those that a mesh axis runs over, the one named last changes fastest.
Arguments:
- momentum: bfloat16 [8192, 28672], P('fsdp', 'tp'), may hold values from -256 to 256
- gradient: bfloat16 [8192, 28672], P('fsdp', 'tp'), may hold values from -256 to 256
- weight: bfloat16 [8192, 28672], P('fsdp', 'tp'), may hold values from -0.75 to 0.75
- right_factor: bfloat16 [512, 28672], P('fsdp', 'tp'), may hold values from -6 to 6
Outputs:
- new_momentum: bfloat16 [8192, 28672], P('fsdp', 'tp')
- new_weight: bfloat16 [8192, 28672], P('fsdp', 'tp')
- new_factor: bfloat16 [512, 28672], P('fsdp', 'tp')
All inputs are finite; a program needn't handle non-finite values.
Results may differ from a plain program's by a relative error of at most 0.013.
Values may be sent and summed in bfloat16 or wider, within the bound.
No kernel may reach another device: no remote copies, remote signals or barrier semaphores. Data moves between devices by JAX's collectives and lax.ppermute only.
A program may use at most 64 MiB of HBM per device.

v0:
```python
import math

import jax
import jax.numpy as jnp
from jax import lax
from jax.sharding import PartitionSpec as P

DM = 8192
DF = 28672


def orthonormal(partial_rows, gram_matrix):
    factor_lower = jnp.linalg.cholesky(gram_matrix)
    solved = jax.scipy.linalg.solve_triangular(factor_lower, partial_rows.T, lower=True)
    return solved.T.astype(jnp.bfloat16)


def local(momentum, gradient, weight, right_factor):
    combined = (momentum.astype(jnp.float32) + gradient.astype(jnp.float32)).astype(jnp.bfloat16)
    partial_value = lax.dot_general(
        combined,
        lax.all_gather(right_factor, "fsdp", axis=0, tiled=True),
        (((1,), (1,)), ((), ())),
        preferred_element_type=jnp.float32,
    )
    initial = lax.psum(partial_value, "tp")
    gram_local = jnp.dot(initial.T, initial, precision=lax.Precision.HIGHEST)
    gram_matrix = lax.psum(gram_local, "fsdp")
    basis = orthonormal(initial, gram_matrix)
    projected = lax.psum_scatter(
        lax.dot_general(
            basis, combined, (((0,), (0,)), ((), ())), preferred_element_type=jnp.float32
        ),
        "fsdp",
        scatter_dimension=0,
        tiled=True,
    ).astype(jnp.bfloat16)
    widened = projected.astype(jnp.float32)
    squares = lax.psum(jnp.sum(widened * widened, axis=1), "tp")
    row_rms = jnp.sqrt(squares / DF + 1e-06)
    new_factor = (widened / row_rms[:, None]).astype(jnp.bfloat16)
    all_project, all_factor = (
        lax.all_gather(projected, "fsdp", axis=0, tiled=True),
        lax.all_gather(new_factor, "fsdp", axis=0, tiled=True),
    )
    feedback = jnp.dot(basis, all_project, preferred_element_type=jnp.float32)
    update = jnp.dot(basis, all_factor, preferred_element_type=jnp.float32)
    new_momentum = (combined.astype(jnp.float32) - 0.4 * feedback).astype(jnp.bfloat16)
    new_weight = (weight.astype(jnp.float32) - 2.0 * math.sqrt(DM / DF) * update).astype(
        jnp.bfloat16
    )
    return (new_momentum, new_weight, new_factor)


def solution(mesh):
    placed = (P("fsdp", "tp"), P("fsdp", "tp"), P("fsdp", "tp"), P("fsdp", "tp"))
    return jax.shard_map(
        local,
        mesh=mesh,
        in_specs=placed,
        out_specs=(P("fsdp", "tp"), P("fsdp", "tp"), P("fsdp", "tp")),
        check_vma=False,
    )
```

profile of v0, /device:TPU:1, one launch (start us, length us, event | category | flops | bytes accessed | tf_op | source)
XLA Modules:
  0.0 829.6 jit_solution(17921255573117079272)
XLA Ops:
  7.9 79.5 %all-gather.4.cloned.1.call-done = bf16[512,1792]{1,0:T(8,128)(2,1)} async-done(((bf16[16,1792]{1,0:T(8,128)(2,1)}), bf16[512,1792]{1,0:T(8,128)(2,1)}) %all-gather.4.cloned.1.call-update) | async-done | bytes 1835024 | tf_op jit(solution)/shard_map/all_gather | solution.py:22
  87.4 3.5 fusion.36
  91.0 111.3 %all-reduce.4.cloned.1.call-done = f32[256,512]{1,0:T(8,128)} async-done(((f32[256,512]{1,0:T(8,128)}), f32[256,512]{1,0:T(8,128)}) %all-reduce.4.cloned.1.call-update) | async-done | bytes 524304 | tf_op jit(solution)/shard_map/psum | solution.py:26
  202.4 3.3 fusion.41
  205.8 211.4 %all-reduce.6.cloned.1.call-done = f32[512,512]{0,1:T(8,128)} async-done(((f32[512,512]{0,1:T(8,128)}), f32[512,512]{0,1:T(8,128)}) %all-reduce.6.cloned.1.call-update) | async-done | bytes 1048592 | tf_op jit(solution)/shard_map/psum | solution.py:28
  419.0 11.7 %cholesky.104 = f32[128,128]{1,0:T(8,128)S(1)} custom-call(f32[128,128]{1,0:T(8,128)S(1)} %cholesky.266), custom_call_target="Cholesky" | custom-call | tf_op jit(solution)/shard_map/jit(cholesky)/cholesky | solution.py:13
  430.8 9.8 %custom-call.31 = f32[1,128,128]{1,2,0:T(8,128)S(1)} custom-call(f32[1,128,128]{2,1,0:T(8,128)S(1)} %get-tuple-element.32), custom_call_target="InvertDiagBlocksLowerTriangular" | custom-call | tf_op jit(solution)/shard_map/jit(cholesky)/cholesky | solution.py:13
  441.4 11.7 %cholesky.217 = f32[128,128]{1,0:T(8,128)S(1)} custom-call(f32[128,128]{1,0:T(8,128)S(1)} %cholesky.270), custom_call_target="Cholesky" | custom-call | tf_op jit(solution)/shard_map/jit(cholesky)/cholesky | solution.py:13
  453.2 10.0 %custom-call.32 = f32[1,128,128]{1,2,0:T(8,128)S(1)} custom-call(f32[1,128,128]{2,1,0:T(8,128)S(1)} %get-tuple-element.29), custom_call_target="InvertDiagBlocksLowerTriangular" | custom-call | tf_op jit(solution)/shard_map/jit(cholesky)/cholesky | solution.py:13
  463.8 11.7 %cholesky.238 = f32[128,128]{1,0:T(8,128)S(1)} custom-call(f32[128,128]{1,0:T(8,128)S(1)} %cholesky.275), custom_call_target="Cholesky" | custom-call | tf_op jit(solution)/shard_map/jit(cholesky)/cholesky | solution.py:13
  476.3 9.8 %custom-call.33 = f32[1,128,128]{1,2,0:T(8,128)S(1)} custom-call(f32[1,128,128]{2,1,0:T(8,128)S(1)} %get-tuple-element.26), custom_call_target="InvertDiagBlocksLowerTriangular" | custom-call | tf_op jit(solution)/shard_map/jit(cholesky)/cholesky | solution.py:13
  486.7 11.7 %cholesky.255 = f32[128,128]{1,0:T(8,128)S(1)} custom-call(f32[128,128]{1,0:T(8,128)S(1)} %convolution_subtract_fusion.5), custom_call_target="Cholesky" | custom-call | tf_op jit(solution)/shard_map/jit(cholesky)/cholesky | solution.py:13
  502.6 10.9 %while.1 = (s32[]{:T(128)}, f32[512,512]{1,0:T(8,128)S(1)}, s32[4,2]{0,1:T(2,128)S(1)}, f32[4,128,128]{2,1,0:T(8,128)}, s32[]{:T(128)}) while((s32[]{:T(128)}, f32[512,512]{1,0:T(8,128)S(1)}, s32[4,2]{0,1:T(2,128)S(1)}, f32[4,128,128]{2,1,0:T(8,128)}, s32[]{:T(128)}) %tuple.35), condition=%wide.while_cond, body=%wide.while_body.sunk | while | flops 2 | bytes 132705 | solution.py:14
  503.3 2.1 bitcast_dynamic-update-slice_fusion.2
  506.0 2.1 bitcast_dynamic-update-slice_fusion.2
  508.8 2.1 bitcast_dynamic-update-slice_fusion.2
  513.6 40.9 %custom-call.34 = f32[4,128,128]{1,2,0:T(8,128)} custom-call(f32[4,128,128]{2,1,0:T(8,128)} %get-tuple-element.10), custom_call_target="InvertDiagBlocksLowerTriangular" | custom-call | tf_op jit(solution)/shard_map/jit(_solve_triangular)/triangular_solve | solution.py:14
  561.0 2.5 fusion.35
  563.5 109.6 %reduce-scatter.2.cloned.1.call-done = f32[16,1792]{1,0:T(8,128)} async-done(((f32[512,1792]{1,0:T(8,128)}), f32[16,1792]{1,0:T(8,128)}) %reduce-scatter.2.cloned.1.call-update) | async-done | bytes 114704 | tf_op jit(solution)/shard_map/reduce_scatter | solution.py:30
  674.9 32.9 %psum.23 = f32[16]{0:T(128)S(1)} all-reduce(f32[16]{0:T(128)S(1)} %get-tuple-element.19), channel_id=1, replica_groups=mesh['fsdp'=32,'tp'=16] {'tp'}, use_global_device_ids=true, to_apply=%region_12.13 | all-reduce | flops 16 | bytes 128 | tf_op jit(solution)/shard_map/psum | solution.py:39
  709.3 39.1 %all-gather.6.cloned.1.call-done = bf16[512,1792]{1,0:T(8,128)(2,1)} async-done(((bf16[16,1792]{1,0:T(8,128)(2,1)}), bf16[512,1792]{1,0:T(8,128)(2,1)}) %all-gather.6.cloned.1.call-update) | async-done | bytes 1835024 | tf_op jit(solution)/shard_map/all_gather | solution.py:43
  748.4 3.1 fusion.2
  751.6 68.1 %all-gather.8.cloned.1.call-done = bf16[512,1792]{1,0:T(8,128)(2,1)} async-done(((bf16[16,1792]{1,0:T(8,128)(2,1)}), bf16[512,1792]{1,0:T(8,128)(2,1)}) %all-gather.8.cloned.1.call-update) | async-done | bytes 1835024 | tf_op jit(solution)/shard_map/all_gather | solution.py:44
  819.7 3.1 fusion.3
  (68 shorter events, 21.8 us)
Async XLA Ops:
  7.2 80.3 %all-gather.4.cloned.1.call-start = ((), (), s32[]{:S(2)}) async-start(), calls=%async_computation.1 | async-start | bytes 1892352 | tf_op jit(solution)/shard_map/all_gather | solution.py:22
  7.9 194.5 %all-reduce.4.cloned.1.call-start = ((), (), s32[]{:S(2)}) async-start(), calls=%async_computation.2 | async-start | bytes 1048576 | tf_op jit(solution)/shard_map/psum | solution.py:26
  91.0 326.1 %all-reduce.6.cloned.1.call-start = ((), (), s32[]{:S(2)}) async-start(), calls=%async_computation.3 | async-start | bytes 2097152 | tf_op jit(solution)/shard_map/psum | solution.py:28
  205.7 467.4 %reduce-scatter.2.cloned.1.call-start = ((), (), s32[]{:S(2)}) async-start(), calls=%async_computation.4 | async-start | bytes 3784704 | tf_op jit(solution)/shard_map/reduce_scatter | solution.py:30
  417.1 1.7 copy-start.3
  475.5 78.9 %copy-start.2 = (f32[256,512]{1,0:T(8,128)S(1)}, f32[256,512]{1,0:T(8,128)}, u32[]{:S(2)}) copy-start(f32[256,512]{1,0:T(8,128)} %all-reduce.4.cloned.1.call-done) | copy-start | bytes 1572868
  513.6 47.4 %copy-start = (bf16[256,1792]{1,0:T(8,128)(2,1)S(1)}, bf16[256,1792]{1,0:T(8,128)(2,1)}, u32[]{:S(2)}) copy-start(bf16[256,1792]{1,0:T(8,128)(2,1)} %param.5) | copy-start | bytes 2752516
  513.6 47.4 %copy-start.1 = (bf16[256,1792]{1,0:T(8,128)(2,1)S(1)}, bf16[256,1792]{1,0:T(8,128)(2,1)}, u32[]{:S(2)}) copy-start(bf16[256,1792]{1,0:T(8,128)(2,1)} %param.4) | copy-start | bytes 2752516
  558.9 2.0 copy-start.4
  563.4 185.0 %copy-start.5 = (bf16[128,256]{1,0:T(8,128)(2,1)S(1)}, bf16[128,256]{1,0:T(8,128)(2,1)}, u32[]{:S(2)}) copy-start(bf16[128,256]{1,0:T(8,128)(2,1)} %copy-done.4) | copy-start | bytes 196612
  563.5 185.0 %all-gather.6.cloned.1.call-start = ((), (), s32[]{:S(2)}) async-start(), calls=%async_computation.5 | async-start | bytes 1892352 | tf_op jit(solution)/shard_map/all_gather | solution.py:43
  674.8 144.9 %all-gather.8.cloned.1.call-start = ((), (), s32[]{:S(2)}) async-start(), calls=%async_computation.6 | async-start | bytes 1892352 | tf_op jit(solution)/shard_map/all_gather | solution.py:44
  709.3 110.4 %copy-start.6 = (bf16[256,1792]{1,0:T(8,128)(2,1)S(1)}, bf16[256,1792]{1,0:T(8,128)(2,1)}, u32[]{:S(2)}) copy-start(bf16[256,1792]{1,0:T(8,128)(2,1)} %param.6) | copy-start | bytes 2752516
Sparse Core Ops, SparseCore 0:
  10.1 77.2 all-gather.3
  91.2 111.1 all-reduce.3
  205.8 211.2 all-reduce.5
  563.6 109.5 reduce-scatter.1
  675.9 72.4 all-gather.5
  751.2 68.4 all-gather.7
where the time goes:
time: 830 us
  waiting for transfers between devices  620 us (75%)
  other arithmetic  123 us (15%)
  blocking collectives  32.9 us (4%)
  matrix products  23.8 us (3%)
  between operations  16.9 us (2%)
  local copies, waits for them, and re-layouts  12.7 us (2%)
    psum x1, waiting for transfers between devices, local(): gram_matrix = lax.psum(gram_local, 'fsdp')  211 us
    psum x1, waiting for transfers between devices, local(): initial = lax.psum(partial_value, 'tp')  111 us
    reduce_scatter x1, waiting for transfers between devices, local(): lax.psum_scatter(lax.dot_general(basis, combined, (((0,), (0,)), ((), ())...  110 us
    all_gather x1, waiting for transfers between devices, local(): lax.all_gather(right_factor, 'fsdp', axis=0, tiled=True)  79.5 us
    another operation x14, other arithmetic, orthonormal(): factor_lower = jnp.linalg.cholesky(gram_matrix)  78.6 us
    all_gather x1, waiting for transfers between devices, local(): lax.all_gather(new_factor, 'fsdp', axis=0, tiled=True)  68.1 us
    another operation x3, other arithmetic, orthonormal(): jax.scipy.linalg.solve_triangular(factor_lower, partial_rows.T, lower=True)  41.2 us
    all_gather x1, waiting for transfers between devices, local(): lax.all_gather(projected, 'fsdp', axis=0, tiled=True)  39.1 us
  transfers between devices with their start and end apart: 6, of which 6 were waited for; matrix products, arithmetic and copies ran while one was open for 1% of the time, Pallas kernels for 0%

commit v1 on v0

v1 whole, which is shorter than its diff:
```python
import math

import jax
import jax.numpy as jnp
from jax import lax
from jax.sharding import PartitionSpec as P

DM = 8192
DF = 28672
Z, Y, X = 16, 4, 4
HI = lax.Precision.HIGHEST
F32 = jnp.float32
BF16 = jnp.bfloat16


def from_z(value, step):
    perm = [(((z + step) % Z) * 2 + c, z * 2 + c) for z in range(Z) for c in range(2)]
    return lax.ppermute(value, "fsdp", perm)


def from_core(value):
    return lax.ppermute(value, "fsdp", [(i ^ 1, i) for i in range(2 * Z)])


def from_x(value, step):
    perm = [(y * X + (x + step) % X, y * X + x) for y in range(Y) for x in range(X)]
    return lax.ppermute(value, "tp", perm)


def from_y(value, step):
    perm = [(((y + step) % Y) * X + x, y * X + x) for y in range(Y) for x in range(X)]
    return lax.ppermute(value, "tp", perm)


def ordered(pieces, first):
    rows = []
    for place in range(4):
        row = pieces[place]
        for start in range(1, 4):
            row = jnp.where(first == start, pieces[(place - start) % 4], row)
        rows.append(row)
    return jnp.stack(rows)


def gather_fsdp(chunk, core, quad, lane):
    far = ordered([chunk] + [from_z(chunk, 4 * j) for j in (1, 2, 3)], quad)
    ahead, behind = from_z(far, 1), from_z(far, -1)
    across = jnp.concatenate([from_z(far[:2], 2), from_z(far[2:], -2)])
    near = ordered([far, ahead, across, behind], lane)
    other = from_core(near)
    return jnp.stack([jnp.where(core == 0, near, other), jnp.where(core == 0, other, near)])


def scatter_fsdp(total, core, quad, lane):
    pick = lambda array, place: lax.dynamic_index_in_dim(array, place, 0, keepdims=False)
    half = pick(total, core) + from_core(pick(total, 1 - core))
    ahead = from_z(pick(half, (lane + 3) % 4), 1)
    behind = from_z(pick(half, (lane + 1) % 4), -1)
    across = pick(half, (lane + 2) % 4)
    across = jnp.concatenate([from_z(across[:2], 2), from_z(across[2:], -2)])
    mine = pick(half, lane) + ahead + behind + across
    out = pick(mine, quad)
    for j in (1, 2, 3):
        out = out + from_z(pick(mine, (quad - j) % 4), 4 * j)
    return out


def sum_tp(value):
    value = value + from_x(value, 1) + from_x(value, 2) + from_x(value, 3)
    return value + from_y(value, 1) + from_y(value, 2) + from_y(value, 3)


def gather_tp(chunk, row, col):
    line = ordered([chunk] + [from_x(chunk, j) for j in (1, 2, 3)], col)
    return ordered([line] + [from_y(line, j) for j in (1, 2, 3)], row)


def inverse_factor(gram):
    lower = jnp.linalg.cholesky(gram)
    return jax.scipy.linalg.solve_triangular(lower, jnp.eye(512, dtype=F32), lower=True)


def nt(a, b, precision=None):
    return lax.dot_general(
        a, b, (((1,), (1,)), ((), ())), precision=precision, preferred_element_type=F32
    )


def local(momentum, gradient, weight, right_factor):
    fsdp, tp = lax.axis_index("fsdp"), lax.axis_index("tp")
    core, z = fsdp % 2, fsdp // 2
    quad, lane = z // 4, z % 4
    row, col = tp // X, tp % X

    blend = (momentum.astype(F32) + gradient.astype(F32)).astype(BF16)

    factor = gather_fsdp(right_factor, core, quad, lane)
    factor = jnp.transpose(factor, (2, 1, 0, 3, 4)).reshape(512, -1)
    partial = nt(blend, factor)
    pieces = lax.all_to_all(partial.reshape(16, 16, 512), "tp", 0, 0)
    start = gather_tp(jnp.sum(pieces, axis=0), row, col).reshape(256, 512)

    gram = jnp.dot(start.T, start, precision=HI)
    band = lax.dynamic_index_in_dim(gram.reshape(16, 2, 16, 512), tp, 0, keepdims=False)
    pick = lambda place: lax.dynamic_index_in_dim(band, place, 0, keepdims=False)
    band = pick(core) + from_core(pick(1 - core))
    band = band + from_z(band, 1) + from_z(band, -1) + from_z(band, 2)
    band = band + from_z(band, 4) + from_z(band, -4) + from_z(band, 8)
    mine = gather_tp(band, row, col)
    other = from_core(mine)
    gram = jnp.stack(
        [jnp.where(core == 0, mine, other), jnp.where(core == 0, other, mine)], axis=2
    ).reshape(512, 512)

    high = start.astype(BF16)
    low = (start - high.astype(F32)).astype(BF16)
    tn = lambda a, b: lax.dot_general(
        a, b, (((0,), (0,)), ((), ())), preferred_element_type=F32
    )
    cross = (tn(blend, high) + tn(blend, low)).reshape(2, 4, 4, 56, 512)
    cross = scatter_fsdp(cross, core, quad, lane)

    inverse = inverse_factor(gram)
    chunk = nt(cross, inverse, HI).astype(BF16)
    project = gather_fsdp(chunk, core, quad, lane).reshape(1792, 512)
    basis = nt(start, inverse, HI).astype(BF16)

    wide = project.astype(F32)
    squares = sum_tp(jnp.sum(wide * wide, axis=0, keepdims=True))
    rms = jnp.sqrt(squares / DF + 1e-06)
    factor_t = (wide / rms).astype(BF16)
    chosen = (jnp.arange(512)[None, :] == 16 * fsdp + jnp.arange(16)[:, None]).astype(BF16)
    new_factor = nt(chosen, factor_t).astype(BF16)
    new_momentum = (blend.astype(F32) - 0.4 * nt(basis, project)).astype(BF16)
    new_weight = (
        weight.astype(F32) - 2.0 * math.sqrt(DM / DF) * nt(basis, factor_t)
    ).astype(BF16)
    return (new_momentum, new_weight, new_factor)


def solution(mesh):
    placed = (P("fsdp", "tp"), P("fsdp", "tp"), P("fsdp", "tp"), P("fsdp", "tp"))
    return jax.shard_map(
        local,
        mesh=mesh,
        in_specs=placed,
        out_specs=(P("fsdp", "tp"), P("fsdp", "tp"), P("fsdp", "tp")),
        check_vma=False,
    )
```

time: 830 us -> 490 us (0.59)
  waiting for transfers between devices: 620 us -> 76.7 us
  starting transfers between devices: 0.24 us -> 208 us
  blocking collectives: 32.9 us -> 14.4 us
  other arithmetic: 123 us -> 137 us
  between operations: 16.9 us -> 4.66 us
    psum x2 -> x0, waiting for transfers between devices: 323 us -> none  [the longest x1 211 us: local(): gram_matrix = lax.psum(gram_local, 'fsdp')]
    ppermute x0 -> x50, starting transfers between devices: none -> 208 us  [the longest x27 130 us: from_z(): return lax.ppermute(value, 'fsdp', perm)]
    all_gather x3 -> x0, waiting for transfers between devices: 187 us -> none  [the longest x1 79.5 us: local(): lax.all_gather(right_factor, 'fsdp', axis=0, tiled=True)]
    reduce_scatter x1 -> x0, waiting for transfers between devices: 110 us -> none  [local(): lax.psum_scatter(lax.dot_general(basis, combined, (((0,), (0,)), ((), ())...]
    ppermute x0 -> x50, waiting for transfers between devices: none -> 76.7 us  [the longest x27 54 us: from_z(): return lax.ppermute(value, 'fsdp', perm)]
    psum x1 -> x0, blocking collectives: 32.9 us -> none  [local(): squares = lax.psum(jnp.sum(widened * widened, axis=1), 'tp')]
    all_to_all x0 -> x1, blocking collectives: none -> 14.4 us  [local(): pieces = lax.all_to_all(partial.reshape(16, 16, 512), 'tp', 0, 0)]
    another operation x17 -> x46, other arithmetic: 120 us -> 128 us  [the longest x14 81 us: inverse_factor(): lower = jnp.linalg.cholesky(gram)]
  transfers between devices with their start and end apart: 6 -> 50, of which waited for: 6 -> 24; matrix products, arithmetic and copies ran while one was open for 1% -> 34% of each run, Pallas kernels for 0% -> 0%
where the time goes in v1:
time: 490 us; the launch traced here: 482 us
  starting transfers between devices  208 us (42%)
  other arithmetic  137 us (28%)
  waiting for transfers between devices  76.7 us (16%)
  matrix products  22.3 us (5%)
  local copies, waits for them, and re-layouts  19.4 us (4%)
  blocking collectives  14.4 us (3%)
    ppermute x27, starting transfers between devices, from_z(): return lax.ppermute(value, 'fsdp', perm)  130 us
    another operation x14, other arithmetic, inverse_factor(): lower = jnp.linalg.cholesky(gram)  81 us
    ppermute x27, waiting for transfers between devices, from_z(): return lax.ppermute(value, 'fsdp', perm)  54 us
    another operation x3, other arithmetic, inverse_factor(): jax.scipy.linalg.solve_triangular(lower, jnp.eye(512, dtype=F32), lower=T...  41.2 us
    ppermute x5, starting transfers between devices, from_core(): return lax.ppermute(value, 'fsdp', [(i ^ 1, i) for i in range(2 * Z)])  30.1 us
    ppermute x9, starting transfers between devices, from_y(): return lax.ppermute(value, 'tp', perm)  24.1 us
    ppermute x9, starting transfers between devices, from_x(): return lax.ppermute(value, 'tp', perm)  23.9 us
    all_to_all x1, blocking collectives, local(): pieces = lax.all_to_all(partial.reshape(16, 16, 512), 'tp', 0, 0)  14.4 us
  transfers between devices with their start and end apart: 50, of which 24 were waited for; matrix products, arithmetic and copies ran while one was open for 34% of the time, Pallas kernels for 0%

profile of v1, /device:TPU:1, one launch (start us, length us, event | category | flops | bytes accessed | tf_op | source)
XLA Modules:
  0.0 482.0 jit_solution(6033306125395869390)
XLA Ops:
  0.6 13.3 %collective-permute-start = (bf16[16,1792]{1,0:T(8,128)(2,1)}, bf16[16,1792]{1,0:T(8,128)(2,1)S(1)}, u32[]{:S(2)}, u32[]{:S(2)}) collective-permute-start(bf16[16,1792]{1,0:T(8,128)(2,1)} %param.7), channel_id=1, source_target_pairs={{128,0},{144,16},{160,32},{176,48},{192,64},{208,80},{224,96},{240... | collective-permute-start | bytes 172040 | tf_op jit(solution)/shard_map/ppermute | solution.py:18
  18.8 7.3 %collective-permute-start.2 = (bf16[16,1792]{1,0:T(8,128)(2,1)}, bf16[16,1792]{1,0:T(8,128)(2,1)S(1)}, u32[]{:S(2)}, u32[]{:S(2)}) collective-permute-start(bf16[16,1792]{1,0:T(8,128)(2,1)} %param.7), channel_id=1, source_target_pairs={{384,0},{400,16},{416,32},{432,48},{448,64},{464,80},{480,96},{496... | collective-permute-start | bytes 172040 | tf_op jit(solution)/shard_map/ppermute | solution.py:18
  33.1 6.5 %collective-permute-start.3 = (bf16[4,16,1792]{2,1,0:T(8,128)(2,1)S(1)}, bf16[4,16,1792]{2,1,0:T(8,128)(2,1)S(1)}, u32[]{:S(2)}, u32[]{:S(2)}) collective-permute-start(bf16[4,16,1792]{2,1,0:T(8,128)(2,1)S(1)} %pad_maximum_fusion.9), channel_id=1, source_target_pairs={{32,0},{48,16},{64,32},{80,48},{96,64},{112,80},{128,96},{144,112}... | collective-permute-start | bytes 688136 | tf_op jit(solution)/shard_map/ppermute | solution.py:18
  52.6 7.3 %collective-permute-start.7 = (bf16[4,4,16,1792]{3,2,1,0:T(8,128)(2,1)S(1)}, bf16[4,4,16,1792]{3,2,1,0:T(8,128)(2,1)}, u32[]{:S(2)}, u32[]{:S(2)}) collective-permute-start(bf16[4,4,16,1792]{3,2,1,0:T(8,128)(2,1)S(1)} %pad_maximum_fusion.3), channel_id=1, source_target_pairs={{16,0},{0,16},{48,32},{32,48},{80,64},{64,80},{112,96},{96,112},{1... | collective-permute-start | bytes 2752520 | tf_op jit(solution)/shard_map/ppermute | solution.py:22
  64.5 14.4 %all_to_all.5 = f32[16,16,512]{2,1,0:T(8,128)S(1)} all-to-all(f32[16,16,512]{2,1,0:T(8,128)S(1)} %fusion.48), channel_id=1, replica_groups=mesh['fsdp'=32,'tp'=16] {'tp'}, dimensions={0} | all-to-all | bytes 1048576 | tf_op jit(solution)/shard_map/all_to_all | solution.py:100
  105.1 6.8 %collective-permute-start.14 = (f32[16,512]{1,0:T(8,128)S(1)}, f32[16,512]{1,0:T(8,128)S(1)}, u32[]{:S(2)}, u32[]{:S(2)}) collective-permute-start(f32[16,512]{1,0:T(8,128)S(1)} %dynamic-slice_bitcast_fusion.8), channel_id=1, source_target_pairs={{16,0},{0,16},{48,32},{32,48},{80,64},{64,80},{112,96},{96,112},{1... | collective-permute-start | bytes 98312 | tf_op jit(solution)/shard_map/ppermute | solution.py:22
  135.0 5.7 %collective-permute-start.20 = (f32[16,512]{1,0:T(8,128)S(1)}, f32[16,512]{1,0:T(8,128)S(1)}, u32[]{:S(2)}, u32[]{:S(2)}) collective-permute-start(f32[16,512]{1,0:T(8,128)S(1)} %add_add_fusion.1), channel_id=1, source_target_pairs={{256,0},{272,16},{288,32},{304,48},{320,64},{336,80},{352,96},{368... | collective-permute-start | bytes 98312 | tf_op jit(solution)/shard_map/ppermute | solution.py:18
  141.5 7.0 %collective-permute-done.20 = f32[16,512]{1,0:T(8,128)S(1)} collective-permute-done((f32[16,512]{1,0:T(8,128)S(1)}, f32[16,512]{1,0:T(8,128)S(1)}, u32[]{:S(2)}, u32[]{:S(2)}) %collective-permute-start.20) | collective-permute-done | bytes 32800 | tf_op jit(solution)/shard_map/ppermute | solution.py:18
  172.2 8.2 %collective-permute-start.27 = (f32[4,4,16,512]{3,2,1,0:T(8,128)S(1)}, f32[4,4,16,512]{3,2,1,0:T(8,128)S(1)}, u32[]{:S(2)}, u32[]{:S(2)}) collective-permute-start(f32[4,4,16,512]{3,2,1,0:T(8,128)S(1)} %pad_maximum_fusion.8), channel_id=1, source_target_pairs={{16,0},{0,16},{48,32},{32,48},{80,64},{64,80},{112,96},{96,112},{1... | collective-permute-start | bytes 1572872 | tf_op jit(solution)/shard_map/ppermute | solution.py:22
  188.6 11.7 %cholesky.104 = f32[128,128]{1,0:T(8,128)S(1)} custom-call(f32[128,128]{1,0:T(8,128)S(1)} %cholesky.266), custom_call_target="Cholesky" | custom-call | tf_op jit(solution)/shard_map/jit(cholesky)/cholesky | solution.py:79
  200.4 9.8 %custom-call.31 = f32[1,128,128]{1,2,0:T(8,128)S(1)} custom-call(f32[1,128,128]{2,1,0:T(8,128)S(1)} %get-tuple-element.71), custom_call_target="InvertDiagBlocksLowerTriangular" | custom-call | tf_op jit(solution)/shard_map/jit(cholesky)/cholesky | solution.py:79
  212.8 11.7 %cholesky.217 = f32[128,128]{1,0:T(8,128)S(1)} custom-call(f32[128,128]{1,0:T(8,128)S(1)} %cholesky.270), custom_call_target="Cholesky" | custom-call | tf_op jit(solution)/shard_map/jit(cholesky)/cholesky | solution.py:79
  224.5 10.0 %custom-call.32 = f32[1,128,128]{1,2,0:T(8,128)S(1)} custom-call(f32[1,128,128]{2,1,0:T(8,128)S(1)} %get-tuple-element.68), custom_call_target="InvertDiagBlocksLowerTriangular" | custom-call | tf_op jit(solution)/shard_map/jit(cholesky)/cholesky | solution.py:79
  236.1 11.7 %cholesky.238 = f32[128,128]{1,0:T(8,128)S(1)} custom-call(f32[128,128]{1,0:T(8,128)S(1)} %cholesky.275), custom_call_target="Cholesky" | custom-call | tf_op jit(solution)/shard_map/jit(cholesky)/cholesky | solution.py:79
  248.4 9.8 %custom-call.33 = f32[1,128,128]{1,2,0:T(8,128)S(1)} custom-call(f32[1,128,128]{2,1,0:T(8,128)S(1)} %get-tuple-element.65), custom_call_target="InvertDiagBlocksLowerTriangular" | custom-call | tf_op jit(solution)/shard_map/jit(cholesky)/cholesky | solution.py:79
  260.4 13.4 %cholesky.255 = f32[128,128]{1,0:T(8,128)} custom-call(f32[128,128]{1,0:T(8,128)} %convolution_subtract_fusion.5), custom_call_target="Cholesky" | custom-call | tf_op jit(solution)/shard_map/jit(cholesky)/cholesky | solution.py:79
  279.5 14.4 %while.1 = (s32[]{:T(128)}, f32[512,512]{1,0:T(8,128)}, s32[4,2]{0,1:T(2,128)S(1)}, f32[4,128,128]{2,1,0:T(8,128)}, s32[]{:T(128)}) while((s32[]{:T(128)}, f32[512,512]{1,0:T(8,128)}, s32[4,2]{0,1:T(2,128)S(1)}, f32[4,128,128]{2,1,0:T(8,128)}, s32[]{:T(128)}) %tuple.58), condition=%wide.while_cond, body=%wide.while_body.sunk | while | flops 2 | bytes 132705 | solution.py:80
  293.9 40.1 %custom-call.34 = f32[4,128,128]{1,2,0:T(8,128)S(1)} custom-call(f32[4,128,128]{2,1,0:T(8,128)} %get-tuple-element.10), custom_call_target="InvertDiagBlocksLowerTriangular" | custom-call | tf_op jit(solution)/shard_map/jit(_solve_triangular)/triangular_solve | solution.py:80
  356.5 9.5 %collective-permute-done.31 = f32[2,56,512]{2,1,0:T(8,128)S(1)} collective-permute-done((f32[2,56,512]{2,1,0:T(8,128)S(1)}, f32[2,56,512]{2,1,0:T(8,128)S(1)}, u32[]{:S(2)}, u32[]{:S(2)}) %collective-permute-start.31) | collective-permute-done | bytes 229408 | tf_op jit(solution)/shard_map/ppermute | solution.py:18
  367.1 6.9 %collective-permute-start.33 = (f32[56,512]{1,0:T(8,128)S(1)}, f32[56,512]{1,0:T(8,128)S(1)}, u32[]{:S(2)}, u32[]{:S(2)}) collective-permute-start(f32[56,512]{1,0:T(8,128)S(1)} %get-tuple-element.43), channel_id=1, source_target_pairs={{128,0},{144,16},{160,32},{176,48},{192,64},{208,80},{224,96},{240... | collective-permute-start | bytes 344072 | tf_op jit(solution)/shard_map/ppermute | solution.py:18
  383.5 15.0 %collective-permute-done.34 = f32[56,512]{1,0:T(8,128)S(1)} collective-permute-done((f32[56,512]{1,0:T(8,128)S(1)}, f32[56,512]{1,0:T(8,128)S(1)}, u32[]{:S(2)}, u32[]{:S(2)}) %collective-permute-start.34) | collective-permute-done | bytes 114720 | tf_op jit(solution)/shard_map/ppermute | solution.py:18
  399.6 7.8 %collective-permute-start.36 = (bf16[56,512]{1,0:T(8,128)(2,1)S(1)}, bf16[56,512]{1,0:T(8,128)(2,1)S(1)}, u32[]{:S(2)}, u32[]{:S(2)}) collective-permute-start(bf16[56,512]{1,0:T(8,128)(2,1)S(1)} %convolution_convert_fusion.2), channel_id=1, source_target_pairs={{128,0},{144,16},{160,32},{176,48},{192,64},{208,80},{224,96},{240... | collective-permute-start | bytes 172040 | tf_op jit(solution)/shard_map/ppermute | solution.py:18
  409.4 7.2 %collective-permute-start.38 = (bf16[56,512]{1,0:T(8,128)(2,1)S(1)}, bf16[56,512]{1,0:T(8,128)(2,1)S(1)}, u32[]{:S(2)}, u32[]{:S(2)}) collective-permute-start(bf16[56,512]{1,0:T(8,128)(2,1)S(1)} %convolution_convert_fusion.2), channel_id=1, source_target_pairs={{384,0},{400,16},{416,32},{432,48},{448,64},{464,80},{480,96},{496... | collective-permute-start | bytes 172040 | tf_op jit(solution)/shard_map/ppermute | solution.py:18
  421.5 6.1 %collective-permute-start.39 = (bf16[4,56,512]{2,1,0:T(8,128)(2,1)S(1)}, bf16[4,56,512]{2,1,0:T(8,128)(2,1)S(1)}, u32[]{:S(2)}, u32[]{:S(2)}) collective-permute-start(bf16[4,56,512]{2,1,0:T(8,128)(2,1)S(1)} %pad_maximum_fusion.10), channel_id=1, source_target_pairs={{32,0},{48,16},{64,32},{80,48},{96,64},{112,80},{128,96},{144,112}... | collective-permute-start | bytes 688136 | tf_op jit(solution)/shard_map/ppermute | solution.py:18
  (207 shorter events, 230.0 us)
Async XLA Ops:
  0.6 25.5 %collective-permute-start = (bf16[16,1792]{1,0:T(8,128)(2,1)}, bf16[16,1792]{1,0:T(8,128)(2,1)S(1)}, u32[]{:S(2)}, u32[]{:S(2)}) collective-permute-start(bf16[16,1792]{1,0:T(8,128)(2,1)} %param.7), channel_id=1, source_target_pairs={{128,0},{144,16},{160,32},{176,48},{192,64},{208,80},{224,96},{240... | collective-permute-start | bytes 172040 | tf_op jit(solution)/shard_map/ppermute | solution.py:18
  13.9 14.1 %collective-permute-start.1 = (bf16[16,1792]{1,0:T(8,128)(2,1)}, bf16[16,1792]{1,0:T(8,128)(2,1)S(1)}, u32[]{:S(2)}, u32[]{:S(2)}) collective-permute-start(bf16[16,1792]{1,0:T(8,128)(2,1)} %param.7), channel_id=1, source_target_pairs={{256,0},{272,16},{288,32},{304,48},{320,64},{336,80},{352,96},{368... | collective-permute-start | bytes 172040 | tf_op jit(solution)/shard_map/ppermute | solution.py:18
  18.8 13.4 %collective-permute-start.2 = (bf16[16,1792]{1,0:T(8,128)(2,1)}, bf16[16,1792]{1,0:T(8,128)(2,1)S(1)}, u32[]{:S(2)}, u32[]{:S(2)}) collective-permute-start(bf16[16,1792]{1,0:T(8,128)(2,1)} %param.7), channel_id=1, source_target_pairs={{384,0},{400,16},{416,32},{432,48},{448,64},{464,80},{480,96},{496... | collective-permute-start | bytes 172040 | tf_op jit(solution)/shard_map/ppermute | solution.py:18
  33.1 19.2 %collective-permute-start.3 = (bf16[4,16,1792]{2,1,0:T(8,128)(2,1)S(1)}, bf16[4,16,1792]{2,1,0:T(8,128)(2,1)S(1)}, u32[]{:S(2)}, u32[]{:S(2)}) collective-permute-start(bf16[4,16,1792]{2,1,0:T(8,128)(2,1)S(1)} %pad_maximum_fusion.9), channel_id=1, source_target_pairs={{32,0},{48,16},{64,32},{80,48},{96,64},{112,80},{128,96},{144,112}... | collective-permute-start | bytes 688136 | tf_op jit(solution)/shard_map/ppermute | solution.py:18
  39.6 12.7 %collective-permute-start.6 = (bf16[4,16,1792]{2,1,0:T(8,128)(2,1)S(1)}, bf16[4,16,1792]{2,1,0:T(8,128)(2,1)S(1)}, u32[]{:S(2)}, u32[]{:S(2)}) collective-permute-start(bf16[4,16,1792]{2,1,0:T(8,128)(2,1)S(1)} %pad_maximum_fusion.9), channel_id=1, source_target_pairs={{480,0},{496,16},{0,32},{16,48},{32,64},{48,80},{64,96},{80,112},{... | collective-permute-start | bytes 688136 | tf_op jit(solution)/shard_map/ppermute | solution.py:18
  112.7 13.1 %collective-permute-start.15 = (f32[16,512]{1,0:T(8,128)S(1)}, f32[16,512]{1,0:T(8,128)S(1)}, u32[]{:S(2)}, u32[]{:S(2)}) collective-permute-start(f32[16,512]{1,0:T(8,128)S(1)} %bitcast_add_fusion.4), channel_id=1, source_target_pairs={{32,0},{48,16},{64,32},{80,48},{96,64},{112,80},{128,96},{144,112}... | collective-permute-start | bytes 98312 | tf_op jit(solution)/shard_map/ppermute | solution.py:18
  125.8 15.7 %collective-permute-start.18 = (f32[16,512]{1,0:T(8,128)S(1)}, f32[16,512]{1,0:T(8,128)S(1)}, u32[]{:S(2)}, u32[]{:S(2)}) collective-permute-start(f32[16,512]{1,0:T(8,128)S(1)} %add_add_fusion.1), channel_id=1, source_target_pairs={{128,0},{144,16},{160,32},{176,48},{192,64},{208,80},{224,96},{240... | collective-permute-start | bytes 98312 | tf_op jit(solution)/shard_map/ppermute | solution.py:18
  131.1 10.4 %collective-permute-start.19 = (f32[16,512]{1,0:T(8,128)S(1)}, f32[16,512]{1,0:T(8,128)S(1)}, u32[]{:S(2)}, u32[]{:S(2)}) collective-permute-start(f32[16,512]{1,0:T(8,128)S(1)} %add_add_fusion.1), channel_id=1, source_target_pairs={{384,0},{400,16},{416,32},{432,48},{448,64},{464,80},{480,96},{496... | collective-permute-start | bytes 98312 | tf_op jit(solution)/shard_map/ppermute | solution.py:18
  135.0 13.5 %collective-permute-start.20 = (f32[16,512]{1,0:T(8,128)S(1)}, f32[16,512]{1,0:T(8,128)S(1)}, u32[]{:S(2)}, u32[]{:S(2)}) collective-permute-start(f32[16,512]{1,0:T(8,128)S(1)} %add_add_fusion.1), channel_id=1, source_target_pairs={{256,0},{272,16},{288,32},{304,48},{320,64},{336,80},{352,96},{368... | collective-permute-start | bytes 98312 | tf_op jit(solution)/shard_map/ppermute | solution.py:18
  172.2 13.7 %collective-permute-start.27 = (f32[4,4,16,512]{3,2,1,0:T(8,128)S(1)}, f32[4,4,16,512]{3,2,1,0:T(8,128)S(1)}, u32[]{:S(2)}, u32[]{:S(2)}) collective-permute-start(f32[4,4,16,512]{3,2,1,0:T(8,128)S(1)} %pad_maximum_fusion.8), channel_id=1, source_target_pairs={{16,0},{0,16},{48,32},{32,48},{80,64},{64,80},{112,96},{96,112},{1... | collective-permute-start | bytes 1572872 | tf_op jit(solution)/shard_map/ppermute | solution.py:22
  183.4 154.7 %collective-permute-start.28 = (f32[4,4,56,512]{3,2,1,0:T(8,128)}, f32[4,4,56,512]{3,2,1,0:T(8,128)}, u32[]{:S(2)}, u32[]{:S(2)}) collective-permute-start(f32[4,4,56,512]{3,2,1,0:T(8,128)} %dynamic-slice_bitcast_fusion), channel_id=1, source_target_pairs={{16,0},{0,16},{48,32},{32,48},{80,64},{64,80},{112,96},{96,112},{1... | collective-permute-start | bytes 5505032 | tf_op jit(solution)/shard_map/ppermute | solution.py:22
  340.8 26.1 %collective-permute-start.29 = (f32[4,56,512]{2,1,0:T(8,128)S(1)}, f32[4,56,512]{2,1,0:T(8,128)S(1)}, u32[]{:S(2)}, u32[]{:S(2)}) collective-permute-start(f32[4,56,512]{2,1,0:T(8,128)S(1)} %get-tuple-element.23), channel_id=1, source_target_pairs={{32,0},{48,16},{64,32},{80,48},{96,64},{112,80},{128,96},{144,112}... | collective-permute-start | bytes 1376264 | tf_op jit(solution)/shard_map/ppermute | solution.py:18
  346.3 20.6 %collective-permute-start.30 = (f32[4,56,512]{2,1,0:T(8,128)S(1)}, f32[4,56,512]{2,1,0:T(8,128)S(1)}, u32[]{:S(2)}, u32[]{:S(2)}) collective-permute-start(f32[4,56,512]{2,1,0:T(8,128)S(1)} %get-tuple-element.24), channel_id=1, source_target_pairs={{480,0},{496,16},{0,32},{16,48},{32,64},{48,80},{64,96},{80,112},{... | collective-permute-start | bytes 1376264 | tf_op jit(solution)/shard_map/ppermute | solution.py:18
  348.7 17.3 %collective-permute-start.31 = (f32[2,56,512]{2,1,0:T(8,128)S(1)}, f32[2,56,512]{2,1,0:T(8,128)S(1)}, u32[]{:S(2)}, u32[]{:S(2)}) collective-permute-start(f32[2,56,512]{2,1,0:T(8,128)S(1)} %get-tuple-element.25), channel_id=1, source_target_pairs={{64,0},{80,16},{96,32},{112,48},{128,64},{144,80},{160,96},{176,11... | collective-permute-start | bytes 688136 | tf_op jit(solution)/shard_map/ppermute | solution.py:18
  352.8 14.1 %collective-permute-start.32 = (f32[2,56,512]{2,1,0:T(8,128)S(1)}, f32[2,56,512]{2,1,0:T(8,128)S(1)}, u32[]{:S(2)}, u32[]{:S(2)}) collective-permute-start(f32[2,56,512]{2,1,0:T(8,128)S(1)} %get-tuple-element.26), channel_id=1, source_target_pairs={{448,0},{464,16},{480,32},{496,48},{0,64},{16,80},{32,96},{48,112}... | collective-permute-start | bytes 688136 | tf_op jit(solution)/shard_map/ppermute | solution.py:18
  367.1 16.3 %collective-permute-start.33 = (f32[56,512]{1,0:T(8,128)S(1)}, f32[56,512]{1,0:T(8,128)S(1)}, u32[]{:S(2)}, u32[]{:S(2)}) collective-permute-start(f32[56,512]{1,0:T(8,128)S(1)} %get-tuple-element.43), channel_id=1, source_target_pairs={{128,0},{144,16},{160,32},{176,48},{192,64},{208,80},{224,96},{240... | collective-permute-start | bytes 344072 | tf_op jit(solution)/shard_map/ppermute | solution.py:18
  374.0 24.5 %collective-permute-start.34 = (f32[56,512]{1,0:T(8,128)S(1)}, f32[56,512]{1,0:T(8,128)S(1)}, u32[]{:S(2)}, u32[]{:S(2)}) collective-permute-start(f32[56,512]{1,0:T(8,128)S(1)} %get-tuple-element.45), channel_id=1, source_target_pairs={{256,0},{272,16},{288,32},{304,48},{320,64},{336,80},{352,96},{368... | collective-permute-start | bytes 344072 | tf_op jit(solution)/shard_map/ppermute | solution.py:18
  378.7 19.8 %collective-permute-start.35 = (f32[56,512]{1,0:T(8,128)S(1)}, f32[56,512]{1,0:T(8,128)S(1)}, u32[]{:S(2)}, u32[]{:S(2)}) collective-permute-start(f32[56,512]{1,0:T(8,128)S(1)} %get-tuple-element.44), channel_id=1, source_target_pairs={{384,0},{400,16},{416,32},{432,48},{448,64},{464,80},{480,96},{496... | collective-permute-start | bytes 344072 | tf_op jit(solution)/shard_map/ppermute | solution.py:18
  399.6 17.0 %collective-permute-start.36 = (bf16[56,512]{1,0:T(8,128)(2,1)S(1)}, bf16[56,512]{1,0:T(8,128)(2,1)S(1)}, u32[]{:S(2)}, u32[]{:S(2)}) collective-permute-start(bf16[56,512]{1,0:T(8,128)(2,1)S(1)} %convolution_convert_fusion.2), channel_id=1, source_target_pairs={{128,0},{144,16},{160,32},{176,48},{192,64},{208,80},{224,96},{240... | collective-permute-start | bytes 172040 | tf_op jit(solution)/shard_map/ppermute | solution.py:18
  407.4 14.0 %collective-permute-start.37 = (bf16[56,512]{1,0:T(8,128)(2,1)S(1)}, bf16[56,512]{1,0:T(8,128)(2,1)S(1)}, u32[]{:S(2)}, u32[]{:S(2)}) collective-permute-start(bf16[56,512]{1,0:T(8,128)(2,1)S(1)} %convolution_convert_fusion.2), channel_id=1, source_target_pairs={{256,0},{272,16},{288,32},{304,48},{320,64},{336,80},{352,96},{368... | collective-permute-start | bytes 172040 | tf_op jit(solution)/shard_map/ppermute | solution.py:18
  409.4 12.0 %collective-permute-start.38 = (bf16[56,512]{1,0:T(8,128)(2,1)S(1)}, bf16[56,512]{1,0:T(8,128)(2,1)S(1)}, u32[]{:S(2)}, u32[]{:S(2)}) collective-permute-start(bf16[56,512]{1,0:T(8,128)(2,1)S(1)} %convolution_convert_fusion.2), channel_id=1, source_target_pairs={{384,0},{400,16},{416,32},{432,48},{448,64},{464,80},{480,96},{496... | collective-permute-start | bytes 172040 | tf_op jit(solution)/shard_map/ppermute | solution.py:18
  421.5 22.5 %collective-permute-start.39 = (bf16[4,56,512]{2,1,0:T(8,128)(2,1)S(1)}, bf16[4,56,512]{2,1,0:T(8,128)(2,1)S(1)}, u32[]{:S(2)}, u32[]{:S(2)}) collective-permute-start(bf16[4,56,512]{2,1,0:T(8,128)(2,1)S(1)} %pad_maximum_fusion.10), channel_id=1, source_target_pairs={{32,0},{48,16},{64,32},{80,48},{96,64},{112,80},{128,96},{144,112}... | collective-permute-start | bytes 688136 | tf_op jit(solution)/shard_map/ppermute | solution.py:18
  427.6 16.4 %collective-permute-start.42 = (bf16[4,56,512]{2,1,0:T(8,128)(2,1)S(1)}, bf16[4,56,512]{2,1,0:T(8,128)(2,1)S(1)}, u32[]{:S(2)}, u32[]{:S(2)}) collective-permute-start(bf16[4,56,512]{2,1,0:T(8,128)(2,1)S(1)} %pad_maximum_fusion.10), channel_id=1, source_target_pairs={{480,0},{496,16},{0,32},{16,48},{32,64},{48,80},{64,96},{80,112},{... | collective-permute-start | bytes 688136 | tf_op jit(solution)/shard_map/ppermute | solution.py:18
  466.0 10.2 %collective-permute-start.47 = (f32[1,512]{1,0:T(1,128)S(1)}, f32[1,512]{1,0:T(1,128)S(1)}, u32[]{:S(2)}, u32[]{:S(2)}) collective-permute-start(f32[1,512]{1,0:T(1,128)S(1)} %add_add_fusion.2), channel_id=1, source_target_pairs={{4,0},{5,1},{6,2},{7,3},{8,4},{9,5},{10,6},{11,7},{12,8},{13,9},{1... | collective-permute-start | bytes 6152 | tf_op jit(solution)/shard_map/ppermute | solution.py:32
  (33 other events, 336.9 us)

commit v2 on v0

v2 whole, which is shorter than its diff:
```python
import math

import jax
import jax.numpy as jnp
from jax import lax
from jax.experimental import pallas as pl
from jax.experimental.pallas import tpu as pltpu
from jax.sharding import PartitionSpec as P

DM = 8192
DF = 28672
Z = 16
HI = lax.Precision.HIGHEST
F32 = jnp.float32
BF16 = jnp.bfloat16
B = 128

LINE = [[(4 * q + k) * 2 + c for k in range(4) for q in range(4)] for c in range(2)]
DEEP = [[z * 2 + c for z in range(Z)] for c in range(2)]
FAR = [[(4 * q + k) * 2 + c for q in range(4)] for k in range(4) for c in range(2)]
NEAR = [[(4 * q + k) * 2 + c for k in range(4)] for q in range(4) for c in range(2)]


def from_core(value):
    return lax.ppermute(value, "fsdp", [(i ^ 1, i) for i in range(2 * Z)])


def spread(value, axis, groups, size):
    return lax.all_to_all(
        jnp.broadcast_to(value, (size,) + value.shape), axis, 0, 0, axis_index_groups=groups
    )


def by_core(core, mine, other, axis):
    return jnp.stack(
        [jnp.where(core == 0, mine, other), jnp.where(core == 0, other, mine)], axis=axis
    )


def pick(array, place):
    return lax.dynamic_index_in_dim(array, place, 0, keepdims=False)


def factor_block(diag):
    sub = lax.broadcasted_iota(jnp.int32, (8, B), 0)
    lanes = lax.broadcasted_iota(jnp.int32, (8, B), 1)
    left = [diag[8 * i : 8 * i + 8] for i in range(B // 8)]
    right = [(lanes == sub + 8 * i).astype(F32) for i in range(B // 8)]
    done = []
    for p in range(B // 8):
        w, v = left[p], right[p]
        spread = lambda x, q: jnp.broadcast_to(x[:, 8 * p + q : 8 * p + q + 1], (8, B))
        full = lambda x, j: jnp.broadcast_to(x[j : j + 1], (8, B))
        cols = [spread(w, q) for q in range(8)]
        roots, above = [], {}
        for j in range(8):
            pivot = full(cols[j], j)
            root = lax.rsqrt(pivot)
            root = root * (1.5 - 0.5 * pivot * root * root)
            roots.append(root)
            col = jnp.where(sub > j, cols[j] * root, 0.0)
            for q in range(j + 1, 8):
                above[j, q] = full(cols[q], j) * root
                cols[q] = cols[q] - col * above[j, q]
            row = full(w, j) * root
            w = jnp.where(sub == j, row, w - col * row)
            row = full(v, j) * root
            v = jnp.where(sub == j, row, v - col * row)
        done.append(v)
        for i in range(p + 1, B // 8):
            a, e = left[i], right[i]
            cols = [spread(a, q) for q in range(8)]
            for j in range(8):
                col = cols[j] * roots[j]
                for q in range(j + 1, 8):
                    cols[q] = cols[q] - col * above[j, q]
                a = a - col * w[j : j + 1]
                e = e - col * v[j : j + 1]
            left[i], right[i] = a, e
    return jnp.concatenate(done)


def inverse_kernel(gram_ref, out_ref, work):
    work[...] = gram_ref[...]
    r = lax.broadcasted_iota(jnp.int32, (512, 512), 0)
    c = lax.broadcasted_iota(jnp.int32, (512, 512), 1)
    out_ref[...] = (r == c).astype(F32)

    @pl.loop(0, 4)
    def _(b):
        at = pl.multiple_of(b * B, B)
        rows = pl.ds(at, B)
        inv = factor_block(work[rows, pl.ds(at, B)])
        upper = jnp.dot(inv, work[rows, :], precision=HI, preferred_element_type=F32)
        lower = jnp.dot(inv, out_ref[rows, :], precision=HI, preferred_element_type=F32)
        out_ref[rows, :] = lower

        @pl.when(b < 3)
        def _():
            lane = lax.broadcasted_iota(jnp.int32, (B, 512), 1)
            coef = jnp.where(lane >= at + B, upper, 0.0)
            tn = lambda x, y: lax.dot_general(
                x, y, (((0,), (0,)), ((), ())), precision=HI, preferred_element_type=F32
            )
            work[...] = work[...] - tn(coef, upper)
            out_ref[...] = out_ref[...] - tn(coef, lower)


def inverse_factor(gram):
    return pl.pallas_call(
        inverse_kernel,
        out_shape=jax.ShapeDtypeStruct((512, 512), F32),
        in_specs=[pl.BlockSpec(memory_space=pltpu.VMEM)],
        out_specs=pl.BlockSpec(memory_space=pltpu.VMEM),
        scratch_shapes=[pltpu.VMEM((512, 512), F32)],
        compiler_params=pltpu.CompilerParams(vmem_limit_bytes=24 * 1024 * 1024),
        cost_estimate=pl.CostEstimate(flops=6 * 10**8, bytes_accessed=3 * 2**20, transcendentals=512),
        name="inverse_factor",
    )(gram)


def nt(a, b, precision=None):
    return lax.dot_general(
        a, b, (((1,), (1,)), ((), ())), precision=precision, preferred_element_type=F32
    )


def tn(a, b):
    return lax.dot_general(a, b, (((0,), (0,)), ((), ())), preferred_element_type=F32)


def local(momentum, gradient, weight, right_factor):
    fsdp, tp = lax.axis_index("fsdp"), lax.axis_index("tp")
    core = fsdp % 2

    blend = (momentum.astype(F32) + gradient.astype(F32)).astype(BF16)

    mine = lax.all_gather(right_factor, "fsdp", axis_index_groups=DEEP)
    factor = by_core(core, mine, from_core(mine), 1).reshape(512, -1)
    partial = nt(blend, factor)
    pieces = lax.all_to_all(partial.reshape(16, 16, 512), "tp", 0, 0)
    start = spread(jnp.sum(pieces, axis=0), "tp", None, 16).reshape(256, 512)

    high = start.astype(BF16)
    low = (start - high.astype(F32)).astype(BF16)
    cross = (tn(blend, high) + tn(blend, low)).reshape(2, 16, 56, 512)
    cross = pick(cross, core) + from_core(pick(cross, 1 - core))
    cross = lax.psum_scatter(cross, "fsdp", scatter_dimension=0, axis_index_groups=LINE)

    gram = jnp.dot(start.T, start, precision=HI)
    band = pick(gram.reshape(16, 2, 16, 512), tp)
    band = pick(band, core) + from_core(pick(band, 1 - core))
    band = jnp.sum(spread(band, "fsdp", NEAR, 4), axis=0)
    band = jnp.sum(spread(band, "fsdp", FAR, 4), axis=0)
    mine = spread(band, "tp", None, 16)
    gram = by_core(core, mine, from_core(mine), 1).reshape(512, 512)

    inverse = inverse_factor(gram)
    chunk = nt(cross, inverse, HI).astype(BF16)
    mine = spread(spread(chunk, "fsdp", FAR, 4), "fsdp", NEAR, 4)
    project = by_core(core, mine, from_core(mine), 0).reshape(1792, 512)
    basis = nt(start, inverse, HI).astype(BF16)

    wide = project.astype(F32)
    squares = jnp.sum(wide * wide, axis=0, keepdims=True)
    squares = jnp.sum(spread(squares, "tp", None, 16), axis=0)
    rms = jnp.sqrt(squares / DF + 1e-06)
    factor_t = (wide / rms).astype(BF16)
    chosen = (jnp.arange(512)[None, :] == 16 * fsdp + jnp.arange(16)[:, None]).astype(BF16)
    new_factor = nt(chosen, factor_t).astype(BF16)
    new_momentum = (blend.astype(F32) - 0.4 * nt(basis, project)).astype(BF16)
    new_weight = (
        weight.astype(F32) - 2.0 * math.sqrt(DM / DF) * nt(basis, factor_t)
    ).astype(BF16)
    return (new_momentum, new_weight, new_factor)


def solution(mesh):
    placed = (P("fsdp", "tp"), P("fsdp", "tp"), P("fsdp", "tp"), P("fsdp", "tp"))
    return jax.shard_map(
        local,
        mesh=mesh,
        in_specs=placed,
        out_specs=(P("fsdp", "tp"), P("fsdp", "tp"), P("fsdp", "tp")),
        check_vma=False,
    )
```

time: 830 us -> 298 us (0.36)
  waiting for transfers between devices: 620 us -> 43.3 us
  other arithmetic: 123 us -> 7.91 us
  blocking collectives: 32.9 us -> 136 us
  starting transfers between devices: 0.24 us -> 51.5 us
  Pallas kernels: 0 us -> 28.1 us
  matrix products: 23.8 us -> 11.2 us
    psum x2 -> x0, waiting for transfers between devices: 323 us -> none  [the longest x1 211 us: local(): gram_matrix = lax.psum(gram_local, 'fsdp')]
    all_gather x3 -> x0, waiting for transfers between devices: 187 us -> none  [the longest x1 79.5 us: local(): lax.all_gather(right_factor, 'fsdp', axis=0, tiled=True)]
    another operation x17 -> x6, other arithmetic: 120 us -> 2 us  [by_core(): jnp.stack([jnp.where(core == 0, mine, other), jnp.where(core == 0, other,...]
    all_to_all x0 -> x6, blocking collectives: none -> 101 us  [the longest x5 83.4 us: spread(): lax.all_to_all(jnp.broadcast_to(value, (size,) + value.shape), axis, 0, 0...]
    reduce_scatter x1, waiting for transfers between devices: 110 us -> 21.9 us  [local(): lax.psum_scatter(cross, 'fsdp', scatter_dimension=0, axis_index_groups=LINE)]
    ppermute x0 -> x5, starting transfers between devices: none -> 39.1 us  [from_core(): return lax.ppermute(value, 'fsdp', [(i ^ 1, i) for i in range(2 * Z)])]
    all_gather x0 -> x1, blocking collectives: none -> 34.9 us  [local(): mine = lax.all_gather(right_factor, 'fsdp', axis_index_groups=DEEP)]
    psum x1 -> x0, blocking collectives: 32.9 us -> none  [local(): squares = lax.psum(jnp.sum(widened * widened, axis=1), 'tp')]
  transfers between devices with their start and end apart: 6 -> 8, of which waited for: 6 -> 8; matrix products, arithmetic and copies ran while one was open for 1% -> 2% of each run, Pallas kernels for 0% -> 9%
where the time goes in v2:
time: 298 us; the launch traced here: 297 us
  blocking collectives  136 us (46%)
  starting transfers between devices  51.5 us (17%)
  waiting for transfers between devices  43.3 us (15%)
  Pallas kernels  28.1 us (9%)
  between operations  14.3 us (5%)
  matrix products  11.2 us (4%)
  other arithmetic  7.91 us (3%)
  local copies, waits for them, and re-layouts  4.89 us (2%)
    all_to_all x5, blocking collectives, spread(): lax.all_to_all(jnp.broadcast_to(value, (size,) + value.shape), axis, 0, 0...  83.4 us
    ppermute x5, starting transfers between devices, from_core(): return lax.ppermute(value, 'fsdp', [(i ^ 1, i) for i in range(2 * Z)])  39.1 us
    all_gather x1, blocking collectives, local(): mine = lax.all_gather(right_factor, 'fsdp', axis_index_groups=DEEP)  34.9 us
    pallas_call x1, Pallas kernels, inverse_factor(): pl.pallas_call(inverse_kernel, out_shape=jax.ShapeDtypeStruct((512, 512),...  28.1 us
    reduce_scatter x1, waiting for transfers between devices, local(): lax.psum_scatter(cross, 'fsdp', scatter_dimension=0, axis_index_groups=LINE)  21.9 us
    all_to_all x1, blocking collectives, local(): pieces = lax.all_to_all(partial.reshape(16, 16, 512), 'tp', 0, 0)  17.3 us
    all_to_all x2, waiting for transfers between devices, spread(): lax.all_to_all(jnp.broadcast_to(value, (size,) + value.shape), axis, 0, 0...  14.7 us
    all_to_all x2, starting transfers between devices, spread(): lax.all_to_all(jnp.broadcast_to(value, (size,) + value.shape), axis, 0, 0...  12.3 us
  transfers between devices with their start and end apart: 8, of which 8 were waited for; matrix products, arithmetic and copies ran while one was open for 2% of the time, Pallas kernels for 9%

profile of v2, /device:TPU:1, one launch (start us, length us, event | category | flops | bytes accessed | tf_op | source)
XLA Modules:
  0.0 296.8 jit_solution(16904220514518862362)
XLA Ops:
  7.2 34.9 %all-gather = bf16[256,1792]{1,0:T(8,128)(2,1)S(1)} all-gather(bf16[16,1792]{1,0:T(8,128)(2,1)} %param.7), channel_id=2, replica_groups={{0,32,64,96,128,160,192,224,256,288,320,352,384,416,448,480},{16,48,80,..., dimensions={0}, use_global_device_ids=true | all-gather | bytes 974848 | tf_op jit(solution)/shard_map/all_gather | solution.py:138
  42.0 9.5 %collective-permute-start = (bf16[16,16,1792]{2,1,0:T(8,128)(2,1)S(1)}, bf16[16,16,1792]{2,1,0:T(8,128)(2,1)S(1)}, u32[]{:S(2)}, u32[]{:S(2)}) collective-permute-start(bf16[16,16,1792]{2,1,0:T(8,128)(2,1)S(1)} %bitcast.69), channel_id=1, source_target_pairs={{16,0},{0,16},{48,32},{32,48},{80,64},{64,80},{112,96},{96,112},{1... | collective-permute-start | bytes 2752520 | tf_op jit(solution)/shard_map/ppermute | solution.py:25
  51.5 1.7 add_convert_fusion
  54.6 17.3 %all_to_all.40 = f32[16,16,512]{2,1,0:T(8,128)S(1)} all-to-all(f32[16,16,512]{2,1,0:T(8,128)S(1)} %fusion.9), channel_id=1, replica_groups=mesh['fsdp'=32,'tp'=16] {'tp'}, dimensions={0} | all-to-all | bytes 1048576 | tf_op jit(solution)/shard_map/all_to_all | solution.py:141
  72.7 3.6 %all-to-all-start.1 = ((f32[16,16,512]{2,1,0:T(8,128)}), f32[16,16,512]{2,1,0:T(8,128)S(1)}, u32[]{:S(2)}, u32[]{:S(2)}) async-start(f32[16,16,512]{2,1,0:T(8,128)} %broadcast_in_dim.24), calls=%async_computation.1 | async-start | bytes 1048576 | tf_op jit(solution)/shard_map/all_to_all | solution.py:29
  76.4 9.9 %all-to-all-done.1 = f32[16,16,512]{2,1,0:T(8,128)S(1)} async-done(((f32[16,16,512]{2,1,0:T(8,128)}), f32[16,16,512]{2,1,0:T(8,128)S(1)}, u32[]{:S(2)}, u32[]{:S(2)}) %all-to-all-start.1) | async-done | bytes 524320 | tf_op jit(solution)/shard_map/all_to_all | solution.py:29
  90.0 4.4 %collective-permute-start.3 = (f32[16,56,512]{2,1,0:T(8,128)}, f32[16,56,512]{2,1,0:T(8,128)S(1)}, u32[]{:S(2)}, u32[]{:S(2)}) collective-permute-start(f32[16,56,512]{2,1,0:T(8,128)} %dynamic-slice_bitcast_fusion), channel_id=1, source_target_pairs={{16,0},{0,16},{48,32},{32,48},{80,64},{64,80},{112,96},{96,112},{1... | collective-permute-start | bytes 5505032 | tf_op jit(solution)/shard_map/ppermute | solution.py:25
  94.4 3.6 %collective-permute-done.3 = f32[16,56,512]{2,1,0:T(8,128)S(1)} collective-permute-done((f32[16,56,512]{2,1,0:T(8,128)}, f32[16,56,512]{2,1,0:T(8,128)S(1)}, u32[]{:S(2)}, u32[]{:S(2)}) %collective-permute-start.3) | collective-permute-done | bytes 1835040 | tf_op jit(solution)/shard_map/ppermute | solution.py:25
  98.0 3.1 %bitcast_add_fusion = f32[16,56,512]{2,1,0:T(8,128)} fusion(f32[16,56,512]{2,1,0:T(8,128)S(1)} %collective-permute-done.3, f32[2,16,56,512]{3,2,1,0:T(8,128)} %bitcast.67, s32[]{:T(128)S(6)} %select_n.70), kind=kLoop, calls=%fused_computation.12 | loop fusion | flops 458752 | bytes 5505028 | tf_op jit(solution)/shard_map/add | solution.py:147
  102.5 2.3 collective-permute-start.1
  105.6 7.3 %all_to_all.41 = f32[4,16,512]{2,1,0:T(8,128)S(1)} all-to-all(f32[4,16,512]{2,1,0:T(8,128)S(1)} %broadcast_in_dim.25), channel_id=1, replica_groups={{0,32,64,96},{16,48,80,112},{128,160,192,224},{144,176,208,240},{256,28..., dimensions={0} | all-to-all | bytes 262144 | tf_op jit(solution)/shard_map/all_to_all | solution.py:29
  112.9 22.3 %all_to_all.42 = f32[4,16,512]{2,1,0:T(8,128)S(1)} all-to-all(f32[4,16,512]{2,1,0:T(8,128)S(1)} %broadcast_in_dim.26), channel_id=1, replica_groups={{0,128,256,384},{16,144,272,400},{32,160,288,416},{48,176,304,432},{64,..., dimensions={0} | all-to-all | bytes 262144 | tf_op jit(solution)/shard_map/all_to_all | solution.py:29
  135.2 14.3 %all_to_all.43 = f32[16,16,512]{2,1,0:T(8,128)S(1)} all-to-all(f32[16,16,512]{2,1,0:T(8,128)S(1)} %broadcast_in_dim.27), channel_id=1, replica_groups=mesh['fsdp'=32,'tp'=16] {'tp'}, dimensions={0} | all-to-all | bytes 1048576 | tf_op jit(solution)/shard_map/all_to_all | solution.py:29
  149.5 10.4 %collective-permute-start.2 = (f32[16,16,512]{2,1,0:T(8,128)S(1)}, f32[16,16,512]{2,1,0:T(8,128)S(1)}, u32[]{:S(2)}, u32[]{:S(2)}) collective-permute-start(f32[16,16,512]{2,1,0:T(8,128)S(1)} %all_to_all.43), channel_id=1, source_target_pairs={{16,0},{0,16},{48,32},{32,48},{80,64},{64,80},{112,96},{96,112},{1... | collective-permute-start | bytes 1572872 | tf_op jit(solution)/shard_map/ppermute | solution.py:25
  161.5 28.1 %inverse_factor.1 = f32[512,512]{1,0:T(8,128)S(1)} custom-call(f32[512,512]{1,0:T(8,128)S(1)} %bitcast.58), custom_call_target="tpu_custom_call" | custom-call | flops 600000000 | bytes 3145728 | tf_op jit(solution)/shard_map/inverse_factor/pallas_call | solution.py:110
  189.7 21.9 %reduce-scatter.2.cloned.1.call-done = f32[1,56,512]{2,1,0:T(8,128)} async-done(((f32[16,56,512]{2,1,0:T(8,128)}), f32[1,56,512]{2,1,0:T(8,128)}) %reduce-scatter.2.cloned.1.call-update) | async-done | bytes 114704 | tf_op jit(solution)/shard_map/reduce_scatter | solution.py:148
  211.6 2.0 convolution_convert_fusion.2
  213.6 21.9 %all_to_all.44 = bf16[4,56,512]{2,1,0:T(8,128)(2,1)S(1)} all-to-all(bf16[4,56,512]{2,1,0:T(8,128)(2,1)S(1)} %broadcast_in_dim.28), channel_id=1, replica_groups={{0,128,256,384},{16,144,272,400},{32,160,288,416},{48,176,304,432},{64,..., dimensions={0} | all-to-all | bytes 458752 | tf_op jit(solution)/shard_map/all_to_all | solution.py:29
  235.6 17.7 %all_to_all.45 = bf16[4,4,56,512]{3,2,1,0:T(8,128)(2,1)S(1)} all-to-all(bf16[4,4,56,512]{3,2,1,0:T(8,128)(2,1)S(1)} %broadcast_in_dim.29), channel_id=1, replica_groups={{0,32,64,96},{16,48,80,112},{128,160,192,224},{144,176,208,240},{256,28..., dimensions={0} | all-to-all | bytes 1835008 | tf_op jit(solution)/shard_map/all_to_all | solution.py:29
  253.4 12.5 %collective-permute-start.4 = (bf16[4,4,56,512]{3,2,1,0:T(8,128)(2,1)S(1)}, bf16[4,4,56,512]{3,2,1,0:T(8,128)(2,1)}, u32[]{:S(2)}, u32[]{:S(2)}) collective-permute-start(bf16[4,4,56,512]{3,2,1,0:T(8,128)(2,1)S(1)} %all_to_all.45), channel_id=1, source_target_pairs={{16,0},{0,16},{48,32},{32,48},{80,64},{64,80},{112,96},{96,112},{1... | collective-permute-start | bytes 2752520 | tf_op jit(solution)/shard_map/ppermute | solution.py:25
  265.9 1.8 convolution_convert_fusion.1
  270.7 8.7 %all-to-all-start.7 = ((f32[16,1,512]{2,1,0:T(1,128)}), f32[16,1,512]{2,1,0:T(1,128)S(1)}, u32[]{:S(2)}, u32[]{:S(2)}) async-start(f32[16,1,512]{2,1,0:T(1,128)} %broadcast_in_dim.30), calls=%async_computation.8 | async-start | bytes 65536 | tf_op jit(solution)/shard_map/all_to_all | solution.py:29
  279.4 1.6 fusion.2
  281.0 4.8 %all-to-all-done.7 = f32[16,1,512]{2,1,0:T(1,128)S(1)} async-done(((f32[16,1,512]{2,1,0:T(1,128)}), f32[16,1,512]{2,1,0:T(1,128)S(1)}, u32[]{:S(2)}, u32[]{:S(2)}) %all-to-all-start.7) | async-done | bytes 32800 | tf_op jit(solution)/shard_map/all_to_all | solution.py:29
  (43 shorter events, 16.9 us)
Async XLA Ops:
  42.0 11.6 %collective-permute-start = (bf16[16,16,1792]{2,1,0:T(8,128)(2,1)S(1)}, bf16[16,16,1792]{2,1,0:T(8,128)(2,1)S(1)}, u32[]{:S(2)}, u32[]{:S(2)}) collective-permute-start(bf16[16,16,1792]{2,1,0:T(8,128)(2,1)S(1)} %bitcast.69), channel_id=1, source_target_pairs={{16,0},{0,16},{48,32},{32,48},{80,64},{64,80},{112,96},{96,112},{1... | collective-permute-start | bytes 2752520 | tf_op jit(solution)/shard_map/ppermute | solution.py:25
  72.7 13.5 %all-to-all-start.1 = ((f32[16,16,512]{2,1,0:T(8,128)}), f32[16,16,512]{2,1,0:T(8,128)S(1)}, u32[]{:S(2)}, u32[]{:S(2)}) async-start(f32[16,16,512]{2,1,0:T(8,128)} %broadcast_in_dim.24), calls=%async_computation.1 | async-start | bytes 1048576 | tf_op jit(solution)/shard_map/all_to_all | solution.py:29
  76.3 135.3 %reduce-scatter.2.cloned.1.call-start = ((), (), s32[]{:S(2)}) async-start(), calls=%async_computation.9 | async-start | bytes 1949696 | tf_op jit(solution)/shard_map/reduce_scatter | solution.py:148
  87.6 2.4 copy-start
  90.0 8.0 %collective-permute-start.3 = (f32[16,56,512]{2,1,0:T(8,128)}, f32[16,56,512]{2,1,0:T(8,128)S(1)}, u32[]{:S(2)}, u32[]{:S(2)}) collective-permute-start(f32[16,56,512]{2,1,0:T(8,128)} %dynamic-slice_bitcast_fusion), channel_id=1, source_target_pairs={{16,0},{0,16},{48,32},{32,48},{80,64},{64,80},{112,96},{96,112},{1... | collective-permute-start | bytes 5505032 | tf_op jit(solution)/shard_map/ppermute | solution.py:25
  102.5 3.1 %collective-permute-start.1 = (f32[16,512]{1,0:T(8,128)S(1)}, f32[16,512]{1,0:T(8,128)S(1)}, u32[]{:S(2)}, u32[]{:S(2)}) collective-permute-start(f32[16,512]{1,0:T(8,128)S(1)} %dynamic-slice_bitcast_fusion.1), channel_id=1, source_target_pairs={{16,0},{0,16},{48,32},{32,48},{80,64},{64,80},{112,96},{96,112},{1... | collective-permute-start | bytes 98312 | tf_op jit(solution)/shard_map/ppermute | solution.py:25
  149.5 11.8 %collective-permute-start.2 = (f32[16,16,512]{2,1,0:T(8,128)S(1)}, f32[16,16,512]{2,1,0:T(8,128)S(1)}, u32[]{:S(2)}, u32[]{:S(2)}) collective-permute-start(f32[16,16,512]{2,1,0:T(8,128)S(1)} %all_to_all.43), channel_id=1, source_target_pairs={{16,0},{0,16},{48,32},{32,48},{80,64},{64,80},{112,96},{96,112},{1... | collective-permute-start | bytes 1572872 | tf_op jit(solution)/shard_map/ppermute | solution.py:25
  253.4 14.7 %collective-permute-start.4 = (bf16[4,4,56,512]{3,2,1,0:T(8,128)(2,1)S(1)}, bf16[4,4,56,512]{3,2,1,0:T(8,128)(2,1)}, u32[]{:S(2)}, u32[]{:S(2)}) collective-permute-start(bf16[4,4,56,512]{3,2,1,0:T(8,128)(2,1)S(1)} %all_to_all.45), channel_id=1, source_target_pairs={{16,0},{0,16},{48,32},{32,48},{80,64},{64,80},{112,96},{96,112},{1... | collective-permute-start | bytes 2752520 | tf_op jit(solution)/shard_map/ppermute | solution.py:25
  269.9 9.5 %copy-start.1 = (bf16[256,512]{1,0:T(8,128)(2,1)S(1)}, bf16[256,512]{1,0:T(8,128)(2,1)}, u32[]{:S(2)}) copy-start(bf16[256,512]{1,0:T(8,128)(2,1)} %convolution_convert_fusion.1) | copy-start | bytes 786436
  270.7 15.2 %all-to-all-start.7 = ((f32[16,1,512]{2,1,0:T(1,128)}), f32[16,1,512]{2,1,0:T(1,128)S(1)}, u32[]{:S(2)}, u32[]{:S(2)}) async-start(f32[16,1,512]{2,1,0:T(1,128)} %broadcast_in_dim.30), calls=%async_computation.8 | async-start | bytes 65536 | tf_op jit(solution)/shard_map/all_to_all | solution.py:29
  285.9 1.2 copy-start.2
Sparse Core Ops, SparseCore 0:
  101.3 110.2 reduce-scatter.1

commit v3 on v2

--- a/solution.py
+++ b/solution.py
@@ -15,10 +15,7 @@
 BF16 = jnp.bfloat16
 B = 128
 
-LINE = [[(4 * q + k) * 2 + c for k in range(4) for q in range(4)] for c in range(2)]
 DEEP = [[z * 2 + c for z in range(Z)] for c in range(2)]
-FAR = [[(4 * q + k) * 2 + c for q in range(4)] for k in range(4) for c in range(2)]
-NEAR = [[(4 * q + k) * 2 + c for k in range(4)] for q in range(4) for c in range(2)]
 
 
 def from_core(value):
@@ -55,13 +52,13 @@
         roots, above = [], {}
         for j in range(8):
             pivot = full(cols[j], j)
-            root = lax.rsqrt(pivot)
-            root = root * (1.5 - 0.5 * pivot * root * root)
+            root, inv = lax.rsqrt(pivot), pl.reciprocal(pivot, approx=True)
             roots.append(root)
+            for q in range(j + 1, 8):
+                across = full(cols[q], j)
+                above[j, q] = across * root
+                cols[q] = cols[q] - (cols[j] * across) * inv
             col = jnp.where(sub > j, cols[j] * root, 0.0)
-            for q in range(j + 1, 8):
-                above[j, q] = full(cols[q], j) * root
-                cols[q] = cols[q] - col * above[j, q]
             row = full(w, j) * root
             w = jnp.where(sub == j, row, w - col * row)
             row = full(v, j) * root
@@ -135,30 +132,37 @@
 
     blend = (momentum.astype(F32) + gradient.astype(F32)).astype(BF16)
 
-    mine = lax.all_gather(right_factor, "fsdp", axis_index_groups=DEEP)
-    factor = by_core(core, mine, from_core(mine), 1).reshape(512, -1)
+    half = blend.shape[1] // 2
+    columns = lambda place: lax.dynamic_slice_in_dim(blend, place * half, half, axis=1)
+    mine, other = columns(core), from_core(columns(1 - core))
+
+    rows = lax.all_gather(right_factor, "fsdp", axis_index_groups=DEEP)
+    factor = by_core(core, rows, from_core(rows), 1).reshape(512, -1)
     partial = nt(blend, factor)
     pieces = lax.all_to_all(partial.reshape(16, 16, 512), "tp", 0, 0)
     start = spread(jnp.sum(pieces, axis=0), "tp", None, 16).reshape(256, 512)
+    second = from_core(start)
 
-    high = start.astype(BF16)
-    low = (start - high.astype(F32)).astype(BF16)
-    cross = (tn(blend, high) + tn(blend, low)).reshape(2, 16, 56, 512)
-    cross = pick(cross, core) + from_core(pick(cross, 1 - core))
-    cross = lax.psum_scatter(cross, "fsdp", scatter_dimension=0, axis_index_groups=LINE)
+    def parts(array):
+        high = array.astype(BF16)
+        return high, (array - high.astype(F32)).astype(BF16)
 
-    gram = jnp.dot(start.T, start, precision=HI)
-    band = pick(gram.reshape(16, 2, 16, 512), tp)
-    band = pick(band, core) + from_core(pick(band, 1 - core))
-    band = jnp.sum(spread(band, "fsdp", NEAR, 4), axis=0)
-    band = jnp.sum(spread(band, "fsdp", FAR, 4), axis=0)
-    mine = spread(band, "tp", None, 16)
-    gram = by_core(core, mine, from_core(mine), 1).reshape(512, 512)
+    cross = sum(tn(mine, part) for part in parts(start))
+    cross = cross + sum(tn(other, part) for part in parts(second))
+    cross = lax.psum_scatter(
+        cross.reshape(16, 56, 512), "fsdp", scatter_dimension=0, axis_index_groups=DEEP
+    )
+
+    gram = jnp.dot(start.T, start, precision=HI) + jnp.dot(second.T, second, precision=HI)
+    band = pick(gram.reshape(32, 16, 512), 2 * tp + core)
+    band = jnp.sum(lax.all_gather(band, "fsdp", axis_index_groups=DEEP), axis=0)
+    bands = spread(band, "tp", None, 16)
+    gram = by_core(core, bands, from_core(bands), 1).reshape(512, 512)
 
     inverse = inverse_factor(gram)
     chunk = nt(cross, inverse, HI).astype(BF16)
-    mine = spread(spread(chunk, "fsdp", FAR, 4), "fsdp", NEAR, 4)
-    project = by_core(core, mine, from_core(mine), 0).reshape(1792, 512)
+    rows = lax.all_gather(chunk, "fsdp", axis_index_groups=DEEP)
+    project = by_core(core, rows, from_core(rows), 0).reshape(1792, 512)
     basis = nt(start, inverse, HI).astype(BF16)
 
     wide = project.astype(F32)

time: 298 us -> 233 us (0.78)
  waiting for transfers between devices: 43.3 us -> 13.7 us
  blocking collectives: 136 us -> 115 us
  starting transfers between devices: 51.5 us -> 43.3 us
  Pallas kernels: 28.1 us -> 24.5 us
  other arithmetic: 7.91 us -> 4.77 us
    all_to_all x5 -> x1, blocking collectives: 83.4 us -> 11.6 us  [spread(): lax.all_to_all(jnp.broadcast_to(value, (size,) + value.shape), axis, 0, 0...]
    all_gather x1 -> x3, blocking collectives: 34.9 us -> 86.6 us  [the longest x1 34.9 us: local(): rows = lax.all_gather(right_factor, 'fsdp', axis_index_groups=DEEP)]
    reduce_scatter x1, waiting for transfers between devices: 21.9 us -> 0.02 us  [local(): lax.psum_scatter(cross.reshape(16, 56, 512), 'fsdp', scatter_dimension=0,...]
    all_to_all x2, starting transfers between devices: 12.3 us -> 7.07 us  [spread(): lax.all_to_all(jnp.broadcast_to(value, (size,) + value.shape), axis, 0, 0...]
    ppermute x5, waiting for transfers between devices: 6.58 us -> 2.77 us  [from_core(): return lax.ppermute(value, 'fsdp', [(i ^ 1, i) for i in range(2 * Z)])]
    all_to_all x2, waiting for transfers between devices: 14.7 us -> 10.9 us  [spread(): lax.all_to_all(jnp.broadcast_to(value, (size,) + value.shape), axis, 0, 0...]
    pallas_call x1, Pallas kernels: 28.1 us -> 24.5 us  [inverse_factor(): pl.pallas_call(inverse_kernel, out_shape=jax.ShapeDtypeStruct((512, 512),...]
    add x2 -> x0, other arithmetic: 3.15 us -> none  [the longest x1 3.15 us: local(): cross = pick(cross, core) + from_core(pick(cross, 1 - core))]
  transfers between devices with their start and end apart: 8 -> 8, of which waited for: 8 -> 6; matrix products, arithmetic and copies ran while one was open for 2% -> 4% of each run, Pallas kernels for 9% -> 11%
where the time goes in v3:
time: 233 us; the launch traced here: 232 us
  blocking collectives  115 us (49%)
  starting transfers between devices  43.3 us (19%)
  Pallas kernels  24.5 us (11%)
  between operations  14.3 us (6%)
  matrix products  13.9 us (6%)
  waiting for transfers between devices  13.7 us (6%)
  other arithmetic  4.77 us (2%)
    ppermute x5, starting transfers between devices, from_core(): return lax.ppermute(value, 'fsdp', [(i ^ 1, i) for i in range(2 * Z)])  36.2 us
    all_gather x1, blocking collectives, local(): rows = lax.all_gather(right_factor, 'fsdp', axis_index_groups=DEEP)  34.9 us
    all_gather x1, blocking collectives, local(): rows = lax.all_gather(chunk, 'fsdp', axis_index_groups=DEEP)  25.9 us
    all_gather x1, blocking collectives, local(): band = jnp.sum(lax.all_gather(band, 'fsdp', axis_index_groups=DEEP), axis=0)  25.8 us
    pallas_call x1, Pallas kernels, inverse_factor(): pl.pallas_call(inverse_kernel, out_shape=jax.ShapeDtypeStruct((512, 512),...  24.5 us
    all_to_all x1, blocking collectives, local(): pieces = lax.all_to_all(partial.reshape(16, 16, 512), 'tp', 0, 0)  17.3 us
    all_to_all x1, blocking collectives, spread(): lax.all_to_all(jnp.broadcast_to(value, (size,) + value.shape), axis, 0, 0...  11.6 us
    all_to_all x2, waiting for transfers between devices, spread(): lax.all_to_all(jnp.broadcast_to(value, (size,) + value.shape), axis, 0, 0...  10.9 us
  transfers between devices with their start and end apart: 8, of which 6 were waited for; matrix products, arithmetic and copies ran while one was open for 4% of the time, Pallas kernels for 11%

profile of v3, /device:TPU:1, one launch (start us, length us, event | category | flops | bytes accessed | tf_op | source)
XLA Modules:
  0.0 232.3 jit_solution(8911663922402547814)
XLA Ops:
  7.2 34.9 %all-gather = bf16[256,1792]{1,0:T(8,128)(2,1)S(1)} all-gather(bf16[16,1792]{1,0:T(8,128)(2,1)} %param.7), channel_id=2, replica_groups={{0,32,64,96,128,160,192,224,256,288,320,352,384,416,448,480},{16,48,80,..., dimensions={0}, use_global_device_ids=true | all-gather | bytes 974848 | tf_op jit(solution)/shard_map/all_gather | solution.py:139
  42.0 9.5 %collective-permute-start = (bf16[16,16,1792]{2,1,0:T(8,128)(2,1)S(1)}, bf16[16,16,1792]{2,1,0:T(8,128)(2,1)S(1)}, u32[]{:S(2)}, u32[]{:S(2)}) collective-permute-start(bf16[16,16,1792]{2,1,0:T(8,128)(2,1)S(1)} %bitcast.58), channel_id=1, source_target_pairs={{16,0},{0,16},{48,32},{32,48},{80,64},{64,80},{112,96},{96,112},{1... | collective-permute-start | bytes 2752520 | tf_op jit(solution)/shard_map/ppermute | solution.py:22
  51.5 1.7 add_convert_fusion
  54.6 17.3 %all_to_all.20 = f32[16,16,512]{2,1,0:T(8,128)S(1)} all-to-all(f32[16,16,512]{2,1,0:T(8,128)S(1)} %fusion.17), channel_id=1, replica_groups=mesh['fsdp'=32,'tp'=16] {'tp'}, dimensions={0} | all-to-all | bytes 1048576 | tf_op jit(solution)/shard_map/all_to_all | solution.py:142
  72.7 3.6 %all-to-all-start.1 = ((f32[16,16,512]{2,1,0:T(8,128)}), f32[16,16,512]{2,1,0:T(8,128)S(1)}, u32[]{:S(2)}, u32[]{:S(2)}) async-start(f32[16,16,512]{2,1,0:T(8,128)} %broadcast_in_dim.12), calls=%async_computation.1 | async-start | bytes 1048576 | tf_op jit(solution)/shard_map/all_to_all | solution.py:26
  76.4 3.7 %collective-permute-start.3 = (bf16[256,896]{1,0:T(8,128)(2,1)S(1)}, bf16[256,896]{1,0:T(8,128)(2,1)S(1)}, u32[]{:S(2)}, u32[]{:S(2)}) collective-permute-start(bf16[256,896]{1,0:T(8,128)(2,1)S(1)} %constant_dynamic-slice_fusion), channel_id=1, source_target_pairs={{16,0},{0,16},{48,32},{32,48},{80,64},{64,80},{112,96},{96,112},{1... | collective-permute-start | bytes 1376264 | tf_op jit(solution)/shard_map/ppermute | solution.py:22
  80.1 6.2 %all-to-all-done.1 = f32[16,16,512]{2,1,0:T(8,128)S(1)} async-done(((f32[16,16,512]{2,1,0:T(8,128)}), f32[16,16,512]{2,1,0:T(8,128)S(1)}, u32[]{:S(2)}, u32[]{:S(2)}) %all-to-all-start.1) | async-done | bytes 524320 | tf_op jit(solution)/shard_map/all_to_all | solution.py:26
  86.3 4.4 %collective-permute-start.1 = (f32[256,512]{1,0:T(8,128)S(1)}, f32[256,512]{1,0:T(8,128)S(1)}, u32[]{:S(2)}, u32[]{:S(2)}) collective-permute-start(f32[256,512]{1,0:T(8,128)S(1)} %bitcast.52), channel_id=1, source_target_pairs={{16,0},{0,16},{48,32},{32,48},{80,64},{64,80},{112,96},{96,112},{1... | collective-permute-start | bytes 1572872 | tf_op jit(solution)/shard_map/ppermute | solution.py:22
  92.7 1.7 add_add_fusion
  96.5 25.8 %all_gather.18 = f32[16,16,512]{2,1,0:T(8,128)S(1)} all-gather(f32[1,16,512]{2,1,0:T(8,128)S(1)} %constant_dynamic-slice_fusion.1), channel_id=1, replica_groups={{0,32,64,96,128,160,192,224,256,288,320,352,384,416,448,480},{16,48,80,..., dimensions={0}, use_global_device_ids=true | all-gather | bytes 557056 | tf_op jit(solution)/shard_map/all_gather | solution.py:158
  122.4 11.6 %all_to_all.21 = f32[16,16,512]{2,1,0:T(8,128)S(1)} all-to-all(f32[16,16,512]{2,1,0:T(8,128)S(1)} %broadcast_in_dim.13), channel_id=1, replica_groups=mesh['fsdp'=32,'tp'=16] {'tp'}, dimensions={0} | all-to-all | bytes 1048576 | tf_op jit(solution)/shard_map/all_to_all | solution.py:26
  134.0 9.4 %collective-permute-start.2 = (f32[16,16,512]{2,1,0:T(8,128)S(1)}, f32[16,16,512]{2,1,0:T(8,128)S(1)}, u32[]{:S(2)}, u32[]{:S(2)}) collective-permute-start(f32[16,16,512]{2,1,0:T(8,128)S(1)} %all_to_all.21), channel_id=1, source_target_pairs={{16,0},{0,16},{48,32},{32,48},{80,64},{64,80},{112,96},{96,112},{1... | collective-permute-start | bytes 1572872 | tf_op jit(solution)/shard_map/ppermute | solution.py:22
  143.5 1.3 collective-permute-done.2
  145.1 24.5 %inverse_factor.1 = f32[512,512]{1,0:T(8,128)S(1)} custom-call(f32[512,512]{1,0:T(8,128)S(1)} %bitcast.49), custom_call_target="tpu_custom_call" | custom-call | flops 600000000 | bytes 3145728 | tf_op jit(solution)/shard_map/inverse_factor/pallas_call | solution.py:107
  169.6 2.0 convolution_convert_fusion.2
  171.6 25.9 %all-gather.1 = bf16[896,512]{1,0:T(8,128)(2,1)S(1)} all-gather(bf16[56,512]{1,0:T(8,128)(2,1)S(1)} %convolution_convert_fusion.2), channel_id=3, replica_groups={{0,32,64,96,128,160,192,224,256,288,320,352,384,416,448,480},{16,48,80,..., dimensions={0}, use_global_device_ids=true | all-gather | bytes 974848 | tf_op jit(solution)/shard_map/all_gather | solution.py:164
  197.5 9.2 %collective-permute-start.4 = (bf16[16,56,512]{2,1,0:T(8,128)(2,1)S(1)}, bf16[16,56,512]{2,1,0:T(8,128)(2,1)}, u32[]{:S(2)}, u32[]{:S(2)}) collective-permute-start(bf16[16,56,512]{2,1,0:T(8,128)(2,1)S(1)} %bitcast.60), channel_id=1, source_target_pairs={{16,0},{0,16},{48,32},{32,48},{80,64},{64,80},{112,96},{96,112},{1... | collective-permute-start | bytes 2752520 | tf_op jit(solution)/shard_map/ppermute | solution.py:22
  206.7 1.8 convolution_convert_fusion.1
  208.9 1.3 select_bitcast_fusion.1
  211.5 3.5 %all-to-all-start.3 = ((f32[16,1,512]{2,1,0:T(1,128)}), f32[16,1,512]{2,1,0:T(1,128)S(1)}, u32[]{:S(2)}, u32[]{:S(2)}) async-start(f32[16,1,512]{2,1,0:T(1,128)} %broadcast_in_dim.14), calls=%async_computation.4 | async-start | bytes 65536 | tf_op jit(solution)/shard_map/all_to_all | solution.py:26
  215.1 1.6 fusion.2
  216.7 4.8 %all-to-all-done.3 = f32[16,1,512]{2,1,0:T(1,128)S(1)} async-done(((f32[16,1,512]{2,1,0:T(1,128)}), f32[16,1,512]{2,1,0:T(1,128)S(1)}, u32[]{:S(2)}, u32[]{:S(2)}) %all-to-all-start.3) | async-done | bytes 32800 | tf_op jit(solution)/shard_map/all_to_all | solution.py:26
  222.7 1.6 fusion.3
  224.3 1.2 convolution_convert_fusion
  (34 shorter events, 9.7 us)
Async XLA Ops:
  42.0 11.6 %collective-permute-start = (bf16[16,16,1792]{2,1,0:T(8,128)(2,1)S(1)}, bf16[16,16,1792]{2,1,0:T(8,128)(2,1)S(1)}, u32[]{:S(2)}, u32[]{:S(2)}) collective-permute-start(bf16[16,16,1792]{2,1,0:T(8,128)(2,1)S(1)} %bitcast.58), channel_id=1, source_target_pairs={{16,0},{0,16},{48,32},{32,48},{80,64},{64,80},{112,96},{96,112},{1... | collective-permute-start | bytes 2752520 | tf_op jit(solution)/shard_map/ppermute | solution.py:22
  72.7 13.5 %all-to-all-start.1 = ((f32[16,16,512]{2,1,0:T(8,128)}), f32[16,16,512]{2,1,0:T(8,128)S(1)}, u32[]{:S(2)}, u32[]{:S(2)}) async-start(f32[16,16,512]{2,1,0:T(8,128)} %broadcast_in_dim.12), calls=%async_computation.1 | async-start | bytes 1048576 | tf_op jit(solution)/shard_map/all_to_all | solution.py:26
  76.3 93.3 %reduce-scatter.2.cloned.1.call-start = ((), (), s32[]{:S(2)}) async-start(), calls=%async_computation.5 | async-start | bytes 1949696 | tf_op jit(solution)/shard_map/reduce_scatter | solution.py:152
  76.4 15.2 %collective-permute-start.3 = (bf16[256,896]{1,0:T(8,128)(2,1)S(1)}, bf16[256,896]{1,0:T(8,128)(2,1)S(1)}, u32[]{:S(2)}, u32[]{:S(2)}) collective-permute-start(bf16[256,896]{1,0:T(8,128)(2,1)S(1)} %constant_dynamic-slice_fusion), channel_id=1, source_target_pairs={{16,0},{0,16},{48,32},{32,48},{80,64},{64,80},{112,96},{96,112},{1... | collective-permute-start | bytes 1376264 | tf_op jit(solution)/shard_map/ppermute | solution.py:22
  86.3 6.0 %collective-permute-start.1 = (f32[256,512]{1,0:T(8,128)S(1)}, f32[256,512]{1,0:T(8,128)S(1)}, u32[]{:S(2)}, u32[]{:S(2)}) collective-permute-start(f32[256,512]{1,0:T(8,128)S(1)} %bitcast.52), channel_id=1, source_target_pairs={{16,0},{0,16},{48,32},{32,48},{80,64},{64,80},{112,96},{96,112},{1... | collective-permute-start | bytes 1572872 | tf_op jit(solution)/shard_map/ppermute | solution.py:22
  134.0 10.8 %collective-permute-start.2 = (f32[16,16,512]{2,1,0:T(8,128)S(1)}, f32[16,16,512]{2,1,0:T(8,128)S(1)}, u32[]{:S(2)}, u32[]{:S(2)}) collective-permute-start(f32[16,16,512]{2,1,0:T(8,128)S(1)} %all_to_all.21), channel_id=1, source_target_pairs={{16,0},{0,16},{48,32},{32,48},{80,64},{64,80},{112,96},{96,112},{1... | collective-permute-start | bytes 1572872 | tf_op jit(solution)/shard_map/ppermute | solution.py:22
  197.5 11.4 %collective-permute-start.4 = (bf16[16,56,512]{2,1,0:T(8,128)(2,1)S(1)}, bf16[16,56,512]{2,1,0:T(8,128)(2,1)}, u32[]{:S(2)}, u32[]{:S(2)}) collective-permute-start(bf16[16,56,512]{2,1,0:T(8,128)(2,1)S(1)} %bitcast.60), channel_id=1, source_target_pairs={{16,0},{0,16},{48,32},{32,48},{80,64},{64,80},{112,96},{96,112},{1... | collective-permute-start | bytes 2752520 | tf_op jit(solution)/shard_map/ppermute | solution.py:22
  210.7 4.3 %copy-start = (bf16[256,512]{1,0:T(8,128)(2,1)S(1)}, bf16[256,512]{1,0:T(8,128)(2,1)}, u32[]{:S(2)}) copy-start(bf16[256,512]{1,0:T(8,128)(2,1)} %convolution_convert_fusion.1) | copy-start | bytes 786436
  211.5 9.9 %all-to-all-start.3 = ((f32[16,1,512]{2,1,0:T(1,128)}), f32[16,1,512]{2,1,0:T(1,128)S(1)}, u32[]{:S(2)}, u32[]{:S(2)}) async-start(f32[16,1,512]{2,1,0:T(1,128)} %broadcast_in_dim.14), calls=%async_computation.4 | async-start | bytes 65536 | tf_op jit(solution)/shard_map/all_to_all | solution.py:26
  221.5 1.2 copy-start.1
Sparse Core Ops, SparseCore 0:
  94.5 55.0 reduce-scatter.1

commit v4 on v3

--- a/solution.py
+++ b/solution.py
@@ -16,6 +16,8 @@
 B = 128
 
 DEEP = [[z * 2 + c for z in range(Z)] for c in range(2)]
+FAR = [[(4 * q + k) * 2 + c for q in range(4)] for k in range(4) for c in range(2)]
+NEAR = [[(4 * q + k) * 2 + c for k in range(4)] for q in range(4) for c in range(2)]
 
 
 def from_core(value):
@@ -26,6 +28,10 @@
     return lax.all_to_all(
         jnp.broadcast_to(value, (size,) + value.shape), axis, 0, 0, axis_index_groups=groups
     )
+
+
+def gather(value, groups):
+    return lax.all_gather(value, "fsdp", axis_index_groups=groups)
 
 
 def by_core(core, mine, other, axis):
@@ -79,28 +85,35 @@
 
 def inverse_kernel(gram_ref, out_ref, work):
     work[...] = gram_ref[...]
-    r = lax.broadcasted_iota(jnp.int32, (512, 512), 0)
-    c = lax.broadcasted_iota(jnp.int32, (512, 512), 1)
-    out_ref[...] = (r == c).astype(F32)
+    out_ref[...] = jnp.zeros_like(out_ref)
+
+    def dot(x, y, axis):
+        return lax.dot_general(
+            x, y, (((axis,), (0,)), ((), ())), precision=HI, preferred_element_type=F32
+        )
 
     @pl.loop(0, 4)
     def _(b):
         at = pl.multiple_of(b * B, B)
-        rows = pl.ds(at, B)
-        inv = factor_block(work[rows, pl.ds(at, B)])
-        upper = jnp.dot(inv, work[rows, :], precision=HI, preferred_element_type=F32)
-        lower = jnp.dot(inv, out_ref[rows, :], precision=HI, preferred_element_type=F32)
-        out_ref[rows, :] = lower
-
-        @pl.when(b < 3)
-        def _():
-            lane = lax.broadcasted_iota(jnp.int32, (B, 512), 1)
-            coef = jnp.where(lane >= at + B, upper, 0.0)
-            tn = lambda x, y: lax.dot_general(
-                x, y, (((0,), (0,)), ((), ())), precision=HI, preferred_element_type=F32
-            )
-            work[...] = work[...] - tn(coef, upper)
-            out_ref[...] = out_ref[...] - tn(coef, lower)
+        inv = factor_block(work[pl.ds(at, B), pl.ds(at, B)])
+
+        for i in range(4):
+
+            @pl.when(b == i)
+            def _():
+                here, rest, before = (
+                    slice(i * B, i * B + B), slice(i * B + B, 512), slice(0, i * B)
+                )
+                out_ref[here, here] = inv
+                if i > 0:
+                    lower = dot(inv, out_ref[here, before], 1)
+                    out_ref[here, before] = lower
+                if i < 3:
+                    upper = dot(inv, work[here, rest], 1)
+                    work[rest, rest] = work[rest, rest] - dot(upper, upper, 0)
+                    out_ref[rest, here] = -dot(upper, inv, 0)
+                    if i > 0:
+                        out_ref[rest, before] = out_ref[rest, before] - dot(upper, lower, 0)
 
 
 def inverse_factor(gram):
@@ -136,8 +149,9 @@
     columns = lambda place: lax.dynamic_slice_in_dim(blend, place * half, half, axis=1)
     mine, other = columns(core), from_core(columns(1 - core))
 
-    rows = lax.all_gather(right_factor, "fsdp", axis_index_groups=DEEP)
-    factor = by_core(core, rows, from_core(rows), 1).reshape(512, -1)
+    rows = gather(gather(right_factor, FAR), NEAR)
+    factor = by_core(core, rows, from_core(rows), 2)
+    factor = jnp.swapaxes(factor, 0, 1).reshape(512, -1)
     partial = nt(blend, factor)
     pieces = lax.all_to_all(partial.reshape(16, 16, 512), "tp", 0, 0)
     start = spread(jnp.sum(pieces, axis=0), "tp", None, 16).reshape(256, 512)
@@ -155,14 +169,15 @@
 
     gram = jnp.dot(start.T, start, precision=HI) + jnp.dot(second.T, second, precision=HI)
     band = pick(gram.reshape(32, 16, 512), 2 * tp + core)
-    band = jnp.sum(lax.all_gather(band, "fsdp", axis_index_groups=DEEP), axis=0)
+    band = jnp.sum(gather(jnp.sum(gather(band, NEAR), axis=0), FAR), axis=0)
     bands = spread(band, "tp", None, 16)
     gram = by_core(core, bands, from_core(bands), 1).reshape(512, 512)
 
     inverse = inverse_factor(gram)
     chunk = nt(cross, inverse, HI).astype(BF16)
-    rows = lax.all_gather(chunk, "fsdp", axis_index_groups=DEEP)
-    project = by_core(core, rows, from_core(rows), 0).reshape(1792, 512)
+    rows = gather(gather(chunk, FAR), NEAR)
+    project = by_core(core, rows, from_core(rows), 0)
+    project = jnp.swapaxes(project, 1, 2).reshape(1792, 512)
     basis = nt(start, inverse, HI).astype(BF16)
 
     wide = project.astype(F32)

time: 233 us -> 243 us (1.043)
  blocking collectives: 115 us -> 132 us
  Pallas kernels: 24.5 us -> 19.4 us
  starting transfers between devices: 43.3 us -> 39.2 us
    all_gather x3 -> x6, blocking collectives: 86.6 us -> 103 us  [gather(): return lax.all_gather(value, 'fsdp', axis_index_groups=groups)]
    pallas_call x1, Pallas kernels: 24.5 us -> 19.4 us  [inverse_factor(): pl.pallas_call(inverse_kernel, out_shape=jax.ShapeDtypeStruct((512, 512),...]
    ppermute x5, starting transfers between devices: 36.2 us -> 32.1 us  [from_core(): return lax.ppermute(value, 'fsdp', [(i ^ 1, i) for i in range(2 * Z)])]
  transfers between devices with their start and end apart: 8 -> 8, of which waited for: 6 -> 6; matrix products, arithmetic and copies ran while one was open for 4% -> 4% of each run, Pallas kernels for 11% -> 8%
where the time goes in v4:
time: 243 us; the launch traced here: 242 us
  blocking collectives  132 us (54%)
  starting transfers between devices  39.2 us (16%)
  Pallas kernels  19.4 us (8%)
  between operations  14.3 us (6%)
  matrix products  13.9 us (6%)
  waiting for transfers between devices  12.4 us (5%)
  other arithmetic  6.91 us (3%)
  local copies, waits for them, and re-layouts  4.21 us (2%)
    all_gather x6, blocking collectives, gather(): return lax.all_gather(value, 'fsdp', axis_index_groups=groups)  103 us
    ppermute x5, starting transfers between devices, from_core(): return lax.ppermute(value, 'fsdp', [(i ^ 1, i) for i in range(2 * Z)])  32.1 us
    pallas_call x1, Pallas kernels, inverse_factor(): pl.pallas_call(inverse_kernel, out_shape=jax.ShapeDtypeStruct((512, 512),...  19.4 us
    all_to_all x1, blocking collectives, local(): pieces = lax.all_to_all(partial.reshape(16, 16, 512), 'tp', 0, 0)  17.3 us
    all_to_all x1, blocking collectives, spread(): lax.all_to_all(jnp.broadcast_to(value, (size,) + value.shape), axis, 0, 0...  11.6 us
    all_to_all x2, waiting for transfers between devices, spread(): lax.all_to_all(jnp.broadcast_to(value, (size,) + value.shape), axis, 0, 0...  9.19 us
    dot_general x6, matrix products, nt(): lax.dot_general(a, b, (((1,), (1,)), ((), ())), precision=precision, pref...  8.84 us
    all_to_all x2, starting transfers between devices, spread(): lax.all_to_all(jnp.broadcast_to(value, (size,) + value.shape), axis, 0, 0...  7.07 us
  transfers between devices with their start and end apart: 8, of which 6 were waited for; matrix products, arithmetic and copies ran while one was open for 4% of the time, Pallas kernels for 8%

profile of v4, /device:TPU:1, one launch (start us, length us, event | category | flops | bytes accessed | tf_op | source)
XLA Modules:
  0.0 242.0 jit_solution(2233575210511691045)
XLA Ops:
  7.2 25.5 %all-gather = bf16[64,1792]{1,0:T(8,128)(2,1)S(1)} all-gather(bf16[16,1792]{1,0:T(8,128)(2,1)} %param.7), channel_id=2, replica_groups={{0,128,256,384},{16,144,272,400},{32,160,288,416},{48,176,304,432},{64,..., dimensions={0}, use_global_device_ids=true | all-gather | bytes 286720 | tf_op jit(solution)/shard_map/all_gather | solution.py:34
  32.7 17.3 %all-gather.1 = bf16[16,16,1792]{2,1,0:T(8,128)(2,1)S(1)} all-gather(bf16[4,16,1792]{2,1,0:T(8,128)(2,1)S(1)} %bitcast.71), channel_id=3, replica_groups={{0,32,64,96},{16,48,80,112},{128,160,192,224},{144,176,208,240},{256,28..., dimensions={0}, use_global_device_ids=true | all-gather | bytes 1146880 | tf_op jit(solution)/shard_map/all_gather | solution.py:34
  50.0 6.8 %collective-permute-start = (bf16[4,4,16,1792]{3,2,1,0:T(8,128)(2,1)S(1)}, bf16[4,4,16,1792]{3,2,1,0:T(8,128)(2,1)}, u32[]{:S(2)}, u32[]{:S(2)}) collective-permute-start(bf16[4,4,16,1792]{3,2,1,0:T(8,128)(2,1)S(1)} %bitcast.65), channel_id=1, source_target_pairs={{16,0},{0,16},{48,32},{32,48},{80,64},{64,80},{112,96},{96,112},{1... | collective-permute-start | bytes 2752520 | tf_op jit(solution)/shard_map/ppermute | solution.py:24
  61.3 17.3 %all_to_all.20 = f32[16,16,512]{2,1,0:T(8,128)S(1)} all-to-all(f32[16,16,512]{2,1,0:T(8,128)S(1)} %fusion.17), channel_id=1, replica_groups=mesh['fsdp'=32,'tp'=16] {'tp'}, dimensions={0} | all-to-all | bytes 1048576 | tf_op jit(solution)/shard_map/all_to_all | solution.py:156
  79.5 3.6 %all-to-all-start.1 = ((f32[16,16,512]{2,1,0:T(8,128)}), f32[16,16,512]{2,1,0:T(8,128)S(1)}, u32[]{:S(2)}, u32[]{:S(2)}) async-start(f32[16,16,512]{2,1,0:T(8,128)} %broadcast_in_dim.12), calls=%async_computation.1 | async-start | bytes 1048576 | tf_op jit(solution)/shard_map/all_to_all | solution.py:28
  83.2 3.7 %collective-permute-start.3 = (bf16[256,896]{1,0:T(8,128)(2,1)S(1)}, bf16[256,896]{1,0:T(8,128)(2,1)S(1)}, u32[]{:S(2)}, u32[]{:S(2)}) collective-permute-start(bf16[256,896]{1,0:T(8,128)(2,1)S(1)} %constant_dynamic-slice_fusion), channel_id=1, source_target_pairs={{16,0},{0,16},{48,32},{32,48},{80,64},{64,80},{112,96},{96,112},{1... | collective-permute-start | bytes 1376264 | tf_op jit(solution)/shard_map/ppermute | solution.py:24
  86.9 6.2 %all-to-all-done.1 = f32[16,16,512]{2,1,0:T(8,128)S(1)} async-done(((f32[16,16,512]{2,1,0:T(8,128)}), f32[16,16,512]{2,1,0:T(8,128)S(1)}, u32[]{:S(2)}, u32[]{:S(2)}) %all-to-all-start.1) | async-done | bytes 524320 | tf_op jit(solution)/shard_map/all_to_all | solution.py:28
  93.0 4.4 %collective-permute-start.1 = (f32[256,512]{1,0:T(8,128)S(1)}, f32[256,512]{1,0:T(8,128)S(1)}, u32[]{:S(2)}, u32[]{:S(2)}) collective-permute-start(f32[256,512]{1,0:T(8,128)S(1)} %bitcast.59), channel_id=1, source_target_pairs={{16,0},{0,16},{48,32},{32,48},{80,64},{64,80},{112,96},{96,112},{1... | collective-permute-start | bytes 1572872 | tf_op jit(solution)/shard_map/ppermute | solution.py:24
  99.4 1.7 add_add_fusion
  103.3 10.9 %all_gather.38 = f32[4,16,512]{2,1,0:T(8,128)S(1)} all-gather(f32[1,16,512]{2,1,0:T(8,128)S(1)} %constant_dynamic-slice_fusion.1), channel_id=1, replica_groups={{0,32,64,96},{16,48,80,112},{128,160,192,224},{144,176,208,240},{256,28..., dimensions={0}, use_global_device_ids=true | all-gather | bytes 163840 | tf_op jit(solution)/shard_map/all_gather | solution.py:34
  114.2 15.7 %all-gather.2 = f32[64,512]{1,0:T(8,128)S(1)} all-gather(f32[16,512]{1,0:T(8,128)S(1)} %reduce_sum.46), channel_id=4, replica_groups={{0,128,256,384},{16,144,272,400},{32,160,288,416},{48,176,304,432},{64,..., dimensions={0}, use_global_device_ids=true | all-gather | bytes 163840 | tf_op jit(solution)/shard_map/all_gather | solution.py:34
  130.0 11.6 %all_to_all.21 = f32[16,16,512]{2,1,0:T(8,128)S(1)} all-to-all(f32[16,16,512]{2,1,0:T(8,128)S(1)} %broadcast_in_dim.13), channel_id=1, replica_groups=mesh['fsdp'=32,'tp'=16] {'tp'}, dimensions={0} | all-to-all | bytes 1048576 | tf_op jit(solution)/shard_map/all_to_all | solution.py:28
  141.6 9.2 %collective-permute-start.2 = (f32[16,16,512]{2,1,0:T(8,128)S(1)}, f32[16,16,512]{2,1,0:T(8,128)S(1)}, u32[]{:S(2)}, u32[]{:S(2)}) collective-permute-start(f32[16,16,512]{2,1,0:T(8,128)S(1)} %all_to_all.21), channel_id=1, source_target_pairs={{16,0},{0,16},{48,32},{32,48},{80,64},{64,80},{112,96},{96,112},{1... | collective-permute-start | bytes 1572872 | tf_op jit(solution)/shard_map/ppermute | solution.py:24
  152.4 19.4 %inverse_factor.1 = f32[512,512]{1,0:T(8,128)S(1)} custom-call(f32[512,512]{1,0:T(8,128)S(1)} %bitcast.56), custom_call_target="tpu_custom_call" | custom-call | flops 600000000 | bytes 3145728 | tf_op jit(solution)/shard_map/inverse_factor/pallas_call | solution.py:120
  171.9 2.0 convolution_convert_fusion.2
  173.9 17.1 %all-gather.3 = bf16[224,512]{1,0:T(8,128)(2,1)S(1)} all-gather(bf16[56,512]{1,0:T(8,128)(2,1)S(1)} %convolution_convert_fusion.2), channel_id=5, replica_groups={{0,128,256,384},{16,144,272,400},{32,160,288,416},{48,176,304,432},{64,..., dimensions={0}, use_global_device_ids=true | all-gather | bytes 286720 | tf_op jit(solution)/shard_map/all_gather | solution.py:34
  190.9 16.2 %all-gather.4 = bf16[16,56,512]{2,1,0:T(8,128)(2,1)S(1)} all-gather(bf16[4,56,512]{2,1,0:T(8,128)(2,1)S(1)} %bitcast.70), channel_id=6, replica_groups={{0,32,64,96},{16,48,80,112},{128,160,192,224},{144,176,208,240},{256,28..., dimensions={0}, use_global_device_ids=true | all-gather | bytes 1146880 | tf_op jit(solution)/shard_map/all_gather | solution.py:34
  207.1 8.0 %collective-permute-start.4 = (bf16[4,4,56,512]{3,2,1,0:T(8,128)(2,1)S(1)}, bf16[4,4,56,512]{3,2,1,0:T(8,128)(2,1)}, u32[]{:S(2)}, u32[]{:S(2)}) collective-permute-start(bf16[4,4,56,512]{3,2,1,0:T(8,128)(2,1)S(1)} %bitcast.67), channel_id=1, source_target_pairs={{16,0},{0,16},{48,32},{32,48},{80,64},{64,80},{112,96},{96,112},{1... | collective-permute-start | bytes 2752520 | tf_op jit(solution)/shard_map/ppermute | solution.py:24
  215.2 1.8 convolution_convert_fusion.1
  221.2 3.5 %all-to-all-start.3 = ((f32[16,1,512]{2,1,0:T(1,128)}), f32[16,1,512]{2,1,0:T(1,128)S(1)}, u32[]{:S(2)}, u32[]{:S(2)}) async-start(f32[16,1,512]{2,1,0:T(1,128)} %broadcast_in_dim.14), calls=%async_computation.4 | async-start | bytes 65536 | tf_op jit(solution)/shard_map/all_to_all | solution.py:28
  224.7 1.7 copy.22
  226.5 1.6 fusion.2
  228.1 3.0 %all-to-all-done.3 = f32[16,1,512]{2,1,0:T(1,128)S(1)} async-done(((f32[16,1,512]{2,1,0:T(1,128)}), f32[16,1,512]{2,1,0:T(1,128)S(1)}, u32[]{:S(2)}, u32[]{:S(2)}) %all-to-all-start.3) | async-done | bytes 32800 | tf_op jit(solution)/shard_map/all_to_all | solution.py:28
  232.3 1.6 fusion.3
  (42 shorter events, 17.9 us)
Async XLA Ops:
  7.2 49.6 %copy-start.1 = (bf16[256,1792]{1,0:T(8,128)(2,1)S(1)}, bf16[256,1792]{1,0:T(8,128)(2,1)}, u32[]{:S(2)}) copy-start(bf16[256,1792]{1,0:T(8,128)(2,1)} %param.5) | copy-start | bytes 2752516
  50.0 9.0 %collective-permute-start = (bf16[4,4,16,1792]{3,2,1,0:T(8,128)(2,1)S(1)}, bf16[4,4,16,1792]{3,2,1,0:T(8,128)(2,1)}, u32[]{:S(2)}, u32[]{:S(2)}) collective-permute-start(bf16[4,4,16,1792]{3,2,1,0:T(8,128)(2,1)S(1)} %bitcast.65), channel_id=1, source_target_pairs={{16,0},{0,16},{48,32},{32,48},{80,64},{64,80},{112,96},{96,112},{1... | collective-permute-start | bytes 2752520 | tf_op jit(solution)/shard_map/ppermute | solution.py:24
  79.5 13.5 %all-to-all-start.1 = ((f32[16,16,512]{2,1,0:T(8,128)}), f32[16,16,512]{2,1,0:T(8,128)S(1)}, u32[]{:S(2)}, u32[]{:S(2)}) async-start(f32[16,16,512]{2,1,0:T(8,128)} %broadcast_in_dim.12), calls=%async_computation.1 | async-start | bytes 1048576 | tf_op jit(solution)/shard_map/all_to_all | solution.py:28
  83.1 88.8 %reduce-scatter.2.cloned.1.call-start = ((), (), s32[]{:S(2)}) async-start(), calls=%async_computation.5 | async-start | bytes 1949696 | tf_op jit(solution)/shard_map/reduce_scatter | solution.py:166
  83.2 15.2 %collective-permute-start.3 = (bf16[256,896]{1,0:T(8,128)(2,1)S(1)}, bf16[256,896]{1,0:T(8,128)(2,1)S(1)}, u32[]{:S(2)}, u32[]{:S(2)}) collective-permute-start(bf16[256,896]{1,0:T(8,128)(2,1)S(1)} %constant_dynamic-slice_fusion), channel_id=1, source_target_pairs={{16,0},{0,16},{48,32},{32,48},{80,64},{64,80},{112,96},{96,112},{1... | collective-permute-start | bytes 1376264 | tf_op jit(solution)/shard_map/ppermute | solution.py:24
  93.0 6.0 %collective-permute-start.1 = (f32[256,512]{1,0:T(8,128)S(1)}, f32[256,512]{1,0:T(8,128)S(1)}, u32[]{:S(2)}, u32[]{:S(2)}) collective-permute-start(f32[256,512]{1,0:T(8,128)S(1)} %bitcast.59), channel_id=1, source_target_pairs={{16,0},{0,16},{48,32},{32,48},{80,64},{64,80},{112,96},{96,112},{1... | collective-permute-start | bytes 1572872 | tf_op jit(solution)/shard_map/ppermute | solution.py:24
  141.6 10.6 %collective-permute-start.2 = (f32[16,16,512]{2,1,0:T(8,128)S(1)}, f32[16,16,512]{2,1,0:T(8,128)S(1)}, u32[]{:S(2)}, u32[]{:S(2)}) collective-permute-start(f32[16,16,512]{2,1,0:T(8,128)S(1)} %all_to_all.21), channel_id=1, source_target_pairs={{16,0},{0,16},{48,32},{32,48},{80,64},{64,80},{112,96},{96,112},{1... | collective-permute-start | bytes 1572872 | tf_op jit(solution)/shard_map/ppermute | solution.py:24
  207.1 10.2 %collective-permute-start.4 = (bf16[4,4,56,512]{3,2,1,0:T(8,128)(2,1)S(1)}, bf16[4,4,56,512]{3,2,1,0:T(8,128)(2,1)}, u32[]{:S(2)}, u32[]{:S(2)}) collective-permute-start(bf16[4,4,56,512]{3,2,1,0:T(8,128)(2,1)S(1)} %bitcast.67), channel_id=1, source_target_pairs={{16,0},{0,16},{48,32},{32,48},{80,64},{64,80},{112,96},{96,112},{1... | collective-permute-start | bytes 2752520 | tf_op jit(solution)/shard_map/ppermute | solution.py:24
  221.2 9.9 %all-to-all-start.3 = ((f32[16,1,512]{2,1,0:T(1,128)}), f32[16,1,512]{2,1,0:T(1,128)S(1)}, u32[]{:S(2)}, u32[]{:S(2)}) async-start(f32[16,1,512]{2,1,0:T(1,128)} %broadcast_in_dim.14), calls=%async_computation.4 | async-start | bytes 65536 | tf_op jit(solution)/shard_map/all_to_all | solution.py:28
  224.7 1.7 copy-start
  231.2 1.2 copy-start.2
Sparse Core Ops, SparseCore 0:
  101.3 55.7 reduce-scatter.1

commit v5 on v4

--- a/solution.py
+++ b/solution.py
@@ -16,8 +16,6 @@
 B = 128
 
 DEEP = [[z * 2 + c for z in range(Z)] for c in range(2)]
-FAR = [[(4 * q + k) * 2 + c for q in range(4)] for k in range(4) for c in range(2)]
-NEAR = [[(4 * q + k) * 2 + c for k in range(4)] for q in range(4) for c in range(2)]
 
 
 def from_core(value):
@@ -28,10 +26,6 @@
     return lax.all_to_all(
         jnp.broadcast_to(value, (size,) + value.shape), axis, 0, 0, axis_index_groups=groups
     )
-
-
-def gather(value, groups):
-    return lax.all_gather(value, "fsdp", axis_index_groups=groups)
 
 
 def by_core(core, mine, other, axis):
@@ -55,16 +49,19 @@
         spread = lambda x, q: jnp.broadcast_to(x[:, 8 * p + q : 8 * p + q + 1], (8, B))
         full = lambda x, j: jnp.broadcast_to(x[j : j + 1], (8, B))
         cols = [spread(w, q) for q in range(8)]
+        tri = {(i, q): full(cols[q], i) for q in range(8) for i in range(q, 8)}
         roots, above = [], {}
         for j in range(8):
-            pivot = full(cols[j], j)
+            pivot = tri[j, j]
             root, inv = lax.rsqrt(pivot), pl.reciprocal(pivot, approx=True)
             roots.append(root)
             for q in range(j + 1, 8):
-                across = full(cols[q], j)
-                above[j, q] = across * root
-                cols[q] = cols[q] - (cols[j] * across) * inv
+                for i in range(q, 8):
+                    tri[i, q] = tri[i, q] - (tri[i, j] * tri[q, j]) * inv
             col = jnp.where(sub > j, cols[j] * root, 0.0)
+            for q in range(j + 1, 8):
+                above[j, q] = tri[q, j] * root
+                cols[q] = cols[q] - col * above[j, q]
             row = full(w, j) * root
             w = jnp.where(sub == j, row, w - col * row)
             row = full(v, j) * root
@@ -139,6 +136,40 @@
     return lax.dot_general(a, b, (((0,), (0,)), ((), ())), preferred_element_type=F32)
 
 
+def cross_kernel(place_ref, mine_ref, other_ref, start_ref, second_ref, cross_ref, band_ref):
+    at = place_ref[0]
+    rank = lax.broadcasted_iota(jnp.int32, (16, 512), 1)
+    row = lax.broadcasted_iota(jnp.int32, (16, 512), 0)
+    chosen = (rank == row + at).astype(F32)
+    total, band = None, None
+    for blend_ref, rows_ref in ((mine_ref, start_ref), (other_ref, second_ref)):
+        rows = rows_ref[...]
+        high = rows.astype(BF16)
+        low = (rows - high.astype(F32)).astype(BF16)
+        part = tn(blend_ref[...], high) + tn(blend_ref[...], low)
+        total = part if total is None else total + part
+        part = jnp.dot(nt(chosen, rows, HI), rows, precision=HI, preferred_element_type=F32)
+        band = part if band is None else band + part
+    cross_ref[...] = total
+    band_ref[...] = band
+
+
+def cross_and_band(place, mine, other, start, second):
+    vmem = pl.BlockSpec(memory_space=pltpu.VMEM)
+    return pl.pallas_call(
+        cross_kernel,
+        out_shape=(
+            jax.ShapeDtypeStruct((mine.shape[1], 512), F32),
+            jax.ShapeDtypeStruct((16, 512), F32),
+        ),
+        in_specs=[pl.BlockSpec(memory_space=pltpu.SMEM)] + [vmem] * 4,
+        out_specs=(vmem, vmem),
+        compiler_params=pltpu.CompilerParams(vmem_limit_bytes=32 * 1024 * 1024),
+        cost_estimate=pl.CostEstimate(flops=10**9, bytes_accessed=4 * 2**20, transcendentals=0),
+        name="cross_and_band",
+    )(place, mine, other, start, second)
+
+
 def local(momentum, gradient, weight, right_factor):
     fsdp, tp = lax.axis_index("fsdp"), lax.axis_index("tp")
     core = fsdp % 2
@@ -149,49 +180,43 @@
     columns = lambda place: lax.dynamic_slice_in_dim(blend, place * half, half, axis=1)
     mine, other = columns(core), from_core(columns(1 - core))
 
-    rows = gather(gather(right_factor, FAR), NEAR)
-    factor = by_core(core, rows, from_core(rows), 2)
-    factor = jnp.swapaxes(factor, 0, 1).reshape(512, -1)
+    rows = lax.all_gather(right_factor, "fsdp", axis_index_groups=DEEP)
+    factor = by_core(core, rows, from_core(rows), 1).reshape(512, -1)
     partial = nt(blend, factor)
     pieces = lax.all_to_all(partial.reshape(16, 16, 512), "tp", 0, 0)
     start = spread(jnp.sum(pieces, axis=0), "tp", None, 16).reshape(256, 512)
     second = from_core(start)
 
-    def parts(array):
-        high = array.astype(BF16)
-        return high, (array - high.astype(F32)).astype(BF16)
-
-    cross = sum(tn(mine, part) for part in parts(start))
-    cross = cross + sum(tn(other, part) for part in parts(second))
+    place = (16 * (2 * tp + core)).astype(jnp.int32).reshape(1)
+    cross, band = cross_and_band(place, mine, other, start, second)
     cross = lax.psum_scatter(
         cross.reshape(16, 56, 512), "fsdp", scatter_dimension=0, axis_index_groups=DEEP
     )
-
-    gram = jnp.dot(start.T, start, precision=HI) + jnp.dot(second.T, second, precision=HI)
-    band = pick(gram.reshape(32, 16, 512), 2 * tp + core)
-    band = jnp.sum(gather(jnp.sum(gather(band, NEAR), axis=0), FAR), axis=0)
+    band = jnp.sum(lax.all_gather(band, "fsdp", axis_index_groups=DEEP), axis=0)
     bands = spread(band, "tp", None, 16)
     gram = by_core(core, bands, from_core(bands), 1).reshape(512, 512)
 
     inverse = inverse_factor(gram)
     chunk = nt(cross, inverse, HI).astype(BF16)
-    rows = gather(gather(chunk, FAR), NEAR)
-    project = by_core(core, rows, from_core(rows), 0)
-    project = jnp.swapaxes(project, 1, 2).reshape(1792, 512)
+    rows = lax.all_gather(chunk, "fsdp", axis_index_groups=DEEP).reshape(-1, 512)
     basis = nt(start, inverse, HI).astype(BF16)
 
-    wide = project.astype(F32)
+    wide = rows.astype(F32)
     squares = jnp.sum(wide * wide, axis=0, keepdims=True)
     squares = jnp.sum(spread(squares, "tp", None, 16), axis=0)
+    squares = squares + from_core(squares)
     rms = jnp.sqrt(squares / DF + 1e-06)
-    factor_t = (wide / rms).astype(BF16)
-    chosen = (jnp.arange(512)[None, :] == 16 * fsdp + jnp.arange(16)[:, None]).astype(BF16)
-    new_factor = nt(chosen, factor_t).astype(BF16)
+
+    project = by_core(core, rows, from_core(rows), 0).reshape(-1, 512)
+    chosen = jnp.arange(512)[None, :] == 16 * fsdp + jnp.arange(16)[:, None]
+    new_factor = nt(chosen.astype(BF16), project)
+    new_factor = new_factor / jnp.sum(jnp.where(chosen, rms, 0.0), axis=1, keepdims=True)
+    factor_t = (project.astype(F32) / rms).astype(BF16)
     new_momentum = (blend.astype(F32) - 0.4 * nt(basis, project)).astype(BF16)
     new_weight = (
         weight.astype(F32) - 2.0 * math.sqrt(DM / DF) * nt(basis, factor_t)
     ).astype(BF16)
-    return (new_momentum, new_weight, new_factor)
+    return (new_momentum, new_weight, new_factor.astype(BF16))
 
 
 def solution(mesh):

time: 243 us -> 236 us (0.971)
  blocking collectives: 132 us -> 116 us
  waiting for transfers between devices: 12.4 us -> 19.9 us
  starting transfers between devices: 39.2 us -> 46.2 us
  matrix products: 13.9 us -> 8.19 us
  Pallas kernels: 19.4 us -> 23.6 us
  local copies, waits for them, and re-layouts: 4.21 us -> 1.67 us
    all_gather x6 -> x3, blocking collectives: 103 us -> 87.4 us  [the longest x1 34.9 us: local(): rows = lax.all_gather(right_factor, 'fsdp', axis_index_groups=DEEP)]
    all_to_all x2, waiting for transfers between devices: 9.19 us -> 16.3 us  [spread(): lax.all_to_all(jnp.broadcast_to(value, (size,) + value.shape), axis, 0, 0...]
    ppermute x5 -> x6, starting transfers between devices: 32.1 us -> 37.6 us  [from_core(): return lax.ppermute(value, 'fsdp', [(i ^ 1, i) for i in range(2 * Z)])]
    dot_general x6 -> x0, matrix products: 5.09 us -> none  [the longest x4 3.01 us: tn(): lax.dot_general(a, b, (((0,), (0,)), ((), ())), preferred_element_type=F32)]
    pallas_call x0 -> x1, Pallas kernels: none -> 3.22 us  [cross_and_band(): pl.pallas_call(cross_kernel, out_shape=(jax.ShapeDtypeStruct((mine.shape[...]
  transfers between devices with their start and end apart: 8 -> 9, of which waited for: 6 -> 5; matrix products, arithmetic and copies ran while one was open for 4% -> 2% of each run, Pallas kernels for 8% -> 9%
where the time goes in v5:
time: 236 us
  blocking collectives  116 us (49%)
  starting transfers between devices  46.2 us (20%)
  Pallas kernels  23.6 us (10%)
  waiting for transfers between devices  19.9 us (8%)
  between operations  14.3 us (6%)
  matrix products  8.19 us (3%)
  other arithmetic  5.7 us (2%)
    ppermute x6, starting transfers between devices, from_core(): return lax.ppermute(value, 'fsdp', [(i ^ 1, i) for i in range(2 * Z)])  37.6 us
    all_gather x1, blocking collectives, local(): rows = lax.all_gather(right_factor, 'fsdp', axis_index_groups=DEEP)  34.9 us
    all_gather x1, blocking collectives, local(): lax.all_gather(chunk, 'fsdp', axis_index_groups=DEEP).reshape(-1, 512)  28 us
    all_gather x1, blocking collectives, local(): band = jnp.sum(lax.all_gather(band, 'fsdp', axis_index_groups=DEEP), axis=0)  24.5 us
    pallas_call x1, Pallas kernels, inverse_factor(): pl.pallas_call(inverse_kernel, out_shape=jax.ShapeDtypeStruct((512, 512),...  20.4 us
    all_to_all x1, blocking collectives, local(): pieces = lax.all_to_all(partial.reshape(16, 16, 512), 'tp', 0, 0)  17.3 us
    all_to_all x2, waiting for transfers between devices, spread(): lax.all_to_all(jnp.broadcast_to(value, (size,) + value.shape), axis, 0, 0...  16.3 us
    all_to_all x1, blocking collectives, spread(): lax.all_to_all(jnp.broadcast_to(value, (size,) + value.shape), axis, 0, 0...  11.7 us
  transfers between devices with their start and end apart: 9, of which 5 were waited for; matrix products, arithmetic and copies ran while one was open for 2% of the time, Pallas kernels for 9%

profile of v5, /device:TPU:1, one launch (start us, length us, event | category | flops | bytes accessed | tf_op | source)
XLA Modules:
  0.0 235.8 jit_solution(5716236225772057172)
XLA Ops:
  7.2 34.9 %all-gather = bf16[256,1792]{1,0:T(8,128)(2,1)S(1)} all-gather(bf16[16,1792]{1,0:T(8,128)(2,1)} %param.7), channel_id=2, replica_groups={{0,32,64,96,128,160,192,224,256,288,320,352,384,416,448,480},{16,48,80,..., dimensions={0}, use_global_device_ids=true | all-gather | bytes 974848 | tf_op jit(solution)/shard_map/all_gather | solution.py:183
  42.0 9.5 %collective-permute-start = (bf16[16,16,1792]{2,1,0:T(8,128)(2,1)S(1)}, bf16[16,16,1792]{2,1,0:T(8,128)(2,1)S(1)}, u32[]{:S(2)}, u32[]{:S(2)}) collective-permute-start(bf16[16,16,1792]{2,1,0:T(8,128)(2,1)S(1)} %bitcast.50), channel_id=1, source_target_pairs={{16,0},{0,16},{48,32},{32,48},{80,64},{64,80},{112,96},{96,112},{1... | collective-permute-start | bytes 2752520 | tf_op jit(solution)/shard_map/ppermute | solution.py:22
  51.5 1.7 add_convert_fusion
  54.6 17.3 %all_to_all.20 = f32[16,16,512]{2,1,0:T(8,128)S(1)} all-to-all(f32[16,16,512]{2,1,0:T(8,128)S(1)} %fusion.7), channel_id=1, replica_groups=mesh['fsdp'=32,'tp'=16] {'tp'}, dimensions={0} | all-to-all | bytes 1048576 | tf_op jit(solution)/shard_map/all_to_all | solution.py:186
  72.7 3.6 %all-to-all-start.1 = ((f32[16,16,512]{2,1,0:T(8,128)}), f32[16,16,512]{2,1,0:T(8,128)S(1)}, u32[]{:S(2)}, u32[]{:S(2)}) async-start(f32[16,16,512]{2,1,0:T(8,128)} %broadcast_in_dim.25), calls=%async_computation.1 | async-start | bytes 1048576 | tf_op jit(solution)/shard_map/all_to_all | solution.py:26
  76.4 9.9 %all-to-all-done.1 = f32[16,16,512]{2,1,0:T(8,128)S(1)} async-done(((f32[16,16,512]{2,1,0:T(8,128)}), f32[16,16,512]{2,1,0:T(8,128)S(1)}, u32[]{:S(2)}, u32[]{:S(2)}) %all-to-all-start.1) | async-done | bytes 524320 | tf_op jit(solution)/shard_map/all_to_all | solution.py:26
  86.3 4.4 %collective-permute-start.2 = (f32[256,512]{1,0:T(8,128)S(1)}, f32[256,512]{1,0:T(8,128)S(1)}, u32[]{:S(2)}, u32[]{:S(2)}) collective-permute-start(f32[256,512]{1,0:T(8,128)S(1)} %bitcast.41), channel_id=1, source_target_pairs={{16,0},{0,16},{48,32},{32,48},{80,64},{64,80},{112,96},{96,112},{1... | collective-permute-start | bytes 1572872 | tf_op jit(solution)/shard_map/ppermute | solution.py:22
  90.9 1.9 collective-permute-start.1
  92.8 1.8 collective-permute-done.1.other_ref
  94.6 3.2 %cross_and_band.1 = (f32[896,512]{1,0:T(8,128)}, f32[16,512]{1,0:T(8,128)S(1)}) custom-call(s32[1]{0:T(128)} %bitcast.8.place_ref, bf16[256,896]{1,0:T(8,128)(2,1)S(1)} %get-tuple-element.14.mine_ref, bf16[256,896]{1,0:T(8,128)(2,1)S(1)} %collective-permute-done.1.other_ref, f32[256,512]{1,0:T(8,128)S(1)} %bitcast.42, ...), custom_call_target="tpu_custom_call" | custom-call | flops 1000000000 | bytes 4194304 | tf_op jit(solution)/shard_map/cross_and_band/pallas_call | solution.py:159
  97.8 24.5 %all-gather.1 = f32[256,512]{1,0:T(8,128)S(1)} all-gather(f32[16,512]{1,0:T(8,128)S(1)} %get-tuple-element.5), channel_id=3, replica_groups={{0,32,64,96,128,160,192,224,256,288,320,352,384,416,448,480},{16,48,80,..., dimensions={0}, use_global_device_ids=true | all-gather | bytes 557056 | tf_op jit(solution)/shard_map/all_gather | solution.py:195
  122.4 11.7 %all_to_all.21 = f32[16,16,512]{2,1,0:T(8,128)S(1)} all-to-all(f32[16,16,512]{2,1,0:T(8,128)S(1)} %broadcast_in_dim.26), channel_id=1, replica_groups=mesh['fsdp'=32,'tp'=16] {'tp'}, dimensions={0} | all-to-all | bytes 1048576 | tf_op jit(solution)/shard_map/all_to_all | solution.py:26
  134.2 9.3 %collective-permute-start.3 = (f32[16,16,512]{2,1,0:T(8,128)S(1)}, f32[16,16,512]{2,1,0:T(8,128)S(1)}, u32[]{:S(2)}, u32[]{:S(2)}) collective-permute-start(f32[16,16,512]{2,1,0:T(8,128)S(1)} %all_to_all.21), channel_id=1, source_target_pairs={{16,0},{0,16},{48,32},{32,48},{80,64},{64,80},{112,96},{96,112},{1... | collective-permute-start | bytes 1572872 | tf_op jit(solution)/shard_map/ppermute | solution.py:22
  145.0 20.4 %inverse_factor.1 = f32[512,512]{1,0:T(8,128)S(1)} custom-call(f32[512,512]{1,0:T(8,128)S(1)} %bitcast.44), custom_call_target="tpu_custom_call" | custom-call | flops 600000000 | bytes 3145728 | tf_op jit(solution)/shard_map/inverse_factor/pallas_call | solution.py:117
  165.4 2.0 convolution_convert_fusion.1
  167.4 28.0 %all-gather.2 = bf16[896,512]{1,0:T(8,128)(2,1)} all-gather(bf16[56,512]{1,0:T(8,128)(2,1)S(1)} %convolution_convert_fusion.1), channel_id=4, replica_groups={{0,32,64,96,128,160,192,224,256,288,320,352,384,416,448,480},{16,48,80,..., dimensions={0}, use_global_device_ids=true | all-gather | bytes 974848 | tf_op jit(solution)/shard_map/all_gather | solution.py:201
  195.4 9.1 %collective-permute-start.4 = (bf16[896,512]{1,0:T(8,128)(2,1)}, bf16[896,512]{1,0:T(8,128)(2,1)}, u32[]{:S(2)}, u32[]{:S(2)}) collective-permute-start(bf16[896,512]{1,0:T(8,128)(2,1)} %all-gather.2), channel_id=1, source_target_pairs={{16,0},{0,16},{48,32},{32,48},{80,64},{64,80},{112,96},{96,112},{1... | collective-permute-start | bytes 2752520 | tf_op jit(solution)/shard_map/ppermute | solution.py:22
  204.6 1.4 multiply_reduce_fusion
  206.6 5.0 %all-to-all-start.3 = ((f32[16,1,512]{2,1,0:T(1,128)}), f32[16,1,512]{2,1,0:T(1,128)S(1)}, u32[]{:S(2)}, u32[]{:S(2)}) async-start(f32[16,1,512]{2,1,0:T(1,128)} %broadcast_in_dim.27), calls=%async_computation.4 | async-start | bytes 65536 | tf_op jit(solution)/shard_map/all_to_all | solution.py:26
  211.6 6.4 %all-to-all-done.3 = f32[16,1,512]{2,1,0:T(1,128)S(1)} async-done(((f32[16,1,512]{2,1,0:T(1,128)}), f32[16,1,512]{2,1,0:T(1,128)S(1)}, u32[]{:S(2)}, u32[]{:S(2)}) %all-to-all-start.3) | async-done | bytes 32800 | tf_op jit(solution)/shard_map/all_to_all | solution.py:26
  218.1 3.3 %collective-permute-start.5 = (f32[1,512]{1,0:T(1,128)S(1)}, f32[1,512]{1,0:T(1,128)S(1)}, u32[]{:S(2)}, u32[]{:S(2)}) collective-permute-start(f32[1,512]{1,0:T(1,128)S(1)} %bitcast.53), channel_id=1, source_target_pairs={{16,0},{0,16},{48,32},{32,48},{80,64},{64,80},{112,96},{96,112},{1... | collective-permute-start | bytes 6152 | tf_op jit(solution)/shard_map/ppermute | solution.py:22
  222.7 1.6 select_bitcast_fusion.1
  224.5 1.6 fusion.2
  227.3 1.7 fusion.3
  (28 shorter events, 7.4 us)
Async XLA Ops:
  42.0 11.6 %collective-permute-start = (bf16[16,16,1792]{2,1,0:T(8,128)(2,1)S(1)}, bf16[16,16,1792]{2,1,0:T(8,128)(2,1)S(1)}, u32[]{:S(2)}, u32[]{:S(2)}) collective-permute-start(bf16[16,16,1792]{2,1,0:T(8,128)(2,1)S(1)} %bitcast.50), channel_id=1, source_target_pairs={{16,0},{0,16},{48,32},{32,48},{80,64},{64,80},{112,96},{96,112},{1... | collective-permute-start | bytes 2752520 | tf_op jit(solution)/shard_map/ppermute | solution.py:22
  72.7 13.5 %all-to-all-start.1 = ((f32[16,16,512]{2,1,0:T(8,128)}), f32[16,16,512]{2,1,0:T(8,128)S(1)}, u32[]{:S(2)}, u32[]{:S(2)}) async-start(f32[16,16,512]{2,1,0:T(8,128)} %broadcast_in_dim.25), calls=%async_computation.1 | async-start | bytes 1048576 | tf_op jit(solution)/shard_map/all_to_all | solution.py:26
  76.3 89.1 %reduce-scatter.2.cloned.1.call-start = ((), (), s32[]{:S(2)}) async-start(), calls=%async_computation.5 | async-start | bytes 1949696 | tf_op jit(solution)/shard_map/reduce_scatter | solution.py:192
  86.3 8.3 %collective-permute-start.2 = (f32[256,512]{1,0:T(8,128)S(1)}, f32[256,512]{1,0:T(8,128)S(1)}, u32[]{:S(2)}, u32[]{:S(2)}) collective-permute-start(f32[256,512]{1,0:T(8,128)S(1)} %bitcast.41), channel_id=1, source_target_pairs={{16,0},{0,16},{48,32},{32,48},{80,64},{64,80},{112,96},{96,112},{1... | collective-permute-start | bytes 1572872 | tf_op jit(solution)/shard_map/ppermute | solution.py:22
  90.9 3.7 %collective-permute-start.1 = (bf16[256,896]{1,0:T(8,128)(2,1)S(1)}, bf16[256,896]{1,0:T(8,128)(2,1)S(1)}, u32[]{:S(2)}, u32[]{:S(2)}) collective-permute-start(bf16[256,896]{1,0:T(8,128)(2,1)S(1)} %get-tuple-element.13), channel_id=1, source_target_pairs={{16,0},{0,16},{48,32},{32,48},{80,64},{64,80},{112,96},{96,112},{1... | collective-permute-start | bytes 1376264 | tf_op jit(solution)/shard_map/ppermute | solution.py:22
  134.2 10.6 %collective-permute-start.3 = (f32[16,16,512]{2,1,0:T(8,128)S(1)}, f32[16,16,512]{2,1,0:T(8,128)S(1)}, u32[]{:S(2)}, u32[]{:S(2)}) collective-permute-start(f32[16,16,512]{2,1,0:T(8,128)S(1)} %all_to_all.21), channel_id=1, source_target_pairs={{16,0},{0,16},{48,32},{32,48},{80,64},{64,80},{112,96},{96,112},{1... | collective-permute-start | bytes 1572872 | tf_op jit(solution)/shard_map/ppermute | solution.py:22
  195.4 27.3 %collective-permute-start.4 = (bf16[896,512]{1,0:T(8,128)(2,1)}, bf16[896,512]{1,0:T(8,128)(2,1)}, u32[]{:S(2)}, u32[]{:S(2)}) collective-permute-start(bf16[896,512]{1,0:T(8,128)(2,1)} %all-gather.2), channel_id=1, source_target_pairs={{16,0},{0,16},{48,32},{32,48},{80,64},{64,80},{112,96},{96,112},{1... | collective-permute-start | bytes 2752520 | tf_op jit(solution)/shard_map/ppermute | solution.py:22
  206.6 11.4 %all-to-all-start.3 = ((f32[16,1,512]{2,1,0:T(1,128)}), f32[16,1,512]{2,1,0:T(1,128)S(1)}, u32[]{:S(2)}, u32[]{:S(2)}) async-start(f32[16,1,512]{2,1,0:T(1,128)} %broadcast_in_dim.27), calls=%async_computation.4 | async-start | bytes 65536 | tf_op jit(solution)/shard_map/all_to_all | solution.py:26
  218.1 4.4 %collective-permute-start.5 = (f32[1,512]{1,0:T(1,128)S(1)}, f32[1,512]{1,0:T(1,128)S(1)}, u32[]{:S(2)}, u32[]{:S(2)}) collective-permute-start(f32[1,512]{1,0:T(1,128)S(1)} %bitcast.53), channel_id=1, source_target_pairs={{16,0},{0,16},{48,32},{32,48},{80,64},{64,80},{112,96},{96,112},{1... | collective-permute-start | bytes 6152 | tf_op jit(solution)/shard_map/ppermute | solution.py:22
  226.1 1.2 copy-start
Sparse Core Ops, SparseCore 0:
  97.9 56.0 reduce-scatter.1

commit v6 on v5

--- a/solution.py
+++ b/solution.py
@@ -49,23 +49,28 @@
         spread = lambda x, q: jnp.broadcast_to(x[:, 8 * p + q : 8 * p + q + 1], (8, B))
         full = lambda x, j: jnp.broadcast_to(x[j : j + 1], (8, B))
         cols = [spread(w, q) for q in range(8)]
-        tri = {(i, q): full(cols[q], i) for q in range(8) for i in range(q, 8)}
         roots, above = [], {}
-        for j in range(8):
-            pivot = tri[j, j]
-            root, inv = lax.rsqrt(pivot), pl.reciprocal(pivot, approx=True)
-            roots.append(root)
-            for q in range(j + 1, 8):
-                for i in range(q, 8):
-                    tri[i, q] = tri[i, q] - (tri[i, j] * tri[q, j]) * inv
-            col = jnp.where(sub > j, cols[j] * root, 0.0)
-            for q in range(j + 1, 8):
-                above[j, q] = tri[q, j] * root
-                cols[q] = cols[q] - col * above[j, q]
-            row = full(w, j) * root
-            w = jnp.where(sub == j, row, w - col * row)
-            row = full(v, j) * root
-            v = jnp.where(sub == j, row, v - col * row)
+        for j in range(0, 8, 2):
+            k = j + 1
+            first, cross, second = full(cols[j], j), full(cols[j], k), full(cols[k], k)
+            inv = pl.reciprocal(first, approx=True)
+            ratio = cross * inv
+            schur = second - cross * ratio
+            inv_schur = first * pl.reciprocal(first * second - cross * cross, approx=True)
+            roots += [lax.rsqrt(first), lax.rsqrt(schur)]
+            above[j, k] = cross * roots[j]
+            next_col = cols[k] - cols[j] * ratio
+            for q in range(k + 1, 8):
+                top, low = full(cols[q], j), full(cols[q], k)
+                low = low - ratio * top
+                above[j, q], above[k, q] = top * roots[j], low * roots[k]
+                cols[q] = (cols[q] - cols[j] * (top * inv)) - next_col * (low * inv_schur)
+            for at, col in ((j, cols[j]), (k, next_col)):
+                col = jnp.where(sub > at, col * roots[at], 0.0)
+                row = full(w, at) * roots[at]
+                w = jnp.where(sub == at, row, w - col * row)
+                row = full(v, at) * roots[at]
+                v = jnp.where(sub == at, row, v - col * row)
         done.append(v)
         for i in range(p + 1, B // 8):
             a, e = left[i], right[i]
@@ -81,7 +86,13 @@
 
 
 def inverse_kernel(gram_ref, out_ref, work):
-    work[...] = gram_ref[...]
+    gram = gram_ref[...]
+    diagonal = lax.broadcasted_iota(jnp.int32, (512, 512), 0) == lax.broadcasted_iota(
+        jnp.int32, (512, 512), 1
+    )
+    only = jnp.where(diagonal, gram, 0.0)
+    scale = lax.rsqrt(jnp.sum(only, axis=0, keepdims=True))
+    work[...] = (gram * lax.rsqrt(jnp.sum(only, axis=1, keepdims=True))) * scale
     out_ref[...] = jnp.zeros_like(out_ref)
 
     def dot(x, y, axis):
@@ -111,6 +122,8 @@
                     out_ref[rest, here] = -dot(upper, inv, 0)
                     if i > 0:
                         out_ref[rest, before] = out_ref[rest, before] - dot(upper, lower, 0)
+
+    out_ref[...] = out_ref[...] * scale
 
 
 def inverse_factor(gram):
@@ -185,6 +198,7 @@
     partial = nt(blend, factor)
     pieces = lax.all_to_all(partial.reshape(16, 16, 512), "tp", 0, 0)
     start = spread(jnp.sum(pieces, axis=0), "tp", None, 16).reshape(256, 512)
+    start, other = lax.optimization_barrier((start, other))
     second = from_core(start)
 
     place = (16 * (2 * tp + core)).astype(jnp.int32).reshape(1)
@@ -202,17 +216,22 @@
     basis = nt(start, inverse, HI).astype(BF16)
 
     wide = rows.astype(F32)
-    squares = jnp.sum(wide * wide, axis=0, keepdims=True)
-    squares = jnp.sum(spread(squares, "tp", None, 16), axis=0)
-    squares = squares + from_core(squares)
-    rms = jnp.sqrt(squares / DF + 1e-06)
-
+    squares = jnp.broadcast_to(jnp.sum(wide * wide, axis=0, keepdims=True), (16, 1, 512))
+    rows, squares = lax.optimization_barrier((rows, squares))
+    squares = lax.all_to_all(squares, "tp", 0, 0)
     project = by_core(core, rows, from_core(rows), 0).reshape(-1, 512)
     chosen = jnp.arange(512)[None, :] == 16 * fsdp + jnp.arange(16)[:, None]
     new_factor = nt(chosen.astype(BF16), project)
+    new_momentum = (blend.astype(F32) - 0.4 * nt(basis, project)).astype(BF16)
+    squares, new_momentum, new_factor = lax.optimization_barrier(
+        (squares, new_momentum, new_factor)
+    )
+    squares = jnp.sum(squares, axis=0)
+    squares = squares + from_core(squares)
+    rms = jnp.sqrt(squares / DF + 1e-06)
+
     new_factor = new_factor / jnp.sum(jnp.where(chosen, rms, 0.0), axis=1, keepdims=True)
     factor_t = (project.astype(F32) / rms).astype(BF16)
-    new_momentum = (blend.astype(F32) - 0.4 * nt(basis, project)).astype(BF16)
     new_weight = (
         weight.astype(F32) - 2.0 * math.sqrt(DM / DF) * nt(basis, factor_t)
     ).astype(BF16)

time: 236 us -> 234 us (level)
  blocking collectives: 116 us -> 99.5 us
  starting transfers between devices: 46.2 us -> 56.3 us
  waiting for transfers between devices: 19.9 us -> 23.3 us
    all_to_all x1 -> x0, blocking collectives: 17.3 us -> none  [local(): pieces = lax.all_to_all(partial.reshape(16, 16, 512), 'tp', 0, 0)]
    all_to_all x0 -> x2, starting transfers between devices: none -> 13.6 us  [the longest x1 6.84 us: local(): squares = lax.all_to_all(squares, 'tp', 0, 0)]
    all_to_all x0 -> x2, waiting for transfers between devices: none -> 13.1 us  [the longest x1 10.7 us: local(): pieces = lax.all_to_all(partial.reshape(16, 16, 512), 'tp', 0, 0)]
    all_to_all x2 -> x1, waiting for transfers between devices: 16.3 us -> 4.72 us  [spread(): lax.all_to_all(jnp.broadcast_to(value, (size,) + value.shape), axis, 0, 0...]
    all_to_all x2 -> x1, starting transfers between devices: 8.55 us -> 3.57 us  [spread(): lax.all_to_all(jnp.broadcast_to(value, (size,) + value.shape), axis, 0, 0...]
  transfers between devices with their start and end apart: 9 -> 10, of which waited for: 5 -> 8; matrix products, arithmetic and copies ran while one was open for 2% -> 3% of each run, Pallas kernels for 9% -> 8%
where the time goes in v6:
time: 234 us; the launch traced here: 233 us
  blocking collectives  99.5 us (43%)
  starting transfers between devices  56.3 us (24%)
  waiting for transfers between devices  23.3 us (10%)
  Pallas kernels  22.4 us (10%)
  between operations  14.3 us (6%)
  matrix products  9.64 us (4%)
  other arithmetic  6.39 us (3%)
    ppermute x6, starting transfers between devices, from_core(): return lax.ppermute(value, 'fsdp', [(i ^ 1, i) for i in range(2 * Z)])  39 us
    all_gather x1, blocking collectives, local(): rows = lax.all_gather(right_factor, 'fsdp', axis_index_groups=DEEP)  34.9 us
    all_gather x1, blocking collectives, local(): lax.all_gather(chunk, 'fsdp', axis_index_groups=DEEP).reshape(-1, 512)  28.3 us
    all_gather x1, blocking collectives, local(): band = jnp.sum(lax.all_gather(band, 'fsdp', axis_index_groups=DEEP), axis=0)  24.7 us
    pallas_call x1, Pallas kernels, inverse_factor(): pl.pallas_call(inverse_kernel, out_shape=jax.ShapeDtypeStruct((512, 512),...  19.2 us
    all_to_all x1, blocking collectives, spread(): lax.all_to_all(jnp.broadcast_to(value, (size,) + value.shape), axis, 0, 0...  11.6 us
    all_to_all x1, waiting for transfers between devices, local(): pieces = lax.all_to_all(partial.reshape(16, 16, 512), 'tp', 0, 0)  10.7 us
    dot_general x6, matrix products, nt(): lax.dot_general(a, b, (((1,), (1,)), ((), ())), precision=precision, pref...  9.64 us
  transfers between devices with their start and end apart: 10, of which 8 were waited for; matrix products, arithmetic and copies ran while one was open for 3% of the time, Pallas kernels for 8%

profile of v6, /device:TPU:1, one launch (start us, length us, event | category | flops | bytes accessed | tf_op | source)
XLA Modules:
  0.0 233.4 jit_solution(15121995113153615527)
XLA Ops:
  7.2 34.9 %all-gather = bf16[256,1792]{1,0:T(8,128)(2,1)S(1)} all-gather(bf16[16,1792]{1,0:T(8,128)(2,1)} %param.7), channel_id=2, replica_groups={{0,32,64,96,128,160,192,224,256,288,320,352,384,416,448,480},{16,48,80,..., dimensions={0}, use_global_device_ids=true | all-gather | bytes 974848 | tf_op jit(solution)/shard_map/all_gather | solution.py:196
  42.0 9.5 %collective-permute-start = (bf16[16,16,1792]{2,1,0:T(8,128)(2,1)S(1)}, bf16[16,16,1792]{2,1,0:T(8,128)(2,1)S(1)}, u32[]{:S(2)}, u32[]{:S(2)}) collective-permute-start(bf16[16,16,1792]{2,1,0:T(8,128)(2,1)S(1)} %bitcast.50), channel_id=1, source_target_pairs={{16,0},{0,16},{48,32},{32,48},{80,64},{64,80},{112,96},{96,112},{1... | collective-permute-start | bytes 2752520 | tf_op jit(solution)/shard_map/ppermute | solution.py:22
  51.5 1.7 add_convert_fusion
  55.4 6.8 %all-to-all-start = ((f32[16,16,512]{2,1,0:T(8,128)}), f32[16,16,512]{2,1,0:T(8,128)S(1)}, u32[]{:S(2)}, u32[]{:S(2)}) async-start(f32[16,16,512]{2,1,0:T(8,128)} %fusion.7), calls=%async_computation | async-start | bytes 1048576 | tf_op jit(solution)/shard_map/all_to_all | solution.py:199
  62.2 10.7 %all-to-all-done = f32[16,16,512]{2,1,0:T(8,128)S(1)} async-done(((f32[16,16,512]{2,1,0:T(8,128)}), f32[16,16,512]{2,1,0:T(8,128)S(1)}, u32[]{:S(2)}, u32[]{:S(2)}) %all-to-all-start) | async-done | bytes 524320 | tf_op jit(solution)/shard_map/all_to_all | solution.py:199
  73.7 3.6 %all-to-all-start.1 = ((f32[16,16,512]{2,1,0:T(8,128)}), f32[16,16,512]{2,1,0:T(8,128)S(1)}, u32[]{:S(2)}, u32[]{:S(2)}) async-start(f32[16,16,512]{2,1,0:T(8,128)} %broadcast_in_dim.25), calls=%async_computation.1 | async-start | bytes 1048576 | tf_op jit(solution)/shard_map/all_to_all | solution.py:26
  77.5 3.6 %collective-permute-start.1 = (bf16[256,896]{1,0:T(8,128)(2,1)S(1)}, bf16[256,896]{1,0:T(8,128)(2,1)S(1)}, u32[]{:S(2)}, u32[]{:S(2)}) collective-permute-start(bf16[256,896]{1,0:T(8,128)(2,1)S(1)} %get-tuple-element.27), channel_id=1, source_target_pairs={{16,0},{0,16},{48,32},{32,48},{80,64},{64,80},{112,96},{96,112},{1... | collective-permute-start | bytes 1376264 | tf_op jit(solution)/shard_map/ppermute | solution.py:22
  82.6 4.7 %all-to-all-done.1 = f32[16,16,512]{2,1,0:T(8,128)S(1)} async-done(((f32[16,16,512]{2,1,0:T(8,128)}), f32[16,16,512]{2,1,0:T(8,128)S(1)}, u32[]{:S(2)}, u32[]{:S(2)}) %all-to-all-start.1) | async-done | bytes 524320 | tf_op jit(solution)/shard_map/all_to_all | solution.py:26
  87.3 4.4 %collective-permute-start.2 = (f32[256,512]{1,0:T(8,128)S(1)}, f32[256,512]{1,0:T(8,128)S(1)}, u32[]{:S(2)}, u32[]{:S(2)}) collective-permute-start(f32[256,512]{1,0:T(8,128)S(1)} %bitcast.41), channel_id=1, source_target_pairs={{16,0},{0,16},{48,32},{32,48},{80,64},{64,80},{112,96},{96,112},{1... | collective-permute-start | bytes 1572872 | tf_op jit(solution)/shard_map/ppermute | solution.py:22
  91.7 1.5 collective-permute-done.2.second_ref
  93.2 3.2 %cross_and_band.1 = (f32[896,512]{1,0:T(8,128)}, f32[16,512]{1,0:T(8,128)S(1)}) custom-call(s32[1]{0:T(128)} %bitcast.place_ref, bf16[256,896]{1,0:T(8,128)(2,1)S(1)} %get-tuple-element.28.mine_ref, bf16[256,896]{1,0:T(8,128)(2,1)S(1)} %collective-permute-done.1.other_ref, f32[256,512]{1,0:T(8,128)S(1)} %bitcast.42, ...), custom_call_target="tpu_custom_call" | custom-call | flops 1000000000 | bytes 4194304 | tf_op jit(solution)/shard_map/cross_and_band/pallas_call | solution.py:172
  96.5 24.7 %all-gather.1 = f32[256,512]{1,0:T(8,128)S(1)} all-gather(f32[16,512]{1,0:T(8,128)S(1)} %get-tuple-element.15), channel_id=3, replica_groups={{0,32,64,96,128,160,192,224,256,288,320,352,384,416,448,480},{16,48,80,..., dimensions={0}, use_global_device_ids=true | all-gather | bytes 557056 | tf_op jit(solution)/shard_map/all_gather | solution.py:209
  121.3 11.6 %all_to_all.20 = f32[16,16,512]{2,1,0:T(8,128)S(1)} all-to-all(f32[16,16,512]{2,1,0:T(8,128)S(1)} %broadcast_in_dim.26), channel_id=1, replica_groups=mesh['fsdp'=32,'tp'=16] {'tp'}, dimensions={0} | all-to-all | bytes 1048576 | tf_op jit(solution)/shard_map/all_to_all | solution.py:26
  132.9 9.5 %collective-permute-start.3 = (f32[16,16,512]{2,1,0:T(8,128)S(1)}, f32[16,16,512]{2,1,0:T(8,128)S(1)}, u32[]{:S(2)}, u32[]{:S(2)}) collective-permute-start(f32[16,16,512]{2,1,0:T(8,128)S(1)} %all_to_all.20), channel_id=1, source_target_pairs={{16,0},{0,16},{48,32},{32,48},{80,64},{64,80},{112,96},{96,112},{1... | collective-permute-start | bytes 1572872 | tf_op jit(solution)/shard_map/ppermute | solution.py:22
  144.0 19.2 %inverse_factor.1 = f32[512,512]{1,0:T(8,128)S(1)} custom-call(f32[512,512]{1,0:T(8,128)S(1)} %bitcast.44), custom_call_target="tpu_custom_call" | custom-call | flops 600000000 | bytes 3145728 | tf_op jit(solution)/shard_map/inverse_factor/pallas_call | solution.py:130
  163.2 2.0 convolution_convert_fusion.1
  165.2 28.3 %all-gather.2 = bf16[896,512]{1,0:T(8,128)(2,1)} all-gather(bf16[56,512]{1,0:T(8,128)(2,1)S(1)} %convolution_convert_fusion.1), channel_id=4, replica_groups={{0,32,64,96,128,160,192,224,256,288,320,352,384,416,448,480},{16,48,80,..., dimensions={0}, use_global_device_ids=true | all-gather | bytes 974848 | tf_op jit(solution)/shard_map/all_gather | solution.py:215
  195.6 8.6 %collective-permute-start.4 = (bf16[896,512]{1,0:T(8,128)(2,1)}, bf16[896,512]{1,0:T(8,128)(2,1)}, u32[]{:S(2)}, u32[]{:S(2)}) collective-permute-start(bf16[896,512]{1,0:T(8,128)(2,1)} %all-gather.2), channel_id=1, source_target_pairs={{16,0},{0,16},{48,32},{32,48},{80,64},{64,80},{112,96},{96,112},{1... | collective-permute-start | bytes 2752520 | tf_op jit(solution)/shard_map/ppermute | solution.py:22
  205.3 6.8 %all-to-all-start.3 = ((f32[16,1,512]{2,1,0:T(1,128)}), f32[16,1,512]{2,1,0:T(1,128)S(1)}, u32[]{:S(2)}, u32[]{:S(2)}) async-start(f32[16,1,512]{2,1,0:T(1,128)} %broadcast_in_dim.27), calls=%async_computation.4 | async-start | bytes 65536 | tf_op jit(solution)/shard_map/all_to_all | solution.py:221
  212.1 1.6 select_bitcast_fusion.1
  213.9 1.7 fusion.2
  216.2 2.4 %all-to-all-done.3 = f32[16,1,512]{2,1,0:T(1,128)S(1)} async-done(((f32[16,1,512]{2,1,0:T(1,128)}), f32[16,1,512]{2,1,0:T(1,128)S(1)}, u32[]{:S(2)}, u32[]{:S(2)}) %all-to-all-start.3) | async-done | bytes 32800 | tf_op jit(solution)/shard_map/all_to_all | solution.py:221
  218.6 3.3 %collective-permute-start.5 = (f32[1,512]{1,0:T(1,128)S(1)}, f32[1,512]{1,0:T(1,128)S(1)}, u32[]{:S(2)}, u32[]{:S(2)}) collective-permute-start(f32[1,512]{1,0:T(1,128)S(1)} %bitcast.53), channel_id=1, source_target_pairs={{16,0},{0,16},{48,32},{32,48},{80,64},{64,80},{112,96},{96,112},{1... | collective-permute-start | bytes 6152 | tf_op jit(solution)/shard_map/ppermute | solution.py:22
  223.0 2.9 %fusion.3 = bf16[256,1792]{1,0:T(8,128)(2,1)} fusion(bf16[256,512]{1,0:T(8,128)(2,1)S(1)} %convolution_convert_fusion, bf16[1792,512]{1,0:T(8,128)(2,1)S(1)} %bitcast.47, f32[512]{0:T(512)S(1)} %bitcast.56, bf16[256,1792]{1,0:T(8,128)(2,1)} %param.6), kind=kOutput, calls=%fused_computation.6 | convolution fusion | flops 474349568 | bytes 3934208 | tf_op jit(solution)/shard_map/dot_general | solution.py:143
  (28 shorter events, 11.9 us)
Async XLA Ops:
  42.0 11.6 %collective-permute-start = (bf16[16,16,1792]{2,1,0:T(8,128)(2,1)S(1)}, bf16[16,16,1792]{2,1,0:T(8,128)(2,1)S(1)}, u32[]{:S(2)}, u32[]{:S(2)}) collective-permute-start(bf16[16,16,1792]{2,1,0:T(8,128)(2,1)S(1)} %bitcast.50), channel_id=1, source_target_pairs={{16,0},{0,16},{48,32},{32,48},{80,64},{64,80},{112,96},{96,112},{1... | collective-permute-start | bytes 2752520 | tf_op jit(solution)/shard_map/ppermute | solution.py:22
  55.4 17.5 %all-to-all-start = ((f32[16,16,512]{2,1,0:T(8,128)}), f32[16,16,512]{2,1,0:T(8,128)S(1)}, u32[]{:S(2)}, u32[]{:S(2)}) async-start(f32[16,16,512]{2,1,0:T(8,128)} %fusion.7), calls=%async_computation | async-start | bytes 1048576 | tf_op jit(solution)/shard_map/all_to_all | solution.py:199
  73.7 13.5 %all-to-all-start.1 = ((f32[16,16,512]{2,1,0:T(8,128)}), f32[16,16,512]{2,1,0:T(8,128)S(1)}, u32[]{:S(2)}, u32[]{:S(2)}) async-start(f32[16,16,512]{2,1,0:T(8,128)} %broadcast_in_dim.25), calls=%async_computation.1 | async-start | bytes 1048576 | tf_op jit(solution)/shard_map/all_to_all | solution.py:26
  77.3 85.9 %reduce-scatter.2.cloned.1.call-start = ((), (), s32[]{:S(2)}) async-start(), calls=%async_computation.5 | async-start | bytes 1949696 | tf_op jit(solution)/shard_map/reduce_scatter | solution.py:206
  77.5 5.1 %collective-permute-start.1 = (bf16[256,896]{1,0:T(8,128)(2,1)S(1)}, bf16[256,896]{1,0:T(8,128)(2,1)S(1)}, u32[]{:S(2)}, u32[]{:S(2)}) collective-permute-start(bf16[256,896]{1,0:T(8,128)(2,1)S(1)} %get-tuple-element.27), channel_id=1, source_target_pairs={{16,0},{0,16},{48,32},{32,48},{80,64},{64,80},{112,96},{96,112},{1... | collective-permute-start | bytes 1376264 | tf_op jit(solution)/shard_map/ppermute | solution.py:22
  87.3 6.0 %collective-permute-start.2 = (f32[256,512]{1,0:T(8,128)S(1)}, f32[256,512]{1,0:T(8,128)S(1)}, u32[]{:S(2)}, u32[]{:S(2)}) collective-permute-start(f32[256,512]{1,0:T(8,128)S(1)} %bitcast.41), channel_id=1, source_target_pairs={{16,0},{0,16},{48,32},{32,48},{80,64},{64,80},{112,96},{96,112},{1... | collective-permute-start | bytes 1572872 | tf_op jit(solution)/shard_map/ppermute | solution.py:22
  132.9 10.9 %collective-permute-start.3 = (f32[16,16,512]{2,1,0:T(8,128)S(1)}, f32[16,16,512]{2,1,0:T(8,128)S(1)}, u32[]{:S(2)}, u32[]{:S(2)}) collective-permute-start(f32[16,16,512]{2,1,0:T(8,128)S(1)} %all_to_all.20), channel_id=1, source_target_pairs={{16,0},{0,16},{48,32},{32,48},{80,64},{64,80},{112,96},{96,112},{1... | collective-permute-start | bytes 1572872 | tf_op jit(solution)/shard_map/ppermute | solution.py:22
  195.6 16.5 %collective-permute-start.4 = (bf16[896,512]{1,0:T(8,128)(2,1)}, bf16[896,512]{1,0:T(8,128)(2,1)}, u32[]{:S(2)}, u32[]{:S(2)}) collective-permute-start(bf16[896,512]{1,0:T(8,128)(2,1)} %all-gather.2), channel_id=1, source_target_pairs={{16,0},{0,16},{48,32},{32,48},{80,64},{64,80},{112,96},{96,112},{1... | collective-permute-start | bytes 2752520 | tf_op jit(solution)/shard_map/ppermute | solution.py:22
  205.3 13.3 %all-to-all-start.3 = ((f32[16,1,512]{2,1,0:T(1,128)}), f32[16,1,512]{2,1,0:T(1,128)S(1)}, u32[]{:S(2)}, u32[]{:S(2)}) async-start(f32[16,1,512]{2,1,0:T(1,128)} %broadcast_in_dim.27), calls=%async_computation.4 | async-start | bytes 65536 | tf_op jit(solution)/shard_map/all_to_all | solution.py:221
  218.6 4.1 %collective-permute-start.5 = (f32[1,512]{1,0:T(1,128)S(1)}, f32[1,512]{1,0:T(1,128)S(1)}, u32[]{:S(2)}, u32[]{:S(2)}) collective-permute-start(f32[1,512]{1,0:T(1,128)S(1)} %bitcast.53), channel_id=1, source_target_pairs={{16,0},{0,16},{48,32},{32,48},{80,64},{64,80},{112,96},{96,112},{1... | collective-permute-start | bytes 6152 | tf_op jit(solution)/shard_map/ppermute | solution.py:22
Sparse Core Ops, SparseCore 0:
  96.6 56.2 reduce-scatter.1

commit v7 on v6

--- a/solution.py
+++ b/solution.py
@@ -44,44 +44,70 @@
     left = [diag[8 * i : 8 * i + 8] for i in range(B // 8)]
     right = [(lanes == sub + 8 * i).astype(F32) for i in range(B // 8)]
     done = []
+    full = lambda x, j: jnp.broadcast_to(x[j : j + 1], (8, B))
+
+    def spread(x, at):
+        return jnp.broadcast_to(x[:, at : at + 1], (8, B))
+
+    cols = [spread(left[0], q) for q in range(8)]
     for p in range(B // 8):
-        w, v = left[p], right[p]
-        spread = lambda x, q: jnp.broadcast_to(x[:, 8 * p + q : 8 * p + q + 1], (8, B))
-        full = lambda x, j: jnp.broadcast_to(x[j : j + 1], (8, B))
-        cols = [spread(w, q) for q in range(8)]
-        roots, above = [], {}
+        inv, unit, pivots = [], {}, []
         for j in range(0, 8, 2):
             k = j + 1
             first, cross, second = full(cols[j], j), full(cols[j], k), full(cols[k], k)
-            inv = pl.reciprocal(first, approx=True)
-            ratio = cross * inv
-            schur = second - cross * ratio
-            inv_schur = first * pl.reciprocal(first * second - cross * cross, approx=True)
-            roots += [lax.rsqrt(first), lax.rsqrt(schur)]
-            above[j, k] = cross * roots[j]
-            next_col = cols[k] - cols[j] * ratio
+            inv_first = pl.reciprocal(first, approx=True)
+            unit[k, j] = cross * inv_first
+            inv += [
+                inv_first,
+                first * pl.reciprocal(first * second - cross * cross, approx=True),
+            ]
+            pivots += [first, second - cross * unit[k, j]]
+            cols[k] = cols[k] - cols[j] * unit[k, j]
             for q in range(k + 1, 8):
                 top, low = full(cols[q], j), full(cols[q], k)
-                low = low - ratio * top
-                above[j, q], above[k, q] = top * roots[j], low * roots[k]
-                cols[q] = (cols[q] - cols[j] * (top * inv)) - next_col * (low * inv_schur)
-            for at, col in ((j, cols[j]), (k, next_col)):
-                col = jnp.where(sub > at, col * roots[at], 0.0)
-                row = full(w, at) * roots[at]
-                w = jnp.where(sub == at, row, w - col * row)
-                row = full(v, at) * roots[at]
-                v = jnp.where(sub == at, row, v - col * row)
-        done.append(v)
+                unit[q, j] = top * inv[j]
+                unit[q, k] = (low - unit[k, j] * top) * inv[k]
+                cols[q] = (cols[q] - cols[j] * unit[q, j]) - cols[k] * unit[q, k]
+
+        def columns(block):
+            c = [spread(block, 8 * p + q) for q in range(8)]
+            for q in range(1, 8):
+                for j in range(q):
+                    c[q] = c[q] - c[j] * unit[q, j]
+            return c, [c[q] * inv[q] for q in range(8)]
+
+        if p + 1 < B // 8:
+            below, scaled = columns(left[p + 1])
+            for_next = [spread(left[p + 1], 8 * (p + 1) + q) for q in range(8)]
+            for q in range(8):
+                for j in range(8):
+                    for_next[q] = for_next[q] - scaled[j] * full(below[j], q)
+
+        lower = [jnp.where(sub > j, cols[j] * inv[j], 0.0) for j in range(7)]
+        w = v = None
+        for c in range(8):
+            t = (sub == c).astype(F32)
+            if c < 7:
+                t = t - lower[c]
+            for j in range(c + 1, 7):
+                t = t - lower[j] * full(t, j)
+            dw, dv = t * full(left[p], c), t * full(right[p], c)
+            w, v = (dw, dv) if c == 0 else (w + dw, v + dv)
+        pivot = pivots[0]
+        for j in range(1, 8):
+            pivot = jnp.where(sub == j, pivots[j], pivot)
+        done.append(v * lax.rsqrt(pivot))
+
         for i in range(p + 1, B // 8):
+            if i > p + 1:
+                _, scaled = columns(left[i])
             a, e = left[i], right[i]
-            cols = [spread(a, q) for q in range(8)]
             for j in range(8):
-                col = cols[j] * roots[j]
-                for q in range(j + 1, 8):
-                    cols[q] = cols[q] - col * above[j, q]
-                a = a - col * w[j : j + 1]
-                e = e - col * v[j : j + 1]
+                a = a - scaled[j] * w[j : j + 1]
+                e = e - scaled[j] * v[j : j + 1]
             left[i], right[i] = a, e
+        if p + 1 < B // 8:
+            cols = for_next
     return jnp.concatenate(done)
 
 
@@ -133,7 +159,7 @@
         in_specs=[pl.BlockSpec(memory_space=pltpu.VMEM)],
         out_specs=pl.BlockSpec(memory_space=pltpu.VMEM),
         scratch_shapes=[pltpu.VMEM((512, 512), F32)],
-        compiler_params=pltpu.CompilerParams(vmem_limit_bytes=24 * 1024 * 1024),
+        compiler_params=pltpu.CompilerParams(vmem_limit_bytes=12 * 2**20),
         cost_estimate=pl.CostEstimate(flops=6 * 10**8, bytes_accessed=3 * 2**20, transcendentals=512),
         name="inverse_factor",
     )(gram)
@@ -177,10 +203,53 @@
         ),
         in_specs=[pl.BlockSpec(memory_space=pltpu.SMEM)] + [vmem] * 4,
         out_specs=(vmem, vmem),
-        compiler_params=pltpu.CompilerParams(vmem_limit_bytes=32 * 1024 * 1024),
+        compiler_params=pltpu.CompilerParams(vmem_limit_bytes=16 * 2**20),
         cost_estimate=pl.CostEstimate(flops=10**9, bytes_accessed=4 * 2**20, transcendentals=0),
         name="cross_and_band",
     )(place, mine, other, start, second)
+
+
+def half_columns(place):
+    return pl.ds(pl.multiple_of(place * 896, 128), 896)
+
+
+def feedback_kernel(core_ref, rows_ref, other_ref, basis_ref, blend_ref, out_ref):
+    basis = basis_ref[...]
+    for place, project_ref in ((core_ref[0], rows_ref), (1 - core_ref[0], other_ref)):
+        at = half_columns(place)
+        product = nt(basis, project_ref[...])
+        out_ref[:, at] = (blend_ref[:, at].astype(F32) - 0.4 * product).astype(BF16)
+
+
+def update_kernel(
+    at_ref, squares_ref, rows_ref, other_ref, basis_ref, weight_ref, out_ref, factor_ref
+):
+    basis = basis_ref[...]
+    squares = jnp.sum(squares_ref[...], axis=0, keepdims=True)
+    rms = jnp.sqrt(squares / DF + 1e-06)
+    rank = lax.broadcasted_iota(jnp.int32, (16, 512), 1)
+    row = lax.broadcasted_iota(jnp.int32, (16, 512), 0)
+    chosen = (rank == row + at_ref[1]).astype(BF16)
+    for place, project_ref in ((at_ref[0], rows_ref), (1 - at_ref[0], other_ref)):
+        at = half_columns(place)
+        factor = (project_ref[...].astype(F32) / rms).astype(BF16)
+        product = nt(basis, factor)
+        step = 2.0 * math.sqrt(DM / DF) * product
+        out_ref[:, at] = (weight_ref[:, at].astype(F32) - step).astype(BF16)
+        factor_ref[:, at] = nt(chosen, factor).astype(BF16)
+
+
+def tail_call(kernel, name, flops, out_rows, *operands):
+    vmem = pl.BlockSpec(memory_space=pltpu.VMEM)
+    return pl.pallas_call(
+        kernel,
+        out_shape=tuple(jax.ShapeDtypeStruct((n, 1792), BF16) for n in out_rows),
+        in_specs=[pl.BlockSpec(memory_space=pltpu.SMEM)] + [vmem] * (len(operands) - 1),
+        out_specs=(vmem,) * len(out_rows),
+        compiler_params=pltpu.CompilerParams(vmem_limit_bytes=16 * 2**20),
+        cost_estimate=pl.CostEstimate(flops=flops, bytes_accessed=4 * 2**20, transcendentals=0),
+        name=name,
+    )(*operands)
 
 
 def local(momentum, gradient, weight, right_factor):
@@ -213,29 +282,23 @@
     inverse = inverse_factor(gram)
     chunk = nt(cross, inverse, HI).astype(BF16)
     rows = lax.all_gather(chunk, "fsdp", axis_index_groups=DEEP).reshape(-1, 512)
+    other = from_core(rows)
+
+    total = lambda half: jnp.sum(jnp.square(half.astype(F32)), axis=0)
+    squares = jnp.broadcast_to(total(rows) + total(other), (16, 1, 512))
+    squares, start = lax.optimization_barrier((squares, start))
     basis = nt(start, inverse, HI).astype(BF16)
-
-    wide = rows.astype(F32)
-    squares = jnp.broadcast_to(jnp.sum(wide * wide, axis=0, keepdims=True), (16, 1, 512))
-    rows, squares = lax.optimization_barrier((rows, squares))
     squares = lax.all_to_all(squares, "tp", 0, 0)
-    project = by_core(core, rows, from_core(rows), 0).reshape(-1, 512)
-    chosen = jnp.arange(512)[None, :] == 16 * fsdp + jnp.arange(16)[:, None]
-    new_factor = nt(chosen.astype(BF16), project)
-    new_momentum = (blend.astype(F32) - 0.4 * nt(basis, project)).astype(BF16)
-    squares, new_momentum, new_factor = lax.optimization_barrier(
-        (squares, new_momentum, new_factor)
-    )
-    squares = jnp.sum(squares, axis=0)
-    squares = squares + from_core(squares)
-    rms = jnp.sqrt(squares / DF + 1e-06)
-
-    new_factor = new_factor / jnp.sum(jnp.where(chosen, rms, 0.0), axis=1, keepdims=True)
-    factor_t = (project.astype(F32) / rms).astype(BF16)
-    new_weight = (
-        weight.astype(F32) - 2.0 * math.sqrt(DM / DF) * nt(basis, factor_t)
-    ).astype(BF16)
-    return (new_momentum, new_weight, new_factor.astype(BF16))
+    place = jnp.stack([core, 16 * fsdp]).astype(jnp.int32)
+    (new_momentum,) = tail_call(
+        feedback_kernel, "feedback", 5 * 10**8, (256,), place, rows, other, basis, blend
+    )
+    squares, new_momentum = lax.optimization_barrier((squares, new_momentum))
+    new_weight, new_factor = tail_call(
+        update_kernel, "update", 5 * 10**8, (256, 16),
+        place, squares.reshape(16, 512), rows, other, basis, weight,
+    )
+    return (new_momentum, new_weight, new_factor)
 
 
 def solution(mesh):

time: 234 us -> 227 us (0.970)
  matrix products: 9.64 us -> 4.63 us
  other arithmetic: 6.39 us -> 2.85 us
  Pallas kernels: 22.4 us -> 25.5 us
  blocking collectives: 99.5 us -> 96.7 us
  waiting for transfers between devices: 23.3 us -> 26 us
    dot_general x6 -> x3, matrix products: 9.64 us -> 4.63 us  [nt(): lax.dot_general(a, b, (((1,), (1,)), ((), ())), precision=precision, pref...]
    pallas_call x0 -> x2, Pallas kernels: none -> 4.83 us  [tail_call(): pl.pallas_call(kernel, out_shape=tuple((jax.ShapeDtypeStruct((n, 1792), B...]
    all_gather x1, blocking collectives: 28.3 us -> 25.5 us  [local(): lax.all_gather(chunk, 'fsdp', axis_index_groups=DEEP).reshape(-1, 512)]
    ppermute x6 -> x5, starting transfers between devices: 39 us -> 36.9 us  [from_core(): return lax.ppermute(value, 'fsdp', [(i ^ 1, i) for i in range(2 * Z)])]
    ppermute x6 -> x5, waiting for transfers between devices: 5.45 us -> 6.39 us  [from_core(): return lax.ppermute(value, 'fsdp', [(i ^ 1, i) for i in range(2 * Z)])]
  transfers between devices with their start and end apart: 10 -> 9, of which waited for: 8 -> 8; matrix products, arithmetic and copies ran while one was open for 3% -> 1% of each run, Pallas kernels for 8% -> 9%
where the time goes in v7:
time: 227 us
  blocking collectives  96.7 us (43%)
  starting transfers between devices  54 us (24%)
  waiting for transfers between devices  26 us (11%)
  Pallas kernels  25.5 us (11%)
  between operations  14.2 us (6%)
  matrix products  4.63 us (2%)
  local copies, waits for them, and re-layouts  2.86 us (1%)
  other arithmetic  2.85 us (1%)
    ppermute x5, starting transfers between devices, from_core(): return lax.ppermute(value, 'fsdp', [(i ^ 1, i) for i in range(2 * Z)])  36.9 us
    all_gather x1, blocking collectives, local(): rows = lax.all_gather(right_factor, 'fsdp', axis_index_groups=DEEP)  34.9 us
    all_gather x1, blocking collectives, local(): lax.all_gather(chunk, 'fsdp', axis_index_groups=DEEP).reshape(-1, 512)  25.5 us
    all_gather x1, blocking collectives, local(): band = jnp.sum(lax.all_gather(band, 'fsdp', axis_index_groups=DEEP), axis=0)  24.7 us
    pallas_call x1, Pallas kernels, inverse_factor(): pl.pallas_call(inverse_kernel, out_shape=jax.ShapeDtypeStruct((512, 512),...  17.5 us
    all_to_all x1, blocking collectives, spread(): lax.all_to_all(jnp.broadcast_to(value, (size,) + value.shape), axis, 0, 0...  11.6 us
    all_to_all x1, waiting for transfers between devices, local(): pieces = lax.all_to_all(partial.reshape(16, 16, 512), 'tp', 0, 0)  10.7 us
    all_to_all x1, starting transfers between devices, local(): pieces = lax.all_to_all(partial.reshape(16, 16, 512), 'tp', 0, 0)  6.76 us
  transfers between devices with their start and end apart: 9, of which 8 were waited for; matrix products, arithmetic and copies ran while one was open for 1% of the time, Pallas kernels for 9%

profile of v7, /device:TPU:1, one launch (start us, length us, event | category | flops | bytes accessed | tf_op | source)
XLA Modules:
  0.0 226.8 jit_solution(3717614244723977977)
XLA Ops:
  7.2 34.9 %all-gather = bf16[256,1792]{1,0:T(8,128)(2,1)S(1)} all-gather(bf16[16,1792]{1,0:T(8,128)(2,1)} %param.7), channel_id=2, replica_groups={{0,32,64,96,128,160,192,224,256,288,320,352,384,416,448,480},{16,48,80,..., dimensions={0}, use_global_device_ids=true | all-gather | bytes 974848 | tf_op jit(solution)/shard_map/all_gather | solution.py:265
  42.0 9.5 %collective-permute-start = (bf16[16,16,1792]{2,1,0:T(8,128)(2,1)S(1)}, bf16[16,16,1792]{2,1,0:T(8,128)(2,1)S(1)}, u32[]{:S(2)}, u32[]{:S(2)}) collective-permute-start(bf16[16,16,1792]{2,1,0:T(8,128)(2,1)S(1)} %bitcast.42), channel_id=1, source_target_pairs={{16,0},{0,16},{48,32},{32,48},{80,64},{64,80},{112,96},{96,112},{1... | collective-permute-start | bytes 2752520 | tf_op jit(solution)/shard_map/ppermute | solution.py:22
  51.5 1.7 add_convert_fusion.blend_ref
  53.9 1.5 fusion.1
  55.4 6.8 %all-to-all-start = ((f32[16,16,512]{2,1,0:T(8,128)}), f32[16,16,512]{2,1,0:T(8,128)S(1)}, u32[]{:S(2)}, u32[]{:S(2)}) async-start(f32[16,16,512]{2,1,0:T(8,128)} %fusion.1), calls=%async_computation | async-start | bytes 1048576 | tf_op jit(solution)/shard_map/all_to_all | solution.py:268
  62.2 10.7 %all-to-all-done = f32[16,16,512]{2,1,0:T(8,128)S(1)} async-done(((f32[16,16,512]{2,1,0:T(8,128)}), f32[16,16,512]{2,1,0:T(8,128)S(1)}, u32[]{:S(2)}, u32[]{:S(2)}) %all-to-all-start) | async-done | bytes 524320 | tf_op jit(solution)/shard_map/all_to_all | solution.py:268
  73.7 3.6 %all-to-all-start.1 = ((f32[16,16,512]{2,1,0:T(8,128)}), f32[16,16,512]{2,1,0:T(8,128)S(1)}, u32[]{:S(2)}, u32[]{:S(2)}) async-start(f32[16,16,512]{2,1,0:T(8,128)} %broadcast_in_dim.9), calls=%async_computation.1 | async-start | bytes 1048576 | tf_op jit(solution)/shard_map/all_to_all | solution.py:26
  77.5 3.6 %collective-permute-start.1 = (bf16[256,896]{1,0:T(8,128)(2,1)S(1)}, bf16[256,896]{1,0:T(8,128)(2,1)S(1)}, u32[]{:S(2)}, u32[]{:S(2)}) collective-permute-start(bf16[256,896]{1,0:T(8,128)(2,1)S(1)} %get-tuple-element.27), channel_id=1, source_target_pairs={{16,0},{0,16},{48,32},{32,48},{80,64},{64,80},{112,96},{96,112},{1... | collective-permute-start | bytes 1376264 | tf_op jit(solution)/shard_map/ppermute | solution.py:22
  82.6 4.7 %all-to-all-done.1 = f32[16,16,512]{2,1,0:T(8,128)S(1)} async-done(((f32[16,16,512]{2,1,0:T(8,128)}), f32[16,16,512]{2,1,0:T(8,128)S(1)}, u32[]{:S(2)}, u32[]{:S(2)}) %all-to-all-start.1) | async-done | bytes 524320 | tf_op jit(solution)/shard_map/all_to_all | solution.py:26
  87.3 4.4 %collective-permute-start.2 = (f32[256,512]{1,0:T(8,128)S(1)}, f32[256,512]{1,0:T(8,128)S(1)}, u32[]{:S(2)}, u32[]{:S(2)}) collective-permute-start(f32[256,512]{1,0:T(8,128)S(1)} %bitcast.36), channel_id=1, source_target_pairs={{16,0},{0,16},{48,32},{32,48},{80,64},{64,80},{112,96},{96,112},{1... | collective-permute-start | bytes 1572872 | tf_op jit(solution)/shard_map/ppermute | solution.py:22
  91.7 1.5 collective-permute-done.2.second_ref
  93.2 3.2 %cross_and_band.1 = (f32[896,512]{1,0:T(8,128)}, f32[16,512]{1,0:T(8,128)S(1)}) custom-call(s32[1]{0:T(128)} %bitcast.place_ref, bf16[256,896]{1,0:T(8,128)(2,1)S(1)} %get-tuple-element.28.mine_ref, bf16[256,896]{1,0:T(8,128)(2,1)S(1)} %collective-permute-done.1.other_ref, f32[256,512]{1,0:T(8,128)S(1)} %bitcast.37, ...), custom_call_target="tpu_custom_call" | custom-call | flops 1000000000 | bytes 4194304 | tf_op jit(solution)/shard_map/cross_and_band/pallas_call | solution.py:198
  96.5 24.7 %all-gather.1 = f32[256,512]{1,0:T(8,128)S(1)} all-gather(f32[16,512]{1,0:T(8,128)S(1)} %get-tuple-element.16), channel_id=3, replica_groups={{0,32,64,96,128,160,192,224,256,288,320,352,384,416,448,480},{16,48,80,..., dimensions={0}, use_global_device_ids=true | all-gather | bytes 557056 | tf_op jit(solution)/shard_map/all_gather | solution.py:278
  121.3 11.6 %all_to_all.20 = f32[16,16,512]{2,1,0:T(8,128)S(1)} all-to-all(f32[16,16,512]{2,1,0:T(8,128)S(1)} %broadcast_in_dim.10), channel_id=1, replica_groups=mesh['fsdp'=32,'tp'=16] {'tp'}, dimensions={0} | all-to-all | bytes 1048576 | tf_op jit(solution)/shard_map/all_to_all | solution.py:26
  132.9 9.5 %collective-permute-start.3 = (f32[16,16,512]{2,1,0:T(8,128)S(1)}, f32[16,16,512]{2,1,0:T(8,128)S(1)}, u32[]{:S(2)}, u32[]{:S(2)}) collective-permute-start(f32[16,16,512]{2,1,0:T(8,128)S(1)} %all_to_all.20), channel_id=1, source_target_pairs={{16,0},{0,16},{48,32},{32,48},{80,64},{64,80},{112,96},{96,112},{1... | collective-permute-start | bytes 1572872 | tf_op jit(solution)/shard_map/ppermute | solution.py:22
  144.0 17.5 %inverse_factor.1 = f32[512,512]{1,0:T(8,128)S(1)} custom-call(f32[512,512]{1,0:T(8,128)S(1)} %bitcast.39), custom_call_target="tpu_custom_call" | custom-call | flops 600000000 | bytes 3145728 | tf_op jit(solution)/shard_map/inverse_factor/pallas_call | solution.py:156
  161.5 2.1 convolution_convert_fusion.1
  163.7 25.5 %all-gather.2.rows_ref = bf16[896,512]{1,0:T(8,128)(2,1)S(1)} all-gather(bf16[56,512]{1,0:T(8,128)(2,1)S(1)} %convolution_convert_fusion.1), channel_id=4, replica_groups={{0,32,64,96,128,160,192,224,256,288,320,352,384,416,448,480},{16,48,80,..., dimensions={0}, use_global_device_ids=true | all-gather | bytes 974848 | tf_op jit(solution)/shard_map/all_gather | solution.py:284
  189.2 9.8 %collective-permute-start.4 = (bf16[896,512]{1,0:T(8,128)(2,1)S(1)}, bf16[896,512]{1,0:T(8,128)(2,1)S(1)}, u32[]{:S(2)}, u32[]{:S(2)}) collective-permute-start(bf16[896,512]{1,0:T(8,128)(2,1)S(1)} %all-gather.2.rows_ref), channel_id=1, source_target_pairs={{16,0},{0,16},{48,32},{32,48},{80,64},{64,80},{112,96},{96,112},{1... | collective-permute-start | bytes 2752520 | tf_op jit(solution)/shard_map/ppermute | solution.py:22
  199.3 1.7 collective-permute-done.4.other_ref
  203.0 6.7 %all-to-all-start.3 = ((f32[16,1,512]{2,1,0:T(1,128)}), f32[16,1,512]{2,1,0:T(1,128)S(1)}, u32[]{:S(2)}, u32[]{:S(2)}) async-start(f32[16,1,512]{2,1,0:T(1,128)} %broadcast_in_dim.11), calls=%async_computation.4 | async-start | bytes 65536 | tf_op jit(solution)/shard_map/all_to_all | solution.py:291
  209.7 2.3 %feedback.1 = bf16[256,1792]{1,0:T(8,128)(2,1)} custom-call(s32[2]{0:T(128)S(1)} %pad_add_fusion.core_ref.at_ref, bf16[896,512]{1,0:T(8,128)(2,1)S(1)} %all-gather.2.rows_ref, bf16[896,512]{1,0:T(8,128)(2,1)S(1)} %collective-permute-done.4.other_ref, bf16[256,512]{1,0:T(8,128)(2,1)S(1)} %convolution_convert_fusion.basis_ref, ...), custom_call_target="tpu_custom_call" | custom-call | flops 500000000 | bytes 4194304 | tf_op jit(solution)/shard_map/feedback/pallas_call | solution.py:244
  212.0 4.2 %all-to-all-done.3 = f32[16,1,512]{2,1,0:T(1,128)S(1)} async-done(((f32[16,1,512]{2,1,0:T(1,128)}), f32[16,1,512]{2,1,0:T(1,128)S(1)}, u32[]{:S(2)}, u32[]{:S(2)}) %all-to-all-start.3) | async-done | bytes 32800 | tf_op jit(solution)/shard_map/all_to_all | solution.py:291
  217.4 2.6 %update.1 = (bf16[256,1792]{1,0:T(8,128)(2,1)}, bf16[16,1792]{1,0:T(8,128)(2,1)}) custom-call(s32[2]{0:T(128)S(1)} %pad_add_fusion.core_ref.at_ref, f32[16,512]{1,0:T(8,128)S(1)} %bitcast.40, bf16[896,512]{1,0:T(8,128)(2,1)S(1)} %all-gather.2.rows_ref, bf16[896,512]{1,0:T(8,128)(2,1)S(1)} %collective-permute-done.4.other_ref, ...), custom_call_target="tpu_custom_call" | custom-call | flops 500000000 | bytes 4194304 | tf_op jit(solution)/shard_map/update/pallas_call | solution.py:244
  (28 shorter events, 8.3 us)
Async XLA Ops:
  42.0 11.6 %collective-permute-start = (bf16[16,16,1792]{2,1,0:T(8,128)(2,1)S(1)}, bf16[16,16,1792]{2,1,0:T(8,128)(2,1)S(1)}, u32[]{:S(2)}, u32[]{:S(2)}) collective-permute-start(bf16[16,16,1792]{2,1,0:T(8,128)(2,1)S(1)} %bitcast.42), channel_id=1, source_target_pairs={{16,0},{0,16},{48,32},{32,48},{80,64},{64,80},{112,96},{96,112},{1... | collective-permute-start | bytes 2752520 | tf_op jit(solution)/shard_map/ppermute | solution.py:22
  55.4 17.5 %all-to-all-start = ((f32[16,16,512]{2,1,0:T(8,128)}), f32[16,16,512]{2,1,0:T(8,128)S(1)}, u32[]{:S(2)}, u32[]{:S(2)}) async-start(f32[16,16,512]{2,1,0:T(8,128)} %fusion.1), calls=%async_computation | async-start | bytes 1048576 | tf_op jit(solution)/shard_map/all_to_all | solution.py:268
  73.7 13.5 %all-to-all-start.1 = ((f32[16,16,512]{2,1,0:T(8,128)}), f32[16,16,512]{2,1,0:T(8,128)S(1)}, u32[]{:S(2)}, u32[]{:S(2)}) async-start(f32[16,16,512]{2,1,0:T(8,128)} %broadcast_in_dim.9), calls=%async_computation.1 | async-start | bytes 1048576 | tf_op jit(solution)/shard_map/all_to_all | solution.py:26
  77.3 84.2 %reduce-scatter.2.cloned.1.call-start = ((), (), s32[]{:S(2)}) async-start(), calls=%async_computation.5 | async-start | bytes 1949696 | tf_op jit(solution)/shard_map/reduce_scatter | solution.py:275
  77.5 5.1 %collective-permute-start.1 = (bf16[256,896]{1,0:T(8,128)(2,1)S(1)}, bf16[256,896]{1,0:T(8,128)(2,1)S(1)}, u32[]{:S(2)}, u32[]{:S(2)}) collective-permute-start(bf16[256,896]{1,0:T(8,128)(2,1)S(1)} %get-tuple-element.27), channel_id=1, source_target_pairs={{16,0},{0,16},{48,32},{32,48},{80,64},{64,80},{112,96},{96,112},{1... | collective-permute-start | bytes 1376264 | tf_op jit(solution)/shard_map/ppermute | solution.py:22
  87.3 6.0 %collective-permute-start.2 = (f32[256,512]{1,0:T(8,128)S(1)}, f32[256,512]{1,0:T(8,128)S(1)}, u32[]{:S(2)}, u32[]{:S(2)}) collective-permute-start(f32[256,512]{1,0:T(8,128)S(1)} %bitcast.36), channel_id=1, source_target_pairs={{16,0},{0,16},{48,32},{32,48},{80,64},{64,80},{112,96},{96,112},{1... | collective-permute-start | bytes 1572872 | tf_op jit(solution)/shard_map/ppermute | solution.py:22
  132.9 10.9 %collective-permute-start.3 = (f32[16,16,512]{2,1,0:T(8,128)S(1)}, f32[16,16,512]{2,1,0:T(8,128)S(1)}, u32[]{:S(2)}, u32[]{:S(2)}) collective-permute-start(f32[16,16,512]{2,1,0:T(8,128)S(1)} %all_to_all.20), channel_id=1, source_target_pairs={{16,0},{0,16},{48,32},{32,48},{80,64},{64,80},{112,96},{96,112},{1... | collective-permute-start | bytes 1572872 | tf_op jit(solution)/shard_map/ppermute | solution.py:22
  161.5 2.2 copy-start
  189.2 11.9 %collective-permute-start.4 = (bf16[896,512]{1,0:T(8,128)(2,1)S(1)}, bf16[896,512]{1,0:T(8,128)(2,1)S(1)}, u32[]{:S(2)}, u32[]{:S(2)}) collective-permute-start(bf16[896,512]{1,0:T(8,128)(2,1)S(1)} %all-gather.2.rows_ref), channel_id=1, source_target_pairs={{16,0},{0,16},{48,32},{32,48},{80,64},{64,80},{112,96},{96,112},{1... | collective-permute-start | bytes 2752520 | tf_op jit(solution)/shard_map/ppermute | solution.py:22
  199.0 3.0 %copy-start.1 = (f32[512,512]{1,0:T(8,128)S(1)}, f32[512,512]{1,0:T(8,128)}, u32[]{:S(2)}) copy-start(f32[512,512]{1,0:T(8,128)} %copy-done) | copy-start | bytes 3145732
  203.0 13.2 %all-to-all-start.3 = ((f32[16,1,512]{2,1,0:T(1,128)}), f32[16,1,512]{2,1,0:T(1,128)S(1)}, u32[]{:S(2)}, u32[]{:S(2)}) async-start(f32[16,1,512]{2,1,0:T(1,128)} %broadcast_in_dim.11), calls=%async_computation.4 | async-start | bytes 65536 | tf_op jit(solution)/shard_map/all_to_all | solution.py:291
  216.2 1.2 copy-start.2
Sparse Core Ops, SparseCore 0:
  96.6 55.8 reduce-scatter.1

commit v8 on v7

--- a/solution.py
+++ b/solution.py
@@ -15,7 +15,7 @@
 BF16 = jnp.bfloat16
 B = 128
 
-DEEP = [[z * 2 + c for z in range(Z)] for c in range(2)]
+DEEP = [[z * 2 + ((z + g) % 2) for z in range(Z)] for g in range(2)]
 
 
 def from_core(value):
@@ -28,9 +28,9 @@
     )
 
 
-def by_core(core, mine, other, axis):
+def by_group(group, mine, other, axis):
     return jnp.stack(
-        [jnp.where(core == 0, mine, other), jnp.where(core == 0, other, mine)], axis=axis
+        [jnp.where(group == 0, mine, other), jnp.where(group == 0, other, mine)], axis=axis
     )
 
 
@@ -254,30 +254,33 @@
 
 def local(momentum, gradient, weight, right_factor):
     fsdp, tp = lax.axis_index("fsdp"), lax.axis_index("tp")
-    core = fsdp % 2
+    group = (fsdp + fsdp // 2) % 2
 
     blend = (momentum.astype(F32) + gradient.astype(F32)).astype(BF16)
 
     half = blend.shape[1] // 2
     columns = lambda place: lax.dynamic_slice_in_dim(blend, place * half, half, axis=1)
-    mine, other = columns(core), from_core(columns(1 - core))
+    mine, other = columns(group), from_core(columns(1 - group))
 
     rows = lax.all_gather(right_factor, "fsdp", axis_index_groups=DEEP)
-    factor = by_core(core, rows, from_core(rows), 1).reshape(512, -1)
+    others = from_core(rows)
+    first = (jnp.arange(Z) + group)[:, None, None] % 2 == 0
+    factor = jnp.stack([jnp.where(first, rows, others), jnp.where(first, others, rows)], axis=1)
+    factor = factor.reshape(512, -1)
     partial = nt(blend, factor)
     pieces = lax.all_to_all(partial.reshape(16, 16, 512), "tp", 0, 0)
     start = spread(jnp.sum(pieces, axis=0), "tp", None, 16).reshape(256, 512)
     start, other = lax.optimization_barrier((start, other))
     second = from_core(start)
 
-    place = (16 * (2 * tp + core)).astype(jnp.int32).reshape(1)
+    place = (16 * (2 * tp + group)).astype(jnp.int32).reshape(1)
     cross, band = cross_and_band(place, mine, other, start, second)
     cross = lax.psum_scatter(
         cross.reshape(16, 56, 512), "fsdp", scatter_dimension=0, axis_index_groups=DEEP
     )
     band = jnp.sum(lax.all_gather(band, "fsdp", axis_index_groups=DEEP), axis=0)
     bands = spread(band, "tp", None, 16)
-    gram = by_core(core, bands, from_core(bands), 1).reshape(512, 512)
+    gram = by_group(group, bands, from_core(bands), 1).reshape(512, 512)
 
     inverse = inverse_factor(gram)
     chunk = nt(cross, inverse, HI).astype(BF16)
@@ -289,7 +292,7 @@
     squares, start = lax.optimization_barrier((squares, start))
     basis = nt(start, inverse, HI).astype(BF16)
     squares = lax.all_to_all(squares, "tp", 0, 0)
-    place = jnp.stack([core, 16 * fsdp]).astype(jnp.int32)
+    place = jnp.stack([group, 16 * fsdp]).astype(jnp.int32)
     (new_momentum,) = tail_call(
         feedback_kernel, "feedback", 5 * 10**8, (256,), place, rows, other, basis, blend
     )

time: 227 us -> 220 us (0.969)
  starting transfers between devices: 54 us -> 29.4 us
  blocking collectives: 96.7 us -> 113 us
    ppermute x5, starting transfers between devices: 36.9 us -> 15.6 us  [from_core(): return lax.ppermute(value, 'fsdp', [(i ^ 1, i) for i in range(2 * Z)])]
    all_gather x1, blocking collectives: 24.7 us -> 30.5 us  [local(): band = jnp.sum(lax.all_gather(band, 'fsdp', axis_index_groups=DEEP), axis=0)]
    all_gather x1, blocking collectives: 34.9 us -> 40 us  [local(): rows = lax.all_gather(right_factor, 'fsdp', axis_index_groups=DEEP)]
    all_gather x1, blocking collectives: 25.5 us -> 28.8 us  [local(): lax.all_gather(chunk, 'fsdp', axis_index_groups=DEEP).reshape(-1, 512)]
    all_to_all x1, starting transfers between devices: 6.71 us -> 3.51 us  [local(): squares = lax.all_to_all(squares, 'tp', 0, 0)]
where the time goes in v8:
time: 220 us; the launch traced here: 219 us
  blocking collectives  113 us (51%)
  starting transfers between devices  29.4 us (13%)
  waiting for transfers between devices  26.6 us (12%)
  Pallas kernels  25.5 us (12%)
  between operations  14.3 us (6%)
  matrix products  4.63 us (2%)
  other arithmetic  2.9 us (1%)
  local copies, waits for them, and re-layouts  2.86 us (1%)
    all_gather x1, blocking collectives, local(): rows = lax.all_gather(right_factor, 'fsdp', axis_index_groups=DEEP)  40 us
    all_gather x1, blocking collectives, local(): band = jnp.sum(lax.all_gather(band, 'fsdp', axis_index_groups=DEEP), axis=0)  30.5 us
    all_gather x1, blocking collectives, local(): lax.all_gather(chunk, 'fsdp', axis_index_groups=DEEP).reshape(-1, 512)  28.8 us
    pallas_call x1, Pallas kernels, inverse_factor(): pl.pallas_call(inverse_kernel, out_shape=jax.ShapeDtypeStruct((512, 512),...  17.5 us
    ppermute x5, starting transfers between devices, from_core(): return lax.ppermute(value, 'fsdp', [(i ^ 1, i) for i in range(2 * Z)])  15.6 us
    all_to_all x1, blocking collectives, spread(): lax.all_to_all(jnp.broadcast_to(value, (size,) + value.shape), axis, 0, 0...  13.7 us
    all_to_all x1, waiting for transfers between devices, local(): pieces = lax.all_to_all(partial.reshape(16, 16, 512), 'tp', 0, 0)  10.9 us
    all_to_all x1, starting transfers between devices, local(): pieces = lax.all_to_all(partial.reshape(16, 16, 512), 'tp', 0, 0)  6.75 us
  transfers between devices with their start and end apart: 9, of which 8 were waited for; matrix products, arithmetic and copies ran while one was open for 1% of the time, Pallas kernels for 9%

profile of v8, /device:TPU:1, one launch (start us, length us, event | category | flops | bytes accessed | tf_op | source)
XLA Modules:
  0.0 219.1 jit_solution(14728130547652950346)
XLA Ops:
  7.2 40.0 %all-gather = bf16[256,1792]{1,0:T(8,128)(2,1)S(1)} all-gather(bf16[16,1792]{1,0:T(8,128)(2,1)} %param.7), channel_id=2, replica_groups={{0,48,64,112,128,176,192,240,256,304,320,368,384,432,448,496},{16,32,80..., dimensions={0}, use_global_device_ids=true | all-gather | bytes 974848 | tf_op jit(solution)/shard_map/all_gather | solution.py:265
  47.2 2.1 collective-permute-start
  49.3 1.7 add_convert_fusion.blend_ref
  51.9 1.5 fusion.3
  53.3 6.8 %all-to-all-start = ((f32[16,16,512]{2,1,0:T(8,128)}), f32[16,16,512]{2,1,0:T(8,128)S(1)}, u32[]{:S(2)}, u32[]{:S(2)}) async-start(f32[16,16,512]{2,1,0:T(8,128)} %fusion.3), calls=%async_computation | async-start | bytes 1048576 | tf_op jit(solution)/shard_map/all_to_all | solution.py:271
  60.1 10.9 %all-to-all-done = f32[16,16,512]{2,1,0:T(8,128)S(1)} async-done(((f32[16,16,512]{2,1,0:T(8,128)}), f32[16,16,512]{2,1,0:T(8,128)S(1)}, u32[]{:S(2)}, u32[]{:S(2)}) %all-to-all-start) | async-done | bytes 524320 | tf_op jit(solution)/shard_map/all_to_all | solution.py:271
  71.9 3.6 %all-to-all-start.1 = ((f32[16,16,512]{2,1,0:T(8,128)}), f32[16,16,512]{2,1,0:T(8,128)S(1)}, u32[]{:S(2)}, u32[]{:S(2)}) async-start(f32[16,16,512]{2,1,0:T(8,128)} %broadcast_in_dim.22), calls=%async_computation.1 | async-start | bytes 1048576 | tf_op jit(solution)/shard_map/all_to_all | solution.py:26
  75.7 3.5 %collective-permute-start.1 = (bf16[256,896]{1,0:T(8,128)(2,1)S(1)}, bf16[256,896]{1,0:T(8,128)(2,1)S(1)}, u32[]{:S(2)}, u32[]{:S(2)}) collective-permute-start(bf16[256,896]{1,0:T(8,128)(2,1)S(1)} %get-tuple-element.27), channel_id=1, source_target_pairs={{16,0},{0,16},{48,32},{32,48},{80,64},{64,80},{112,96},{96,112},{1... | collective-permute-start | bytes 1376264 | tf_op jit(solution)/shard_map/ppermute | solution.py:22
  80.5 5.0 %all-to-all-done.1 = f32[16,16,512]{2,1,0:T(8,128)S(1)} async-done(((f32[16,16,512]{2,1,0:T(8,128)}), f32[16,16,512]{2,1,0:T(8,128)S(1)}, u32[]{:S(2)}, u32[]{:S(2)}) %all-to-all-start.1) | async-done | bytes 524320 | tf_op jit(solution)/shard_map/all_to_all | solution.py:26
  85.6 4.3 %collective-permute-start.2 = (f32[256,512]{1,0:T(8,128)S(1)}, f32[256,512]{1,0:T(8,128)S(1)}, u32[]{:S(2)}, u32[]{:S(2)}) collective-permute-start(f32[256,512]{1,0:T(8,128)S(1)} %bitcast.36), channel_id=1, source_target_pairs={{16,0},{0,16},{48,32},{32,48},{80,64},{64,80},{112,96},{96,112},{1... | collective-permute-start | bytes 1572872 | tf_op jit(solution)/shard_map/ppermute | solution.py:22
  89.8 1.5 collective-permute-done.2.second_ref
  91.4 3.2 %cross_and_band.1 = (f32[896,512]{1,0:T(8,128)}, f32[16,512]{1,0:T(8,128)S(1)}) custom-call(s32[1]{0:T(128)} %bitcast.place_ref, bf16[256,896]{1,0:T(8,128)(2,1)S(1)} %get-tuple-element.28.mine_ref, bf16[256,896]{1,0:T(8,128)(2,1)S(1)} %collective-permute-done.1.other_ref, f32[256,512]{1,0:T(8,128)S(1)} %bitcast.37, ...), custom_call_target="tpu_custom_call" | custom-call | flops 1000000000 | bytes 4194304 | tf_op jit(solution)/shard_map/cross_and_band/pallas_call | solution.py:198
  94.6 30.5 %all-gather.1 = f32[256,512]{1,0:T(8,128)S(1)} all-gather(f32[16,512]{1,0:T(8,128)S(1)} %get-tuple-element.16), channel_id=3, replica_groups={{0,48,64,112,128,176,192,240,256,304,320,368,384,432,448,496},{16,32,80..., dimensions={0}, use_global_device_ids=true | all-gather | bytes 557056 | tf_op jit(solution)/shard_map/all_gather | solution.py:281
  125.2 13.7 %all_to_all.20 = f32[16,16,512]{2,1,0:T(8,128)S(1)} all-to-all(f32[16,16,512]{2,1,0:T(8,128)S(1)} %broadcast_in_dim.23), channel_id=1, replica_groups=mesh['fsdp'=32,'tp'=16] {'tp'}, dimensions={0} | all-to-all | bytes 1048576 | tf_op jit(solution)/shard_map/all_to_all | solution.py:26
  138.8 3.5 %collective-permute-start.3 = (f32[16,16,512]{2,1,0:T(8,128)S(1)}, f32[16,16,512]{2,1,0:T(8,128)S(1)}, u32[]{:S(2)}, u32[]{:S(2)}) collective-permute-start(f32[16,16,512]{2,1,0:T(8,128)S(1)} %all_to_all.20), channel_id=1, source_target_pairs={{16,0},{0,16},{48,32},{32,48},{80,64},{64,80},{112,96},{96,112},{1... | collective-permute-start | bytes 1572872 | tf_op jit(solution)/shard_map/ppermute | solution.py:22
  143.9 17.5 %inverse_factor.1 = f32[512,512]{1,0:T(8,128)S(1)} custom-call(f32[512,512]{1,0:T(8,128)S(1)} %bitcast.39), custom_call_target="tpu_custom_call" | custom-call | flops 600000000 | bytes 3145728 | tf_op jit(solution)/shard_map/inverse_factor/pallas_call | solution.py:156
  161.4 2.1 convolution_convert_fusion.1
  163.6 28.8 %all-gather.2.rows_ref = bf16[896,512]{1,0:T(8,128)(2,1)S(1)} all-gather(bf16[56,512]{1,0:T(8,128)(2,1)S(1)} %convolution_convert_fusion.1), channel_id=4, replica_groups={{0,48,64,112,128,176,192,240,256,304,320,368,384,432,448,496},{16,32,80..., dimensions={0}, use_global_device_ids=true | all-gather | bytes 974848 | tf_op jit(solution)/shard_map/all_gather | solution.py:287
  192.3 2.2 %collective-permute-start.4 = (bf16[896,512]{1,0:T(8,128)(2,1)S(1)}, bf16[896,512]{1,0:T(8,128)(2,1)S(1)}, u32[]{:S(2)}, u32[]{:S(2)}) collective-permute-start(bf16[896,512]{1,0:T(8,128)(2,1)S(1)} %all-gather.2.rows_ref), channel_id=1, source_target_pairs={{16,0},{0,16},{48,32},{32,48},{80,64},{64,80},{112,96},{96,112},{1... | collective-permute-start | bytes 2752520 | tf_op jit(solution)/shard_map/ppermute | solution.py:22
  194.9 1.8 collective-permute-done.4.other_ref
  198.7 3.5 %all-to-all-start.3 = ((f32[16,1,512]{2,1,0:T(1,128)}), f32[16,1,512]{2,1,0:T(1,128)S(1)}, u32[]{:S(2)}, u32[]{:S(2)}) async-start(f32[16,1,512]{2,1,0:T(1,128)} %broadcast_in_dim.24), calls=%async_computation.4 | async-start | bytes 65536 | tf_op jit(solution)/shard_map/all_to_all | solution.py:294
  202.2 2.3 %feedback.1 = bf16[256,1792]{1,0:T(8,128)(2,1)} custom-call(s32[2]{0:T(128)S(1)} %pad_add_fusion.core_ref.at_ref, bf16[896,512]{1,0:T(8,128)(2,1)S(1)} %all-gather.2.rows_ref, bf16[896,512]{1,0:T(8,128)(2,1)S(1)} %collective-permute-done.4.other_ref, bf16[256,512]{1,0:T(8,128)(2,1)S(1)} %convolution_convert_fusion.basis_ref, ...), custom_call_target="tpu_custom_call" | custom-call | flops 500000000 | bytes 4194304 | tf_op jit(solution)/shard_map/feedback/pallas_call | solution.py:244
  204.4 4.1 %all-to-all-done.3 = f32[16,1,512]{2,1,0:T(1,128)S(1)} async-done(((f32[16,1,512]{2,1,0:T(1,128)}), f32[16,1,512]{2,1,0:T(1,128)S(1)}, u32[]{:S(2)}, u32[]{:S(2)}) %all-to-all-start.3) | async-done | bytes 32800 | tf_op jit(solution)/shard_map/all_to_all | solution.py:294
  209.7 2.6 %update.1 = (bf16[256,1792]{1,0:T(8,128)(2,1)}, bf16[16,1792]{1,0:T(8,128)(2,1)}) custom-call(s32[2]{0:T(128)S(1)} %pad_add_fusion.core_ref.at_ref, f32[16,512]{1,0:T(8,128)S(1)} %bitcast.40, bf16[896,512]{1,0:T(8,128)(2,1)S(1)} %all-gather.2.rows_ref, bf16[896,512]{1,0:T(8,128)(2,1)S(1)} %collective-permute-done.4.other_ref, ...), custom_call_target="tpu_custom_call" | custom-call | flops 500000000 | bytes 4194304 | tf_op jit(solution)/shard_map/update/pallas_call | solution.py:244
  (29 shorter events, 8.5 us)
Async XLA Ops:
  47.2 4.4 %collective-permute-start = (bf16[16,16,1792]{2,1,0:T(8,128)(2,1)S(1)}, bf16[16,16,1792]{2,1,0:T(8,128)(2,1)S(1)}, u32[]{:S(2)}, u32[]{:S(2)}) collective-permute-start(bf16[16,16,1792]{2,1,0:T(8,128)(2,1)S(1)} %bitcast.42), channel_id=1, source_target_pairs={{16,0},{0,16},{48,32},{32,48},{80,64},{64,80},{112,96},{96,112},{1... | collective-permute-start | bytes 2752520 | tf_op jit(solution)/shard_map/ppermute | solution.py:22
  53.3 17.7 %all-to-all-start = ((f32[16,16,512]{2,1,0:T(8,128)}), f32[16,16,512]{2,1,0:T(8,128)S(1)}, u32[]{:S(2)}, u32[]{:S(2)}) async-start(f32[16,16,512]{2,1,0:T(8,128)} %fusion.3), calls=%async_computation | async-start | bytes 1048576 | tf_op jit(solution)/shard_map/all_to_all | solution.py:271
  71.9 13.7 %all-to-all-start.1 = ((f32[16,16,512]{2,1,0:T(8,128)}), f32[16,16,512]{2,1,0:T(8,128)S(1)}, u32[]{:S(2)}, u32[]{:S(2)}) async-start(f32[16,16,512]{2,1,0:T(8,128)} %broadcast_in_dim.22), calls=%async_computation.1 | async-start | bytes 1048576 | tf_op jit(solution)/shard_map/all_to_all | solution.py:26
  75.5 85.9 %reduce-scatter.2.cloned.1.call-start = ((), (), s32[]{:S(2)}) async-start(), calls=%async_computation.5 | async-start | bytes 1949696 | tf_op jit(solution)/shard_map/reduce_scatter | solution.py:278
  75.7 4.9 %collective-permute-start.1 = (bf16[256,896]{1,0:T(8,128)(2,1)S(1)}, bf16[256,896]{1,0:T(8,128)(2,1)S(1)}, u32[]{:S(2)}, u32[]{:S(2)}) collective-permute-start(bf16[256,896]{1,0:T(8,128)(2,1)S(1)} %get-tuple-element.27), channel_id=1, source_target_pairs={{16,0},{0,16},{48,32},{32,48},{80,64},{64,80},{112,96},{96,112},{1... | collective-permute-start | bytes 1376264 | tf_op jit(solution)/shard_map/ppermute | solution.py:22
  85.6 5.8 %collective-permute-start.2 = (f32[256,512]{1,0:T(8,128)S(1)}, f32[256,512]{1,0:T(8,128)S(1)}, u32[]{:S(2)}, u32[]{:S(2)}) collective-permute-start(f32[256,512]{1,0:T(8,128)S(1)} %bitcast.36), channel_id=1, source_target_pairs={{16,0},{0,16},{48,32},{32,48},{80,64},{64,80},{112,96},{96,112},{1... | collective-permute-start | bytes 1572872 | tf_op jit(solution)/shard_map/ppermute | solution.py:22
  138.8 4.9 %collective-permute-start.3 = (f32[16,16,512]{2,1,0:T(8,128)S(1)}, f32[16,16,512]{2,1,0:T(8,128)S(1)}, u32[]{:S(2)}, u32[]{:S(2)}) collective-permute-start(f32[16,16,512]{2,1,0:T(8,128)S(1)} %all_to_all.20), channel_id=1, source_target_pairs={{16,0},{0,16},{48,32},{32,48},{80,64},{64,80},{112,96},{96,112},{1... | collective-permute-start | bytes 1572872 | tf_op jit(solution)/shard_map/ppermute | solution.py:22
  161.4 2.2 copy-start
  192.3 4.4 %collective-permute-start.4 = (bf16[896,512]{1,0:T(8,128)(2,1)S(1)}, bf16[896,512]{1,0:T(8,128)(2,1)S(1)}, u32[]{:S(2)}, u32[]{:S(2)}) collective-permute-start(bf16[896,512]{1,0:T(8,128)(2,1)S(1)} %all-gather.2.rows_ref), channel_id=1, source_target_pairs={{16,0},{0,16},{48,32},{32,48},{80,64},{64,80},{112,96},{96,112},{1... | collective-permute-start | bytes 2752520 | tf_op jit(solution)/shard_map/ppermute | solution.py:22
  194.6 3.0 %copy-start.1 = (f32[512,512]{1,0:T(8,128)S(1)}, f32[512,512]{1,0:T(8,128)}, u32[]{:S(2)}) copy-start(f32[512,512]{1,0:T(8,128)} %copy-done) | copy-start | bytes 3145732
  198.7 9.9 %all-to-all-start.3 = ((f32[16,1,512]{2,1,0:T(1,128)}), f32[16,1,512]{2,1,0:T(1,128)S(1)}, u32[]{:S(2)}, u32[]{:S(2)}) async-start(f32[16,1,512]{2,1,0:T(1,128)} %broadcast_in_dim.24), calls=%async_computation.4 | async-start | bytes 65536 | tf_op jit(solution)/shard_map/all_to_all | solution.py:294
  208.6 1.2 copy-start.2
Sparse Core Ops, SparseCore 0:
  94.7 61.2 reduce-scatter.1

commit v9 on v8

--- a/solution.py
+++ b/solution.py
@@ -213,8 +213,11 @@
     return pl.ds(pl.multiple_of(place * 896, 128), 896)
 
 
-def feedback_kernel(core_ref, rows_ref, other_ref, basis_ref, blend_ref, out_ref):
-    basis = basis_ref[...]
+def feedback_kernel(
+    core_ref, rows_ref, other_ref, start_ref, inverse_ref, blend_ref, out_ref, basis_ref
+):
+    basis = nt(start_ref[...], inverse_ref[...], HI).astype(BF16)
+    basis_ref[...] = basis
     for place, project_ref in ((core_ref[0], rows_ref), (1 - core_ref[0], other_ref)):
         at = half_columns(place)
         product = nt(basis, project_ref[...])
@@ -239,13 +242,13 @@
         factor_ref[:, at] = nt(chosen, factor).astype(BF16)
 
 
-def tail_call(kernel, name, flops, out_rows, *operands):
+def tail_call(kernel, name, flops, outs, *operands):
     vmem = pl.BlockSpec(memory_space=pltpu.VMEM)
     return pl.pallas_call(
         kernel,
-        out_shape=tuple(jax.ShapeDtypeStruct((n, 1792), BF16) for n in out_rows),
+        out_shape=tuple(jax.ShapeDtypeStruct(shape, BF16) for shape in outs),
         in_specs=[pl.BlockSpec(memory_space=pltpu.SMEM)] + [vmem] * (len(operands) - 1),
-        out_specs=(vmem,) * len(out_rows),
+        out_specs=(vmem,) * len(outs),
         compiler_params=pltpu.CompilerParams(vmem_limit_bytes=16 * 2**20),
         cost_estimate=pl.CostEstimate(flops=flops, bytes_accessed=4 * 2**20, transcendentals=0),
         name=name,
@@ -289,16 +292,15 @@
 
     total = lambda half: jnp.sum(jnp.square(half.astype(F32)), axis=0)
     squares = jnp.broadcast_to(total(rows) + total(other), (16, 1, 512))
-    squares, start = lax.optimization_barrier((squares, start))
-    basis = nt(start, inverse, HI).astype(BF16)
     squares = lax.all_to_all(squares, "tp", 0, 0)
     place = jnp.stack([group, 16 * fsdp]).astype(jnp.int32)
-    (new_momentum,) = tail_call(
-        feedback_kernel, "feedback", 5 * 10**8, (256,), place, rows, other, basis, blend
-    )
-    squares, new_momentum = lax.optimization_barrier((squares, new_momentum))
+    new_momentum, basis = tail_call(
+        feedback_kernel, "feedback", 13 * 10**8, ((256, 1792), (256, 512)),
+        place, rows, other, start, inverse, blend,
+    )
+    squares, new_momentum, basis = lax.optimization_barrier((squares, new_momentum, basis))
     new_weight, new_factor = tail_call(
-        update_kernel, "update", 5 * 10**8, (256, 16),
+        update_kernel, "update", 5 * 10**8, ((256, 1792), (16, 1792)),
         place, squares.reshape(16, 512), rows, other, basis, weight,
     )
     return (new_momentum, new_weight, new_factor)

time: 220 us -> 222 us (level)
  local copies, waits for them, and re-layouts: 2.86 us -> 5.79 us
    unnamed x7, local copies, waits for them, and re-layouts: 1.19 us -> 4.12 us
    dot_general x3 -> x2, matrix products: 4.63 us -> 3.46 us  [nt(): lax.dot_general(a, b, (((1,), (1,)), ((), ())), precision=precision, pref...]
  transfers between devices with their start and end apart: 9 -> 9, of which waited for: 8 -> 8; matrix products, arithmetic and copies ran while one was open for 1% -> 2% of each run, Pallas kernels for 9% -> 9%
where the time goes in v9:
time: 222 us
  blocking collectives  113 us (51%)
  starting transfers between devices  30.1 us (14%)
  Pallas kernels  26.4 us (12%)
  waiting for transfers between devices  24.7 us (11%)
  between operations  14.3 us (6%)
  local copies, waits for them, and re-layouts  5.79 us (3%)
  other arithmetic  3.95 us (2%)
  matrix products  3.46 us (2%)
    all_gather x1, blocking collectives, local(): rows = lax.all_gather(right_factor, 'fsdp', axis_index_groups=DEEP)  40 us
    all_gather x1, blocking collectives, local(): band = jnp.sum(lax.all_gather(band, 'fsdp', axis_index_groups=DEEP), axis=0)  30.5 us
    all_gather x1, blocking collectives, local(): lax.all_gather(chunk, 'fsdp', axis_index_groups=DEEP).reshape(-1, 512)  28.8 us
    pallas_call x1, Pallas kernels, inverse_factor(): pl.pallas_call(inverse_kernel, out_shape=jax.ShapeDtypeStruct((512, 512),...  17.5 us
    ppermute x5, starting transfers between devices, from_core(): return lax.ppermute(value, 'fsdp', [(i ^ 1, i) for i in range(2 * Z)])  15.6 us
    all_to_all x1, blocking collectives, spread(): lax.all_to_all(jnp.broadcast_to(value, (size,) + value.shape), axis, 0, 0...  13.7 us
    all_to_all x1, waiting for transfers between devices, local(): pieces = lax.all_to_all(partial.reshape(16, 16, 512), 'tp', 0, 0)  10.9 us
    all_to_all x1, starting transfers between devices, local(): pieces = lax.all_to_all(partial.reshape(16, 16, 512), 'tp', 0, 0)  6.75 us
  transfers between devices with their start and end apart: 9, of which 8 were waited for; matrix products, arithmetic and copies ran while one was open for 2% of the time, Pallas kernels for 9%

profile of v9, /device:TPU:1, one launch (start us, length us, event | category | flops | bytes accessed | tf_op | source)
XLA Modules:
  0.0 221.5 jit_solution(2758749364566659037)
XLA Ops:
  7.2 40.0 %all-gather = bf16[256,1792]{1,0:T(8,128)(2,1)S(1)} all-gather(bf16[16,1792]{1,0:T(8,128)(2,1)} %param.7), channel_id=2, replica_groups={{0,48,64,112,128,176,192,240,256,304,320,368,384,432,448,496},{16,32,80..., dimensions={0}, use_global_device_ids=true | all-gather | bytes 974848 | tf_op jit(solution)/shard_map/all_gather | solution.py:268
  47.2 2.1 collective-permute-start
  49.3 1.7 add_convert_fusion.blend_ref
  51.9 1.5 fusion.3
  53.3 6.8 %all-to-all-start = ((f32[16,16,512]{2,1,0:T(8,128)}), f32[16,16,512]{2,1,0:T(8,128)S(1)}, u32[]{:S(2)}, u32[]{:S(2)}) async-start(f32[16,16,512]{2,1,0:T(8,128)} %fusion.3), calls=%async_computation | async-start | bytes 1048576 | tf_op jit(solution)/shard_map/all_to_all | solution.py:274
  60.1 10.9 %all-to-all-done = f32[16,16,512]{2,1,0:T(8,128)S(1)} async-done(((f32[16,16,512]{2,1,0:T(8,128)}), f32[16,16,512]{2,1,0:T(8,128)S(1)}, u32[]{:S(2)}, u32[]{:S(2)}) %all-to-all-start) | async-done | bytes 524320 | tf_op jit(solution)/shard_map/all_to_all | solution.py:274
  71.9 3.6 %all-to-all-start.1 = ((f32[16,16,512]{2,1,0:T(8,128)}), f32[16,16,512]{2,1,0:T(8,128)S(1)}, u32[]{:S(2)}, u32[]{:S(2)}) async-start(f32[16,16,512]{2,1,0:T(8,128)} %broadcast_in_dim.22), calls=%async_computation.1 | async-start | bytes 1048576 | tf_op jit(solution)/shard_map/all_to_all | solution.py:26
  75.7 3.5 %collective-permute-start.1 = (bf16[256,896]{1,0:T(8,128)(2,1)S(1)}, bf16[256,896]{1,0:T(8,128)(2,1)S(1)}, u32[]{:S(2)}, u32[]{:S(2)}) collective-permute-start(bf16[256,896]{1,0:T(8,128)(2,1)S(1)} %get-tuple-element.29), channel_id=1, source_target_pairs={{16,0},{0,16},{48,32},{32,48},{80,64},{64,80},{112,96},{96,112},{1... | collective-permute-start | bytes 1376264 | tf_op jit(solution)/shard_map/ppermute | solution.py:22
  80.5 5.0 %all-to-all-done.1 = f32[16,16,512]{2,1,0:T(8,128)S(1)} async-done(((f32[16,16,512]{2,1,0:T(8,128)}), f32[16,16,512]{2,1,0:T(8,128)S(1)}, u32[]{:S(2)}, u32[]{:S(2)}) %all-to-all-start.1) | async-done | bytes 524320 | tf_op jit(solution)/shard_map/all_to_all | solution.py:26
  85.6 4.3 %collective-permute-start.2 = (f32[256,512]{1,0:T(8,128)S(1)}, f32[256,512]{1,0:T(8,128)S(1)}, u32[]{:S(2)}, u32[]{:S(2)}) collective-permute-start(f32[256,512]{1,0:T(8,128)S(1)} %bitcast.35), channel_id=1, source_target_pairs={{16,0},{0,16},{48,32},{32,48},{80,64},{64,80},{112,96},{96,112},{1... | collective-permute-start | bytes 1572872 | tf_op jit(solution)/shard_map/ppermute | solution.py:22
  89.8 1.5 collective-permute-done.2.second_ref
  91.4 3.2 %cross_and_band.1 = (f32[896,512]{1,0:T(8,128)}, f32[16,512]{1,0:T(8,128)S(1)}) custom-call(s32[1]{0:T(128)} %bitcast.place_ref, bf16[256,896]{1,0:T(8,128)(2,1)S(1)} %get-tuple-element.30.mine_ref, bf16[256,896]{1,0:T(8,128)(2,1)S(1)} %collective-permute-done.1.other_ref, f32[256,512]{1,0:T(8,128)S(1)} %bitcast.36, ...), custom_call_target="tpu_custom_call" | custom-call | flops 1000000000 | bytes 4194304 | tf_op jit(solution)/shard_map/cross_and_band/pallas_call | solution.py:198
  94.6 30.5 %all-gather.1 = f32[256,512]{1,0:T(8,128)S(1)} all-gather(f32[16,512]{1,0:T(8,128)S(1)} %get-tuple-element.17), channel_id=3, replica_groups={{0,48,64,112,128,176,192,240,256,304,320,368,384,432,448,496},{16,32,80..., dimensions={0}, use_global_device_ids=true | all-gather | bytes 557056 | tf_op jit(solution)/shard_map/all_gather | solution.py:284
  125.2 13.7 %all_to_all.20 = f32[16,16,512]{2,1,0:T(8,128)S(1)} all-to-all(f32[16,16,512]{2,1,0:T(8,128)S(1)} %broadcast_in_dim.23), channel_id=1, replica_groups=mesh['fsdp'=32,'tp'=16] {'tp'}, dimensions={0} | all-to-all | bytes 1048576 | tf_op jit(solution)/shard_map/all_to_all | solution.py:26
  138.8 3.5 %collective-permute-start.3 = (f32[16,16,512]{2,1,0:T(8,128)S(1)}, f32[16,16,512]{2,1,0:T(8,128)}, u32[]{:S(2)}, u32[]{:S(2)}) collective-permute-start(f32[16,16,512]{2,1,0:T(8,128)S(1)} %all_to_all.20), channel_id=1, source_target_pairs={{16,0},{0,16},{48,32},{32,48},{80,64},{64,80},{112,96},{96,112},{1... | collective-permute-start | bytes 1572872 | tf_op jit(solution)/shard_map/ppermute | solution.py:22
  145.1 17.5 %inverse_factor.1.inverse_ref = f32[512,512]{1,0:T(8,128)S(1)} custom-call(f32[512,512]{1,0:T(8,128)S(1)} %bitcast.34), custom_call_target="tpu_custom_call" | custom-call | flops 600000000 | bytes 3145728 | tf_op jit(solution)/shard_map/inverse_factor/pallas_call | solution.py:156
  162.6 2.0 convolution_convert_fusion
  165.6 28.8 %all-gather.2.rows_ref = bf16[896,512]{1,0:T(8,128)(2,1)S(1)} all-gather(bf16[56,512]{1,0:T(8,128)(2,1)S(1)} %convolution_convert_fusion), channel_id=4, replica_groups={{0,48,64,112,128,176,192,240,256,304,320,368,384,432,448,496},{16,32,80..., dimensions={0}, use_global_device_ids=true | all-gather | bytes 974848 | tf_op jit(solution)/shard_map/all_gather | solution.py:290
  194.3 2.3 %collective-permute-start.4 = (bf16[896,512]{1,0:T(8,128)(2,1)S(1)}, bf16[896,512]{1,0:T(8,128)(2,1)S(1)}, u32[]{:S(2)}, u32[]{:S(2)}) collective-permute-start(bf16[896,512]{1,0:T(8,128)(2,1)S(1)} %all-gather.2.rows_ref), channel_id=1, source_target_pairs={{16,0},{0,16},{48,32},{32,48},{80,64},{64,80},{112,96},{96,112},{1... | collective-permute-start | bytes 2752520 | tf_op jit(solution)/shard_map/ppermute | solution.py:22
  197.0 1.7 collective-permute-done.4.other_ref
  199.6 4.1 %all-to-all-start.3 = ((f32[16,1,512]{2,1,0:T(1,128)}), f32[16,1,512]{2,1,0:T(1,128)}, u32[]{:S(2)}, u32[]{:S(2)}) async-start(f32[16,1,512]{2,1,0:T(1,128)} %broadcast_in_dim.24), calls=%async_computation.4 | async-start | bytes 65536 | tf_op jit(solution)/shard_map/all_to_all | solution.py:295
  205.0 3.1 %feedback.1 = (bf16[256,1792]{1,0:T(8,128)(2,1)}, bf16[256,512]{1,0:T(8,128)(2,1)S(1)}) custom-call(s32[2]{0:T(128)S(1)} %pad_add_fusion.core_ref.at_ref, bf16[896,512]{1,0:T(8,128)(2,1)S(1)} %all-gather.2.rows_ref, bf16[896,512]{1,0:T(8,128)(2,1)S(1)} %collective-permute-done.4.other_ref, f32[256,512]{1,0:T(8,128)S(1)} %bitcast.37, ...), custom_call_target="tpu_custom_call" | custom-call | flops 1300000000 | bytes 4194304 | tf_op jit(solution)/shard_map/feedback/pallas_call | solution.py:247
  208.1 2.1 all-to-all-done.3
  212.1 2.6 %update.1 = (bf16[256,1792]{1,0:T(8,128)(2,1)}, bf16[16,1792]{1,0:T(8,128)(2,1)}) custom-call(s32[2]{0:T(128)S(1)} %pad_add_fusion.core_ref.at_ref, f32[16,512]{1,0:T(8,128)S(1)} %bitcast.38, bf16[896,512]{1,0:T(8,128)(2,1)S(1)} %all-gather.2.rows_ref, bf16[896,512]{1,0:T(8,128)(2,1)S(1)} %collective-permute-done.4.other_ref, ...), custom_call_target="tpu_custom_call" | custom-call | flops 500000000 | bytes 4194304 | tf_op jit(solution)/shard_map/update/pallas_call | solution.py:247
  (28 shorter events, 11.6 us)
Async XLA Ops:
  47.2 4.4 %collective-permute-start = (bf16[16,16,1792]{2,1,0:T(8,128)(2,1)S(1)}, bf16[16,16,1792]{2,1,0:T(8,128)(2,1)S(1)}, u32[]{:S(2)}, u32[]{:S(2)}) collective-permute-start(bf16[16,16,1792]{2,1,0:T(8,128)(2,1)S(1)} %bitcast.40), channel_id=1, source_target_pairs={{16,0},{0,16},{48,32},{32,48},{80,64},{64,80},{112,96},{96,112},{1... | collective-permute-start | bytes 2752520 | tf_op jit(solution)/shard_map/ppermute | solution.py:22
  53.3 17.7 %all-to-all-start = ((f32[16,16,512]{2,1,0:T(8,128)}), f32[16,16,512]{2,1,0:T(8,128)S(1)}, u32[]{:S(2)}, u32[]{:S(2)}) async-start(f32[16,16,512]{2,1,0:T(8,128)} %fusion.3), calls=%async_computation | async-start | bytes 1048576 | tf_op jit(solution)/shard_map/all_to_all | solution.py:274
  71.9 13.7 %all-to-all-start.1 = ((f32[16,16,512]{2,1,0:T(8,128)}), f32[16,16,512]{2,1,0:T(8,128)S(1)}, u32[]{:S(2)}, u32[]{:S(2)}) async-start(f32[16,16,512]{2,1,0:T(8,128)} %broadcast_in_dim.22), calls=%async_computation.1 | async-start | bytes 1048576 | tf_op jit(solution)/shard_map/all_to_all | solution.py:26
  75.5 87.1 %reduce-scatter.2.cloned.1.call-start = ((), (), s32[]{:S(2)}) async-start(), calls=%async_computation.5 | async-start | bytes 1949696 | tf_op jit(solution)/shard_map/reduce_scatter | solution.py:281
  75.7 4.9 %collective-permute-start.1 = (bf16[256,896]{1,0:T(8,128)(2,1)S(1)}, bf16[256,896]{1,0:T(8,128)(2,1)S(1)}, u32[]{:S(2)}, u32[]{:S(2)}) collective-permute-start(bf16[256,896]{1,0:T(8,128)(2,1)S(1)} %get-tuple-element.29), channel_id=1, source_target_pairs={{16,0},{0,16},{48,32},{32,48},{80,64},{64,80},{112,96},{96,112},{1... | collective-permute-start | bytes 1376264 | tf_op jit(solution)/shard_map/ppermute | solution.py:22
  85.6 5.8 %collective-permute-start.2 = (f32[256,512]{1,0:T(8,128)S(1)}, f32[256,512]{1,0:T(8,128)S(1)}, u32[]{:S(2)}, u32[]{:S(2)}) collective-permute-start(f32[256,512]{1,0:T(8,128)S(1)} %bitcast.35), channel_id=1, source_target_pairs={{16,0},{0,16},{48,32},{32,48},{80,64},{64,80},{112,96},{96,112},{1... | collective-permute-start | bytes 1572872 | tf_op jit(solution)/shard_map/ppermute | solution.py:22
  138.8 5.0 %collective-permute-start.3 = (f32[16,16,512]{2,1,0:T(8,128)S(1)}, f32[16,16,512]{2,1,0:T(8,128)}, u32[]{:S(2)}, u32[]{:S(2)}) collective-permute-start(f32[16,16,512]{2,1,0:T(8,128)S(1)} %all_to_all.20), channel_id=1, source_target_pairs={{16,0},{0,16},{48,32},{32,48},{80,64},{64,80},{112,96},{96,112},{1... | collective-permute-start | bytes 1572872 | tf_op jit(solution)/shard_map/ppermute | solution.py:22
  164.6 1.0 copy-start
  194.3 4.4 %collective-permute-start.4 = (bf16[896,512]{1,0:T(8,128)(2,1)S(1)}, bf16[896,512]{1,0:T(8,128)(2,1)S(1)}, u32[]{:S(2)}, u32[]{:S(2)}) collective-permute-start(bf16[896,512]{1,0:T(8,128)(2,1)S(1)} %all-gather.2.rows_ref), channel_id=1, source_target_pairs={{16,0},{0,16},{48,32},{32,48},{80,64},{64,80},{112,96},{96,112},{1... | collective-permute-start | bytes 2752520 | tf_op jit(solution)/shard_map/ppermute | solution.py:22
  199.6 10.6 %all-to-all-start.3 = ((f32[16,1,512]{2,1,0:T(1,128)}), f32[16,1,512]{2,1,0:T(1,128)}, u32[]{:S(2)}, u32[]{:S(2)}) async-start(f32[16,1,512]{2,1,0:T(1,128)} %broadcast_in_dim.24), calls=%async_computation.4 | async-start | bytes 65536 | tf_op jit(solution)/shard_map/all_to_all | solution.py:295
  203.7 1.2 copy-start.1
  210.9 1.2 copy-start.2
Sparse Core Ops, SparseCore 0:
  94.7 61.2 reduce-scatter.1
